TPU v7x, 256 devices: a whole 4x4x8 slice. The times are simulated.
256 devices in a mesh: comp: 4 (over z_hi), dom: 32 (over y, x, core), lev: 2 (over z_lo).
Axes of the slice: x: 4, y: 4, z: 8 (z_hi: 4, z_lo: 2; z = z_hi * 2 + z_lo), core: 2. Of those that a mesh axis runs over, the one named last changes fastest.
Arguments:
- air_profile_vector: float32 [144, 262144], P(None, ('comp', 'dom', 'lev')), may hold values from -6 to 6
- profile_pass_kind: int32 [262144], P(('comp', 'dom', 'lev')), may hold values from 1 to 3, as said below
- position_profile_map: int32 [262144], P(('comp', 'dom', 'lev')), may hold values from 0 to 1023, as said below
- sunlight_aerosol_drive: float32 [144, 262144], P(None, ('comp', 'dom', 'lev')), may hold values from -6 to 6
- profile_link_operator: float32 [144, 144], replicated, may hold values from -0.5 to 0.5
- bottom_warmth_seen: float32 [262144], P(('comp', 'dom', 'lev')), may hold values from -6 to 6
- intersect_sender_index: int32 [8192, 256], P(('comp', 'dom', 'lev')), may hold values from 0 to 1023
- intersect_share: float32 [8192, 256], P(('comp', 'dom', 'lev')), may hold values from 0.1 to 1
- intersect_receiver_tile: int32 [8192, 256], P(('comp', 'dom', 'lev')), may hold values from 0 to 8191
- marine_warmth_departure: float32 [80, 1024, 1024], P('lev', ('comp', 'dom')), may hold values from -6 to 6
- earlier_bottom_inflow: float32 [1024, 1024], P(('comp', 'dom')), may hold values from -6 to 6
- marine_tile_indicator: int32 [1024, 1024], P(('comp', 'dom')), may hold values 0 or 1
Outputs:
- air_profile_updated: float32 [144, 262144], P(None, ('comp', 'dom', 'lev'))
- ocean_temp_out: float32 [80, 1024, 1024], P('lev', ('comp', 'dom'))
- marine_warming_rate: float32 [1024, 1024], P(('comp', 'dom'))
- air_bottom_warmth: float32 [262144], P(('comp', 'dom', 'lev'))
Inputs may be any that keep to these rules, and one draw needn't show every extreme that they name: `profile_pass_kind`: each column's number of physics sweeps; some device holds columns of class 3. `position_profile_map`: on each device the first 512 entries are distinct local columns of the device itself; the last 512 are distinct local columns of the device half the dom axis away (same comp and lev), namely those that device does not keep; so every dynamics column is held by exactly one slot.
All inputs are finite; a program needn't handle non-finite values. No bound on the sum of `marine_tile_indicator` on one device may be relied on, other than what follows from the above.
Results may differ from a plain program's by a relative error of at most 0.0001.
Values sent between devices are 32-bit elements; how exact they have to be, the bound alone decides.
No kernel may reach another device: no remote copies, remote signals or barrier semaphores. Data moves between devices by JAX's collectives and lax.ppermute only.
A program may use at most 64 MiB of HBM per device.

v0:
```python
import jax
import jax.numpy as jnp
from jax import lax
from jax.sharding import PartitionSpec as P

STEPS = 4


surface_exchange_factor = 0.8
humidity_exchange_factor = 0.5
tendency_scale = 0.5
horizontal_rate = 0.15
vertical_rate = 0.1
flux_gain = 0.5
top_precision = lax.Precision.HIGHEST


def shifted(value, axis, steps):
    count = lax.axis_size(axis)
    pairs = [(source, (source + steps) % count) for source in range(count)]
    return lax.ppermute(value, axis, pairs)


def extended(array, sides, width):
    for axis, dim in sides:
        size, length = (lax.axis_size(axis), array.shape[dim])
        up = [(i, (i + 1) % size) for i in range(size - 1)]
        down = [(j, i) for i, j in up]
        last = lax.slice_in_dim(array, length - width, length, axis=dim)
        initial = lax.slice_in_dim(array, 0, width, axis=dim)
        before = lax.ppermute(last, axis, up)
        after = lax.ppermute(initial, axis, down)
        array = jnp.concatenate([before, array, after], axis=dim)
    return array


def broadcast(value, axis, source):
    kept = jnp.where(lax.axis_index(axis) == source, value, 0).astype(value.dtype)
    return lax.psum(kept, axis)


def pick_matrix(positions, extent):
    return (jnp.arange(extent, dtype=jnp.int32)[:, None] == positions[None, :]).astype(jnp.float32)


def entry_matrix(positions, extent):
    return (positions[:, None] == jnp.arange(extent, dtype=jnp.int32)[None, :]).astype(jnp.float32)


def group_count(row_total, slot_width):
    rows_group = row_total
    while rows_group * slot_width > 2048 and rows_group % 2 == 0:
        rows_group = rows_group // 2
    return row_total // rows_group


def on_device(
    air_profile_vector,
    profile_pass_kind,
    position_profile_map,
    sunlight_aerosol_drive,
    profile_link_operator,
    bottom_warmth_seen,
    intersect_sender_index,
    intersect_share,
    intersect_receiver_tile,
    marine_warmth_departure,
    earlier_bottom_inflow,
    marine_tile_indicator,
):
    columns = air_profile_vector.shape[1]
    half_cols = columns // 2
    partner_gap = lax.axis_size("dom") // 2
    own_slots = position_profile_map[:half_cols]
    far_slots = position_profile_map[half_cols:]
    own_pick = pick_matrix(own_slots, columns)
    partner_state, partner_class = shifted(
        (air_profile_vector, profile_pass_kind), "dom", partner_gap
    )
    far_pick = pick_matrix(far_slots, columns)
    far_state = jnp.dot(
        partner_state, far_pick, precision=top_precision, preferred_element_type=jnp.float32
    )
    far_class = jnp.dot(
        partner_class.astype(jnp.float32),
        far_pick,
        precision=top_precision,
        preferred_element_type=jnp.float32,
    )
    own_state = jnp.dot(
        air_profile_vector, own_pick, precision=top_precision, preferred_element_type=jnp.float32
    )
    own_class = jnp.dot(
        profile_pass_kind.astype(jnp.float32),
        own_pick,
        precision=top_precision,
        preferred_element_type=jnp.float32,
    )
    slots_state = jnp.concatenate([own_state, far_state], axis=1)
    slots_class = jnp.concatenate([own_class, far_class])
    rows_state = slots_state.shape[0]
    block_width = min(128, columns)
    block_count = columns // block_width

    def to_blocks(array):
        return array.reshape(rows_state, block_count, block_width).transpose(1, 0, 2)

    def one_block(block):
        state, forcing, classes = block

        def sweep(sweep_index, current):
            drive = (
                jnp.dot(
                    profile_link_operator,
                    current,
                    precision=top_precision,
                    preferred_element_type=jnp.float32,
                )
                + forcing
            )
            return current + jnp.where(
                classes[None, :] > sweep_index, tendency_scale * jnp.tanh(drive), jnp.float32(0.0)
            )

        return lax.fori_loop(0, jnp.max(classes).astype(jnp.int32), sweep, state)

    new_blocks = lax.map(
        one_block,
        (
            to_blocks(slots_state),
            to_blocks(sunlight_aerosol_drive),
            slots_class.reshape(block_count, block_width),
        ),
    )
    new_slots = new_blocks.transpose(1, 0, 2).reshape(rows_state, columns)
    own_new = new_slots[:, :half_cols]
    far_new = new_slots[:, half_cols:]
    gathered_back, taken = shifted((far_new, far_slots), "dom", partner_gap)
    taken_pick = pick_matrix(taken, columns)
    air_profile_updated = jnp.dot(
        own_new, own_pick.T, precision=top_precision, preferred_element_type=jnp.float32
    ) + jnp.dot(
        gathered_back, taken_pick.T, precision=top_precision, preferred_element_type=jnp.float32
    )
    atmos_level_count = rows_state // 2
    heat_flux = (
        surface_exchange_factor * (air_profile_updated[atmos_level_count - 1] - bottom_warmth_seen)
        + humidity_exchange_factor * air_profile_updated[2 * atmos_level_count - 1]
    )
    entry_rows = intersect_sender_index.shape[0]
    slot_width = intersect_sender_index.shape[1]
    groups = group_count(entry_rows, slot_width)
    sender_groups = intersect_sender_index.reshape(groups, -1)

    def source_values(sender_block):
        return jnp.dot(
            entry_matrix(sender_block, columns),
            heat_flux,
            precision=top_precision,
            preferred_element_type=jnp.float32,
        )

    flux_at_source = lax.map(source_values, sender_groups).reshape(entry_rows, slot_width)
    pieces = intersect_share * flux_at_source
    received = lax.all_to_all(pieces, "dom", split_axis=0, concat_axis=0, tiled=True)
    tier_total = marine_warmth_departure.shape[0]
    line_total = marine_warmth_departure.shape[1]
    span_total = marine_warmth_departure.shape[2]
    line_groups = (intersect_receiver_tile // span_total).reshape(groups, -1)
    along_groups = (intersect_receiver_tile % span_total).reshape(groups, -1)
    received_groups = received.reshape(groups, -1)

    def add_flux(total, block):
        line_block, along_block, value_block = block
        weighted_rows = entry_matrix(line_block, line_total) * value_block[:, None]
        term = lax.dot_general(
            weighted_rows,
            entry_matrix(along_block, span_total),
            (((0,), (0,)), ((), ())),
            precision=top_precision,
            preferred_element_type=jnp.float32,
        )
        return (total + term, None)

    partial_flux, unused = lax.scan(
        add_flux,
        jnp.zeros((line_total, span_total), jnp.float32),
        (line_groups, along_groups, received_groups),
    )
    marine_warming_rate = lax.psum(partial_flux, "lev")
    wet_plane = marine_tile_indicator.astype(jnp.float32)
    surface_term = flux_gain * earlier_bottom_inflow
    marine = wet_plane[None]
    level_rows = jnp.arange(tier_total, dtype=jnp.int32)
    top_row = ((level_rows == 0) & (lax.axis_index("lev") == 0)).astype(jnp.float32)[:, None, None]
    theta_profile = marine_warmth_departure
    for step_index in range(STEPS):
        bordered = extended(theta_profile, ((("comp", "dom"), 1), ("lev", 0)), 1)
        sideways = (
            bordered[1:-1, 2:]
            + bordered[1:-1, :-2]
            + jnp.roll(theta_profile, 1, 2)
            + jnp.roll(theta_profile, -1, 2)
            - 4.0 * theta_profile
        )
        upright = bordered[2:, 1:-1] + bordered[:-2, 1:-1] - 2.0 * theta_profile
        increment = horizontal_rate * sideways + vertical_rate * upright
        increment = increment + top_row * surface_term[None]
        theta_profile = theta_profile + marine * increment
    bottom_boundary = broadcast(theta_profile[0], "lev", 0)

    def target_values(block):
        line_block, along_block = block
        along_rows = jnp.dot(
            entry_matrix(along_block, span_total),
            bottom_boundary.T,
            precision=top_precision,
            preferred_element_type=jnp.float32,
        )
        return jnp.sum(along_rows * entry_matrix(line_block, line_total), axis=1)

    sent = lax.map(target_values, (line_groups, along_groups)).reshape(entry_rows, slot_width)
    back = lax.all_to_all(sent, "dom", split_axis=0, concat_axis=0, tiled=True)
    back_groups = (intersect_share * back).reshape(groups, -1)

    def add_warmth(total, block):
        sender_block, value_block = block
        return (
            total
            + jnp.dot(
                value_block,
                entry_matrix(sender_block, columns),
                precision=top_precision,
                preferred_element_type=jnp.float32,
            ),
            None,
        )

    air_bottom_warmth, unused_back = lax.scan(
        add_warmth, jnp.zeros((columns,), jnp.float32), (sender_groups, back_groups)
    )
    return (air_profile_updated, theta_profile, marine_warming_rate, air_bottom_warmth)


def solution(mesh):
    placed = (
        P(None, ("comp", "dom", "lev")),
        P(("comp", "dom", "lev")),
        P(("comp", "dom", "lev")),
        P(None, ("comp", "dom", "lev")),
        P(),
        P(("comp", "dom", "lev")),
        P(("comp", "dom", "lev"), None),
        P(("comp", "dom", "lev"), None),
        P(("comp", "dom", "lev"), None),
        P("lev", ("comp", "dom"), None),
        P(("comp", "dom"), None),
        P(("comp", "dom"), None),
    )
    return jax.shard_map(
        on_device,
        mesh=mesh,
        in_specs=placed,
        out_specs=(
            P(None, ("comp", "dom", "lev")),
            P("lev", ("comp", "dom"), None),
            P(("comp", "dom"), None),
            P(("comp", "dom", "lev")),
        ),
        check_vma=False,
    )
```

profile of v0, /device:TPU:64, one launch (start us, length us, event | category | flops | bytes accessed | tf_op | source)
XLA Modules:
  0.0 299.8 jit_solution(8711280105315330268)
XLA Ops:
  7.2 2.1 fusion.99
  10.0 5.6 %collective-permute-start.4 = (f32[40,1,1024]{2,0,1:T(8,128)}, f32[40,1,1024]{2,0,1:T(8,128)}, u32[]{:S(2)}, u32[]{:S(2)}) collective-permute-start(f32[40,1,1024]{2,0,1:T(8,128)} %copy.65), channel_id=1, source_target_pairs={{2,0},{4,2},{6,4},{8,6},{10,8},{12,10},{14,12},{16,14},{18,16},{20... | collective-permute-start | bytes 491528 | tf_op jit(solution)/shard_map/ppermute | solution.py:32
  19.9 2.0 collective-permute-start.1
  27.1 2.6 fusion.76
  33.7 3.2 %collective-permute-done.1 = s32[1024]{0:T(1024)S(1)} collective-permute-done((s32[1024]{0:T(1024)}, s32[1024]{0:T(1024)S(1)}, u32[]{:S(2)}, u32[]{:S(2)}) %collective-permute-start.1) | collective-permute-done | bytes 4128 | tf_op jit(solution)/shard_map/ppermute | solution.py:21
  41.9 4.5 %collective-permute-start.7 = (f32[1,10,1024]{2,1,0:T(8,128)S(1)}, f32[1,10,1024]{2,1,0:T(8,128)S(1)}, u32[]{:S(2)}, u32[]{:S(2)}) collective-permute-start(f32[1,10,1024]{2,1,0:T(8,128)S(1)} %get-tuple-element.302), channel_id=1, source_target_pairs={{0,1},{2,3},{4,5},{6,7},{8,9},{10,11},{12,13},{14,15},{16,17},{18,... | collective-permute-start | bytes 122888 | tf_op jit(solution)/shard_map/ppermute | solution.py:31
  48.4 2.6 fusion.32
  51.3 2.5 collective-permute-start.8
  56.8 8.9 %collective-permute-done.9 = f32[40,1,1024]{2,0,1:T(8,128)S(1)} collective-permute-done((f32[40,1,1024]{2,0,1:T(8,128)S(1)}, f32[40,1,1024]{2,0,1:T(8,128)S(1)}, u32[]{:S(2)}, u32[]{:S(2)}) %collective-permute-start.9) | collective-permute-done | bytes 163872 | tf_op jit(solution)/shard_map/ppermute | solution.py:31
  67.1 5.0 %collective-permute-start.11 = (f32[1,10,1024]{2,1,0:T(8,128)S(1)}, f32[1,10,1024]{2,1,0:T(8,128)S(1)}, u32[]{:S(2)}, u32[]{:S(2)}) collective-permute-start(f32[1,10,1024]{2,1,0:T(8,128)S(1)} %get-tuple-element.300), channel_id=1, source_target_pairs={{0,1},{2,3},{4,5},{6,7},{8,9},{10,11},{12,13},{14,15},{16,17},{18,... | collective-permute-start | bytes 122888 | tf_op jit(solution)/shard_map/ppermute | solution.py:31
  74.1 2.6 fusion.34
  78.9 2.4 collective-permute-start.13
  83.9 6.9 %collective-permute-done.13 = f32[40,1,1024]{2,0,1:T(8,128)S(1)} collective-permute-done((f32[40,1,1024]{2,0,1:T(8,128)S(1)}, f32[40,1,1024]{2,0,1:T(8,128)S(1)}, u32[]{:S(2)}, u32[]{:S(2)}) %collective-permute-start.13) | collective-permute-done | bytes 163872 | tf_op jit(solution)/shard_map/ppermute | solution.py:31
  93.1 6.3 %collective-permute-start.15 = (f32[1,10,1024]{2,1,0:T(8,128)}, f32[1,10,1024]{2,1,0:T(8,128)}, u32[]{:S(2)}, u32[]{:S(2)}) collective-permute-start(f32[1,10,1024]{2,1,0:T(8,128)} %get-tuple-element.298), channel_id=1, source_target_pairs={{0,1},{2,3},{4,5},{6,7},{8,9},{10,11},{12,13},{14,15},{16,17},{18,... | collective-permute-start | bytes 122888 | tf_op jit(solution)/shard_map/ppermute | solution.py:31
  99.4 1.9 fusion.77
  102.2 31.9 %while.63 = (s32[]{:T(128)}, f32[8,144,128]{2,1,0:T(8,128)}, f32[8,144,128]{2,1,0:T(8,128)}, f32[8,128]{1,0:T(8,128)S(1)}, f32[8,144,128]{2,0,1:T(8,128)S(1)}, /...) while((s32[]{:T(128)}, f32[8,144,128]{2,1,0:T(8,128)}, ...), condition=%wide.region_4.5_spmd, body=%wide.region_0.4_spmd.sunk | while | flops 31924484 | bytes 896534 | solution.py:127
  135.4 2.0 fusion.27
  137.6 3.5 %fusion.36 = f32[40,8,1024]{2,1,0:T(8,128)S(1)} fusion(f32[40,8,1024]{2,1,0:T(8,128)S(1)} %fusion.34, f32[1,10,1024]{2,1,0:T(8,128)} %collective-permute-done.15, f32[40,1,1024]{2,1,0:T(1,128)S(1)} %copy-done.5, f32[40,1,1024]{2,1,0:T(1,128)S(1)} %copy-done.7, f32[1,10,1024]{2,1,0:T(8,128)} %collective-permute-done.14, f32[40,8,1023]{2,1,0:T(8,128)S(1)} %copy-done.2, ...), kind=kLoop, calls=%fused_computation.63 | loop fusion | flops 8192000 | bytes 5718176 | tf_op jit(solution)/shard_map/add | solution.py:209
  141.4 1.9 collective-permute-start.16
  143.4 2.4 collective-permute-start.17
  146.5 9.2 %collective-permute-done.17 = f32[40,1,1024]{2,0,1:T(8,128)S(1)} collective-permute-done((f32[40,1,1024]{2,0,1:T(8,128)S(1)}, f32[40,1,1024]{2,0,1:T(8,128)S(1)}, u32[]{:S(2)}, u32[]{:S(2)}) %collective-permute-start.17) | collective-permute-done | bytes 163872 | tf_op jit(solution)/shard_map/ppermute | solution.py:31
  157.2 4.5 %collective-permute-start.19 = (f32[1,10,1024]{2,1,0:T(8,128)S(1)}, f32[1,10,1024]{2,1,0:T(8,128)S(1)}, u32[]{:S(2)}, u32[]{:S(2)}) collective-permute-start(f32[1,10,1024]{2,1,0:T(8,128)S(1)} %get-tuple-element.296), channel_id=1, source_target_pairs={{0,1},{2,3},{4,5},{6,7},{8,9},{10,11},{12,13},{14,15},{16,17},{18,... | collective-permute-start | bytes 122888 | tf_op jit(solution)/shard_map/ppermute | solution.py:31
  163.7 2.6 fusion.38
  168.5 16.7 %while.64 = (s32[]{:T(128)}, f32[4,2048]{1,0:T(4,128)S(1)}, s32[4,2048]{1,0:T(4,128)S(1)}, f32[1024]{0:T(1024)S(1)}, s32[]{:T(128)}, /*index=5*/s32[]{:T(128)}) while((s32[]{:T(128)}, f32[4,2048]{1,0:T(4,128)S(1)}, s32[4,2048]{1,0:T(4,128)S(1)}, f32[1024]{0:T(1024)S(1)}, s32[]{:T(128)}, /*index=5*/s32[]{:T(128)}) %tuple.157), condition=%wide.region_6.7_spmd, body=%wide.region_5.6_spmd.sunk | while | flops 27262976 | bytes 53325 | solution.py:163
  168.5 4.0 %fusion.126 = f32[1,2048]{1,0:T(1,128)S(1)} fusion(f32[1024,1]{0,1:T(1,128)S(1)} %bitcast.122, s32[2048]{0:T(1024)S(1)} %bitcast.111), kind=kOutput, calls=%fused_computation.13.clone.1 | convolution fusion | flops 27262976 | bytes 20480 | tf_op jit(solution)/shard_map/while/body/eval_jaxpr/dot_general | solution.py:156
  172.7 4.0 %fusion.126 = f32[1,2048]{1,0:T(1,128)S(1)} fusion(f32[1024,1]{0,1:T(1,128)S(1)} %bitcast.122, s32[2048]{0:T(1024)S(1)} %bitcast.111), kind=kOutput, calls=%fused_computation.13.clone.1 | convolution fusion | flops 27262976 | bytes 20480 | tf_op jit(solution)/shard_map/while/body/eval_jaxpr/dot_general | solution.py:156
  176.9 4.0 %fusion.126 = f32[1,2048]{1,0:T(1,128)S(1)} fusion(f32[1024,1]{0,1:T(1,128)S(1)} %bitcast.122, s32[2048]{0:T(1024)S(1)} %bitcast.111), kind=kOutput, calls=%fused_computation.13.clone.1 | convolution fusion | flops 27262976 | bytes 20480 | tf_op jit(solution)/shard_map/while/body/eval_jaxpr/dot_general | solution.py:156
  181.1 4.0 %fusion.126 = f32[1,2048]{1,0:T(1,128)S(1)} fusion(f32[1024,1]{0,1:T(1,128)S(1)} %bitcast.122, s32[2048]{0:T(1024)S(1)} %bitcast.111), kind=kOutput, calls=%fused_computation.13.clone.1 | convolution fusion | flops 27262976 | bytes 20480 | tf_op jit(solution)/shard_map/while/body/eval_jaxpr/dot_general | solution.py:156
  185.9 5.3 %all-to-all-start = ((f32[32,1,256]{2,1,0:T(1,128)}), f32[32,1,256]{2,1,0:T(1,128)S(1)}, u32[]{:S(2)}, u32[]{:S(2)}) async-start(f32[32,1,256]{2,1,0:T(1,128)} %all_to_all.14), calls=%async_computation | async-start | bytes 65536 | tf_op jit(solution)/shard_map/all_to_all | solution.py:165
  192.1 6.5 %all-to-all-done = f32[32,1,256]{2,1,0:T(1,128)S(1)} async-done(((f32[32,1,256]{2,1,0:T(1,128)}), f32[32,1,256]{2,1,0:T(1,128)S(1)}, u32[]{:S(2)}, u32[]{:S(2)}) %all-to-all-start) | async-done | bytes 32800 | tf_op jit(solution)/shard_map/all_to_all | solution.py:165
  198.7 11.8 %while.66 = (s32[]{:T(128)}, f32[8,1024]{1,0:T(8,128)S(1)}, s32[4,2048]{1,0:T(4,128)S(1)}, f32[4,2048]{1,0:T(4,128)S(1)}, s32[4,2048]{1,0:T(4,128)S(1)}, /*index=5*/s32[]{:T(128)}, s32[]{:T(128)}) while((s32[]{:T(128)}, f32[8,1024]{1,0:T(8,128)S(1)}, s32[4,2048]{1,0:T(4,128)S(1)}, f32[4,2048]{1,0:T(4,128)S(1)}, ...), condition=%wide.region_8.9_spmd.clone, body=%wide.region_7.8_spmd.clone.sunk | while | flops 203472896 | bytes 139359 | solution.py:185
  198.8 2.9 fusion.130
  201.7 2.9 fusion.130
  204.7 2.9 fusion.130
  207.6 2.9 fusion.130
  211.1 34.8 %all-reduce.3.cloned.1.call-done = (f32[8,1024]{1,0:T(8,128)}, f32[8,1024]{1,0:T(8,128)}) async-done(((f32[8,1024]{1,0:T(8,128)}, f32[8,1024]{1,0:T(8,128)}), (f32[8,1024]{1,0:T(8,128)}, f32[8,1024]{1,0:T(8,128)})) %all-reduce.3.cloned.1.call-update) | async-done | bytes 65552 | tf_op jit(solution)/shard_map/psum | solution.py:190
  246.0 20.1 %while.65 = (s32[]{:T(128)}, f32[4,2048]{1,0:T(4,128)S(1)}, s32[4,2048]{1,0:T(4,128)S(1)}, s32[4,2048]{1,0:T(4,128)S(1)}, f32[8,1024]{1,0:T(8,128)}, /*index=5*/s32[]{:T(128)}, s32[]{:T(128)}) while((s32[]{:T(128)}, f32[4,2048]{1,0:T(4,128)S(1)}, s32[4,2048]{1,0:T(4,128)S(1)}, s32[4,2048]{1,0:T(4,128)S(1)}, f32[8,1024]{1,0:T(8,128)}, ...), condition=%wide.region_13.14_spmd, body=%wide.region_11.13_spmd.sunk | while | flops 203470848 | bytes 106581 | solution.py:222
  246.0 4.8 %fusion.128 = f32[2048]{0:T(1024)S(1)} fusion(f32[8,1024]{1,0:T(8,128)} %get-tuple-element.652, s32[2048]{0:T(1024)S(1)} %bitcast.115, s32[2048]{0:T(1024)S(1)} %bitcast.116), kind=kOutput, calls=%fused_computation.20.clone.1 | convolution fusion | flops 203470848 | bytes 57344 | tf_op jit(solution)/shard_map/while/body/eval_jaxpr/dot_general | solution.py:214
  251.0 4.8 %fusion.128 = f32[2048]{0:T(1024)S(1)} fusion(f32[8,1024]{1,0:T(8,128)} %get-tuple-element.652, s32[2048]{0:T(1024)S(1)} %bitcast.115, s32[2048]{0:T(1024)S(1)} %bitcast.116), kind=kOutput, calls=%fused_computation.20.clone.1 | convolution fusion | flops 203470848 | bytes 57344 | tf_op jit(solution)/shard_map/while/body/eval_jaxpr/dot_general | solution.py:214
  256.0 4.8 %fusion.128 = f32[2048]{0:T(1024)S(1)} fusion(f32[8,1024]{1,0:T(8,128)} %get-tuple-element.652, s32[2048]{0:T(1024)S(1)} %bitcast.115, s32[2048]{0:T(1024)S(1)} %bitcast.116), kind=kOutput, calls=%fused_computation.20.clone.1 | convolution fusion | flops 203470848 | bytes 57344 | tf_op jit(solution)/shard_map/while/body/eval_jaxpr/dot_general | solution.py:214
  261.1 4.8 %fusion.128 = f32[2048]{0:T(1024)S(1)} fusion(f32[8,1024]{1,0:T(8,128)} %get-tuple-element.652, s32[2048]{0:T(1024)S(1)} %bitcast.115, s32[2048]{0:T(1024)S(1)} %bitcast.116), kind=kOutput, calls=%fused_computation.20.clone.1 | convolution fusion | flops 203470848 | bytes 57344 | tf_op jit(solution)/shard_map/while/body/eval_jaxpr/dot_general | solution.py:214
  266.7 7.1 %all-to-all-start.1 = ((f32[32,1,256]{2,1,0:T(1,128)}), f32[32,1,256]{2,1,0:T(1,128)S(1)}, u32[]{:S(2)}, u32[]{:S(2)}) async-start(f32[32,1,256]{2,1,0:T(1,128)} %all_to_all.16), calls=%async_computation.1 | async-start | bytes 65536 | tf_op jit(solution)/shard_map/all_to_all | solution.py:223
  273.8 7.4 %all-to-all-done.1 = f32[32,1,256]{2,1,0:T(1,128)S(1)} async-done(((f32[32,1,256]{2,1,0:T(1,128)}), f32[32,1,256]{2,1,0:T(1,128)S(1)}, u32[]{:S(2)}, u32[]{:S(2)}) %all-to-all-start.1) | async-done | bytes 32800 | tf_op jit(solution)/shard_map/all_to_all | solution.py:223
  281.3 11.1 %while.67 = (s32[]{:T(128)}, f32[1024]{0:T(1024)S(1)}, f32[4,2048]{1,0:T(4,128)S(1)}, s32[4,2048]{1,0:T(4,128)S(1)}, s32[]{:T(128)}, /*index=5*/s32[]{:T(128)}) while((s32[]{:T(128)}, f32[1024]{0:T(1024)S(1)}, f32[4,2048]{1,0:T(4,128)S(1)}, s32[4,2048]{1,0:T(4,128)S(1)}, s32[]{:T(128)}, /*index=5*/s32[]{:T(128)}) %tuple.158), condition=%wide.region_15.16_spmd.clone, body=%wide.region_14.15_spmd.clone.sunk | while | flops 27265024 | bytes 49239 | solution.py:239
  281.3 2.7 fusion.132
  284.1 2.7 fusion.132
  286.8 2.7 fusion.132
  289.6 2.7 fusion.132
  (300 shorter events, 81.4 us)
Async XLA Ops:
  7.2 17.6 %copy-start.1 = (f32[40,8,1024]{2,1,0:T(8,128)S(1)}, f32[40,8,1024]{2,1,0:T(8,128)}, u32[]{:S(2)}) copy-start(f32[40,8,1024]{2,1,0:T(8,128)} %param.33) | copy-start | bytes 3932164
  10.0 28.3 %collective-permute-start.4 = (f32[40,1,1024]{2,0,1:T(8,128)}, f32[40,1,1024]{2,0,1:T(8,128)}, u32[]{:S(2)}, u32[]{:S(2)}) collective-permute-start(f32[40,1,1024]{2,0,1:T(8,128)} %copy.65), channel_id=1, source_target_pairs={{2,0},{4,2},{6,4},{8,6},{10,8},{12,10},{14,12},{16,14},{18,16},{20... | collective-permute-start | bytes 491528 | tf_op jit(solution)/shard_map/ppermute | solution.py:32
  16.4 23.1 %collective-permute-start.5 = (f32[40,1,1024]{2,0,1:T(8,128)}, f32[40,1,1024]{2,0,1:T(8,128)}, u32[]{:S(2)}, u32[]{:S(2)}) collective-permute-start(f32[40,1,1024]{2,0,1:T(8,128)} %copy.66), channel_id=1, source_target_pairs={{0,2},{2,4},{4,6},{6,8},{8,10},{10,12},{12,14},{14,16},{16,18},{18... | collective-permute-start | bytes 491528 | tf_op jit(solution)/shard_map/ppermute | solution.py:31
  18.3 81.1 %collective-permute-start = (f32[144,1024]{1,0:T(8,128)}, f32[144,1024]{1,0:T(8,128)}, u32[]{:S(2)}, u32[]{:S(2)}) collective-permute-start(f32[144,1024]{1,0:T(8,128)} %param.24), channel_id=1, source_target_pairs={{0,32},{2,34},{4,36},{6,38},{8,40},{10,42},{12,44},{14,46},{16,48}... | collective-permute-start | bytes 1769480 | tf_op jit(solution)/shard_map/ppermute | solution.py:21
  19.9 17.0 %collective-permute-start.1 = (s32[1024]{0:T(1024)}, s32[1024]{0:T(1024)S(1)}, u32[]{:S(2)}, u32[]{:S(2)}) collective-permute-start(s32[1024]{0:T(1024)} %param.25), channel_id=1, source_target_pairs={{0,32},{2,34},{4,36},{6,38},{8,40},{10,42},{12,44},{14,46},{16,48}... | collective-permute-start | bytes 12296 | tf_op jit(solution)/shard_map/ppermute | solution.py:21
  23.3 6.5 %copy-start.30 = (s32[512]{0:T(512)}, s32[512]{0:T(512)S(1)}, u32[]{:S(2)}) copy-start(s32[512]{0:T(512)S(1)} %get-tuple-element.332) | copy-start | bytes 6148
  23.3 143.1 %collective-permute-start.3 = (s32[512]{0:T(512)}, s32[512]{0:T(512)S(1)}, u32[]{:S(2)}, u32[]{:S(2)}) collective-permute-start(s32[512]{0:T(512)} %get-tuple-element.331), channel_id=1, source_target_pairs={{0,32},{2,34},{4,36},{6,38},{8,40},{10,42},{12,44},{14,46},{16,48}... | collective-permute-start | bytes 6152 | tf_op jit(solution)/shard_map/ppermute | solution.py:21
  24.8 2.3 copy-start.28
  24.8 2.3 copy-start.22
  26.3 4.2 %copy-start.21 = (s32[32,256]{1,0:T(8,128)S(1)}, s32[32,256]{1,0:T(8,128)}, u32[]{:S(2)}) copy-start(s32[32,256]{1,0:T(8,128)} %param.32) | copy-start | bytes 98308
  26.3 4.2 %copy-start.23 = (s32[8,1024]{1,0:T(8,128)S(1)}, s32[8,1024]{1,0:T(8,128)}, u32[]{:S(2)}) copy-start(s32[8,1024]{1,0:T(8,128)} %param.35) | copy-start | bytes 98308
  27.1 4.7 %copy-start.24 = (s32[32,256]{1,0:T(8,128)S(1)}, s32[32,256]{1,0:T(8,128)}, u32[]{:S(2)}) copy-start(s32[32,256]{1,0:T(8,128)} %param.30) | copy-start | bytes 98308
  30.6 43.5 %copy-start.9 = (f32[8,1024]{1,0:T(8,128)}, f32[8,1024]{1,0:T(8,128)S(1)}, u32[]{:S(2)}) copy-start(f32[8,1024]{1,0:T(8,128)S(1)} %convert_element_type.35) | copy-start | bytes 98308
  38.3 10.1 %copy-start.3 = (f32[40,8,1023]{2,1,0:T(8,128)S(1)}, f32[40,8,1023]{2,1,0:T(8,128)}, u32[]{:S(2)}) copy-start(f32[40,8,1023]{2,1,0:T(8,128)} %get-tuple-element.322) | copy-start | bytes 3928324
  38.3 10.1 %copy-start.13 = (f32[40,8,1]{2,1,0:T(8,128)S(1)}, f32[40,8,1]{2,1,0:T(8,128)}, u32[]{:S(2)}) copy-start(f32[40,8,1]{2,1,0:T(8,128)} %get-tuple-element.324) | copy-start | bytes 3844
  40.6 6.2 %collective-permute-start.6 = (f32[1,10,1024]{2,1,0:T(8,128)S(1)}, f32[1,10,1024]{2,1,0:T(8,128)S(1)}, u32[]{:S(2)}, u32[]{:S(2)}) collective-permute-start(f32[1,10,1024]{2,1,0:T(8,128)S(1)} %get-tuple-element.301), channel_id=1, source_target_pairs={{1,0},{3,2},{5,4},{7,6},{9,8},{11,10},{13,12},{15,14},{17,16},{19,... | collective-permute-start | bytes 122888 | tf_op jit(solution)/shard_map/ppermute | solution.py:32
  41.9 6.4 %collective-permute-start.7 = (f32[1,10,1024]{2,1,0:T(8,128)S(1)}, f32[1,10,1024]{2,1,0:T(8,128)S(1)}, u32[]{:S(2)}, u32[]{:S(2)}) collective-permute-start(f32[1,10,1024]{2,1,0:T(8,128)S(1)} %get-tuple-element.302), channel_id=1, source_target_pairs={{0,1},{2,3},{4,5},{6,7},{8,9},{10,11},{12,13},{14,15},{16,17},{18,... | collective-permute-start | bytes 122888 | tf_op jit(solution)/shard_map/ppermute | solution.py:31
  51.3 5.3 %collective-permute-start.8 = (f32[40,1,1024]{2,0,1:T(8,128)S(1)}, f32[40,1,1024]{2,0,1:T(8,128)S(1)}, u32[]{:S(2)}, u32[]{:S(2)}) collective-permute-start(f32[40,1,1024]{2,0,1:T(8,128)S(1)} %copy.45), channel_id=1, source_target_pairs={{2,0},{4,2},{6,4},{8,6},{10,8},{12,10},{14,12},{16,14},{18,16},{20... | collective-permute-start | bytes 491528 | tf_op jit(solution)/shard_map/ppermute | solution.py:32
  53.8 11.9 %collective-permute-start.9 = (f32[40,1,1024]{2,0,1:T(8,128)S(1)}, f32[40,1,1024]{2,0,1:T(8,128)S(1)}, u32[]{:S(2)}, u32[]{:S(2)}) collective-permute-start(f32[40,1,1024]{2,0,1:T(8,128)S(1)} %copy.47), channel_id=1, source_target_pairs={{0,2},{2,4},{4,6},{6,8},{8,10},{10,12},{12,14},{14,16},{16,18},{18... | collective-permute-start | bytes 491528 | tf_op jit(solution)/shard_map/ppermute | solution.py:31
  65.8 6.7 %collective-permute-start.10 = (f32[1,10,1024]{2,1,0:T(8,128)S(1)}, f32[1,10,1024]{2,1,0:T(8,128)S(1)}, u32[]{:S(2)}, u32[]{:S(2)}) collective-permute-start(f32[1,10,1024]{2,1,0:T(8,128)S(1)} %get-tuple-element.299), channel_id=1, source_target_pairs={{1,0},{3,2},{5,4},{7,6},{9,8},{11,10},{13,12},{15,14},{17,16},{19,... | collective-permute-start | bytes 122888 | tf_op jit(solution)/shard_map/ppermute | solution.py:32
  67.1 6.9 %collective-permute-start.11 = (f32[1,10,1024]{2,1,0:T(8,128)S(1)}, f32[1,10,1024]{2,1,0:T(8,128)S(1)}, u32[]{:S(2)}, u32[]{:S(2)}) collective-permute-start(f32[1,10,1024]{2,1,0:T(8,128)S(1)} %get-tuple-element.300), channel_id=1, source_target_pairs={{0,1},{2,3},{4,5},{6,7},{8,9},{10,11},{12,13},{14,15},{16,17},{18,... | collective-permute-start | bytes 122888 | tf_op jit(solution)/shard_map/ppermute | solution.py:31
  77.0 6.7 %collective-permute-start.12 = (f32[40,1,1024]{2,0,1:T(8,128)S(1)}, f32[40,1,1024]{2,0,1:T(8,128)S(1)}, u32[]{:S(2)}, u32[]{:S(2)}) collective-permute-start(f32[40,1,1024]{2,0,1:T(8,128)S(1)} %copy.51), channel_id=1, source_target_pairs={{2,0},{4,2},{6,4},{8,6},{10,8},{12,10},{14,12},{16,14},{18,16},{20... | collective-permute-start | bytes 491528 | tf_op jit(solution)/shard_map/ppermute | solution.py:32
  78.9 11.8 %collective-permute-start.13 = (f32[40,1,1024]{2,0,1:T(8,128)S(1)}, f32[40,1,1024]{2,0,1:T(8,128)S(1)}, u32[]{:S(2)}, u32[]{:S(2)}) collective-permute-start(f32[40,1,1024]{2,0,1:T(8,128)S(1)} %copy.53), channel_id=1, source_target_pairs={{0,2},{2,4},{4,6},{6,8},{8,10},{10,12},{12,14},{14,16},{16,18},{18... | collective-permute-start | bytes 491528 | tf_op jit(solution)/shard_map/ppermute | solution.py:31
  83.8 7.1 %copy-start.4 = (f32[40,1,1024]{2,1,0:T(1,128)}, f32[40,1,1024]{2,1,0:T(1,128)S(1)}, u32[]{:S(2)}) copy-start(f32[40,1,1024]{2,1,0:T(1,128)S(1)} %copy.52) | copy-start | bytes 491524
  91.0 10.3 %copy-start.18 = (f32[144,512]{1,0:T(8,128)S(1)}, f32[144,512]{1,0:T(8,128)}, u32[]{:S(2)}) copy-start(f32[144,512]{1,0:T(8,128)} %fusion.76) | copy-start | bytes 884740
  91.7 10.6 %copy-start = (f32[144,144]{1,0:T(8,128)S(1)}, f32[144,144]{1,0:T(8,128)}, u32[]{:S(2)}) copy-start(f32[144,144]{1,0:T(8,128)} %param.28) | copy-start | bytes 248836
  91.7 45.9 %collective-permute-start.14 = (f32[1,10,1024]{2,1,0:T(8,128)}, f32[1,10,1024]{2,1,0:T(8,128)}, u32[]{:S(2)}, u32[]{:S(2)}) collective-permute-start(f32[1,10,1024]{2,1,0:T(8,128)} %get-tuple-element.297), channel_id=1, source_target_pairs={{1,0},{3,2},{5,4},{7,6},{9,8},{11,10},{13,12},{15,14},{17,16},{19,... | collective-permute-start | bytes 122888 | tf_op jit(solution)/shard_map/ppermute | solution.py:32
  93.1 44.5 %collective-permute-start.15 = (f32[1,10,1024]{2,1,0:T(8,128)}, f32[1,10,1024]{2,1,0:T(8,128)}, u32[]{:S(2)}, u32[]{:S(2)}) collective-permute-start(f32[1,10,1024]{2,1,0:T(8,128)} %get-tuple-element.298), channel_id=1, source_target_pairs={{0,1},{2,3},{4,5},{6,7},{8,9},{10,11},{12,13},{14,15},{16,17},{18,... | collective-permute-start | bytes 122888 | tf_op jit(solution)/shard_map/ppermute | solution.py:31
  134.2 3.4 %copy-start.2 = (f32[40,8,1023]{2,1,0:T(8,128)S(1)}, f32[40,8,1023]{2,1,0:T(8,128)}, u32[]{:S(2)}) copy-start(f32[40,8,1023]{2,1,0:T(8,128)} %get-tuple-element.310) | copy-start | bytes 3928324
  134.2 3.4 %copy-start.5 = (f32[40,1,1024]{2,1,0:T(1,128)S(1)}, f32[40,1,1024]{2,1,0:T(1,128)}, u32[]{:S(2)}) copy-start(f32[40,1,1024]{2,1,0:T(1,128)} %copy-done.4) | copy-start | bytes 491524
  134.2 3.4 %copy-start.7 = (f32[40,1,1024]{2,1,0:T(1,128)S(1)}, f32[40,1,1024]{2,1,0:T(1,128)}, u32[]{:S(2)}) copy-start(f32[40,1,1024]{2,1,0:T(1,128)} %copy-done.6) | copy-start | bytes 491524
  134.2 3.4 %copy-start.10 = (f32[8,1024]{1,0:T(8,128)S(1)}, f32[8,1024]{1,0:T(8,128)}, u32[]{:S(2)}) copy-start(f32[8,1024]{1,0:T(8,128)} %copy-done.9) | copy-start | bytes 98308
  134.2 3.5 %copy-start.11 = (f32[40,8,1]{2,1,0:T(8,128)S(1)}, f32[40,8,1]{2,1,0:T(8,128)}, u32[]{:S(2)}) copy-start(f32[40,8,1]{2,1,0:T(8,128)} %get-tuple-element.311) | copy-start | bytes 3844
  134.2 3.5 %copy-start.12 = (f32[40,8,1]{2,1,0:T(8,128)S(1)}, f32[40,8,1]{2,1,0:T(8,128)}, u32[]{:S(2)}) copy-start(f32[40,8,1]{2,1,0:T(8,128)} %get-tuple-element.312) | copy-start | bytes 3844
  137.5 28.9 %collective-permute-start.2 = (f32[144,512]{1,0:T(8,128)S(1)}, f32[144,512]{1,0:T(8,128)S(1)}, u32[]{:S(2)}, u32[]{:S(2)}) collective-permute-start(f32[144,512]{1,0:T(8,128)S(1)} %slice.241), channel_id=1, source_target_pairs={{0,32},{2,34},{4,36},{6,38},{8,40},{10,42},{12,44},{14,46},{16,48}... | collective-permute-start | bytes 884744 | tf_op jit(solution)/shard_map/ppermute | solution.py:21
  141.4 4.9 %collective-permute-start.16 = (f32[40,1,1024]{2,0,1:T(8,128)S(1)}, f32[40,1,1024]{2,0,1:T(8,128)S(1)}, u32[]{:S(2)}, u32[]{:S(2)}) collective-permute-start(f32[40,1,1024]{2,0,1:T(8,128)S(1)} %copy.57), channel_id=1, source_target_pairs={{2,0},{4,2},{6,4},{8,6},{10,8},{12,10},{14,12},{16,14},{18,16},{20... | collective-permute-start | bytes 491528 | tf_op jit(solution)/shard_map/ppermute | solution.py:32
  143.4 12.3 %collective-permute-start.17 = (f32[40,1,1024]{2,0,1:T(8,128)S(1)}, f32[40,1,1024]{2,0,1:T(8,128)S(1)}, u32[]{:S(2)}, u32[]{:S(2)}) collective-permute-start(f32[40,1,1024]{2,0,1:T(8,128)S(1)} %copy.59), channel_id=1, source_target_pairs={{0,2},{2,4},{4,6},{6,8},{8,10},{10,12},{12,14},{14,16},{16,18},{18... | collective-permute-start | bytes 491528 | tf_op jit(solution)/shard_map/ppermute | solution.py:31
  155.9 6.2 %collective-permute-start.18 = (f32[1,10,1024]{2,1,0:T(8,128)S(1)}, f32[1,10,1024]{2,1,0:T(8,128)S(1)}, u32[]{:S(2)}, u32[]{:S(2)}) collective-permute-start(f32[1,10,1024]{2,1,0:T(8,128)S(1)} %get-tuple-element.295), channel_id=1, source_target_pairs={{1,0},{3,2},{5,4},{7,6},{9,8},{11,10},{13,12},{15,14},{17,16},{19,... | collective-permute-start | bytes 122888 | tf_op jit(solution)/shard_map/ppermute | solution.py:32
  157.2 6.4 %collective-permute-start.19 = (f32[1,10,1024]{2,1,0:T(8,128)S(1)}, f32[1,10,1024]{2,1,0:T(8,128)S(1)}, u32[]{:S(2)}, u32[]{:S(2)}) collective-permute-start(f32[1,10,1024]{2,1,0:T(8,128)S(1)} %get-tuple-element.296), channel_id=1, source_target_pairs={{0,1},{2,3},{4,5},{6,7},{8,9},{10,11},{12,13},{14,15},{16,17},{18,... | collective-permute-start | bytes 122888 | tf_op jit(solution)/shard_map/ppermute | solution.py:31
  166.3 25.1 %copy-start.8 = (f32[40,8,1024]{2,1,0:T(8,128)}, f32[40,8,1024]{2,1,0:T(8,128)S(1)}, u32[]{:S(2)}) copy-start(f32[40,8,1024]{2,1,0:T(8,128)S(1)} %fusion.38) | copy-start | bytes 3932164
  167.7 17.5 %copy-start.19 = (f32[32,256]{1,0:T(8,128)S(1)}, f32[32,256]{1,0:T(8,128)}, u32[]{:S(2)}) copy-start(f32[32,256]{1,0:T(8,128)} %param.31) | copy-start | bytes 98308
  167.8 30.9 %copy-start.16 = (s32[4,2048]{1,0:T(4,128)S(1)}, s32[4,2048]{1,0:T(4,128)}, u32[]{:S(2)}) copy-start(s32[4,2048]{1,0:T(4,128)} %reshape.82) | copy-start | bytes 98308
  167.8 30.9 %copy-start.17 = (s32[4,2048]{1,0:T(4,128)S(1)}, s32[4,2048]{1,0:T(4,128)}, u32[]{:S(2)}) copy-start(s32[4,2048]{1,0:T(4,128)} %reshape.86) | copy-start | bytes 98308
  167.8 30.9 %copy-start.25 = (f32[8,1024]{1,0:T(8,128)S(1)}, f32[8,1024]{1,0:T(8,128)}, u32[]{:S(2)}) copy-start(f32[8,1024]{1,0:T(8,128)} %custom-call) | copy-start | bytes 98308
  185.9 12.7 %all-to-all-start = ((f32[32,1,256]{2,1,0:T(1,128)}), f32[32,1,256]{2,1,0:T(1,128)S(1)}, u32[]{:S(2)}, u32[]{:S(2)}) async-start(f32[32,1,256]{2,1,0:T(1,128)} %all_to_all.14), calls=%async_computation | async-start | bytes 65536 | tf_op jit(solution)/shard_map/all_to_all | solution.py:165
  191.2 54.8 %all-reduce.3.cloned.1.call-start = ((), (), s32[]{:S(2)}) async-start(), calls=%async_computation.2 | async-start | bytes 131072 | tf_op jit(solution)/shard_map/psum | solution.py:190
  266.7 14.5 %all-to-all-start.1 = ((f32[32,1,256]{2,1,0:T(1,128)}), f32[32,1,256]{2,1,0:T(1,128)S(1)}, u32[]{:S(2)}, u32[]{:S(2)}) async-start(f32[32,1,256]{2,1,0:T(1,128)} %all_to_all.16), calls=%async_computation.1 | async-start | bytes 65536 | tf_op jit(solution)/shard_map/all_to_all | solution.py:223
  281.3 11.1 %copy-start.27 = (f32[8,1024]{1,0:T(8,128)S(1)}, f32[8,1024]{1,0:T(8,128)}, u32[]{:S(2)}) copy-start(f32[8,1024]{1,0:T(8,128)} %get-tuple-element.675) | copy-start | bytes 98308
  (6 other events, 5.6 us)
Sparse Core Ops, SparseCore 0:
  211.3 34.6 all-reduce.2
where the time goes:
time: 303 us; the launch traced here: 300 us
  waiting for transfers between devices  82.8 us (27%)
  matrix products  74.8 us (25%)
  starting transfers between devices  64.2 us (21%)
  local copies, waits for them, and re-layouts  36.8 us (12%)
  other arithmetic  19.5 us (6%)
  between operations  14.9 us (5%)
  loops' own time  6.94 us (2%)
    psum x1, waiting for transfers between devices, on_device(): marine_warming_rate = lax.psum(partial_flux, 'lev')  34.8 us
    ppermute x8, waiting for transfers between devices, extended(): before = lax.ppermute(last, axis, up)  29.8 us
    ppermute x8, starting transfers between devices, extended(): before = lax.ppermute(last, axis, up)  29.1 us
    dot_general x4, matrix products, target_values(): jnp.dot(entry_matrix(along_block, span_total), bottom_boundary.T, precisi...  19.4 us
    ppermute x8, starting transfers between devices, extended(): after = lax.ppermute(initial, axis, down)  17.2 us
    dot_general x4, matrix products, source_values(): jnp.dot(entry_matrix(sender_block, columns), heat_flux, precision=top_pre...  16.1 us
    dot_general x4, matrix products, add_flux(): lax.dot_general(weighted_rows, entry_matrix(along_block, span_total), (((...  11.5 us
    add x4, other arithmetic, on_device(): theta_profile = theta_profile + marine * increment  11.4 us
  transfers between devices with their start and end apart: 23, of which 14 were waited for; matrix products, arithmetic and copies ran while one was open for 21% of the time, Pallas kernels for 0%

commit v1 on v0

v1 whole, which is shorter than its diff:
```python
import jax
import jax.numpy as jnp
from jax import lax
from jax.experimental import pallas as pl
from jax.experimental.pallas import tpu as pltpu
from jax.sharding import PartitionSpec as P

STEPS = 4
CLASSES = 3
LANES = 128
SUBLANES = 8

surface_exchange_factor = 0.8
humidity_exchange_factor = 0.5
tendency_scale = 0.5
horizontal_rate = 0.15
vertical_rate = 0.1
flux_gain = 0.5

f32 = jnp.float32
bf16 = jnp.bfloat16
i32 = jnp.int32


def whole():
    return pl.BlockSpec(memory_space=pltpu.VMEM)


def call(body, out_shapes, specs, args, name, microseconds, scratch=(), mib=32, grid=()):
    one = not isinstance(out_shapes, (list, tuple))
    shapes = [out_shapes] if one else list(out_shapes)
    out = pl.pallas_call(
        body,
        out_shape=shapes,
        grid=grid,
        in_specs=specs,
        out_specs=[whole() for _ in shapes],
        scratch_shapes=list(scratch),
        compiler_params=pltpu.CompilerParams(vmem_limit_bytes=mib * 1024 * 1024),
        cost_estimate=pl.CostEstimate(
            flops=0, bytes_accessed=int(microseconds * 3.0e6), transcendentals=0
        ),
        name=name,
    )(*args)
    return out[0] if one else out


def split(value):
    high = value.astype(bf16)
    low = (value - high.astype(f32)).astype(bf16)
    return high, low


def dot_nt(a, b):
    return lax.dot_general(a, b, (((1,), (1,)), ((), ())), preferred_element_type=f32)


def dot_nn(a, b):
    return lax.dot_general(a, b, (((1,), (0,)), ((), ())), preferred_element_type=f32)


def pack_forcing(drive_ref, place_ref, out_ref):
    rows, half = drive_ref.shape
    out_ref[0:rows, :] = drive_ref[...]
    far = place_ref[:, half : 2 * half].astype(f32)
    out_ref[rows : rows + SUBLANES, :] = jnp.broadcast_to(far, (SUBLANES, half))


def pack_ocean(theta_ref, inflow_ref, wet_ref, up_ref, down_ref, level_ref, up_corner_ref, down_corner_ref):
    tiers = theta_ref.shape[0]
    up_ref[0] = inflow_ref[4:8, :]
    down_ref[0] = inflow_ref[0:4, :]
    up_ref[1] = wet_ref[4:8, :].astype(f32)
    down_ref[1] = wet_ref[0:4, :].astype(f32)

    def copy_level(tier, carry):
        up_ref[tier + 2] = theta_ref[tier, 4:8, :]
        down_ref[tier + 2] = theta_ref[tier, 0:4, :]
        return carry

    lax.fori_loop(0, tiers, copy_level, 0, unroll=4)
    base = jnp.where(lax.axis_index("lev") == 0, tiers - STEPS, 0)
    for j in range(STEPS):
        level_ref[j] = theta_ref[base + j]
        up_corner_ref[j] = theta_ref[base + j, 4:8, :]
        down_corner_ref[j] = theta_ref[base + j, 0:4, :]


def across(own, halo):
    span = own.shape[1]
    row = lax.broadcasted_iota(i32, own.shape, 0)
    first, last = row == 0, row == SUBLANES - 1
    own_less, halo_less = pltpu.roll(own, 1, 0), pltpu.roll(halo, 1, 0)
    own_more, halo_more = pltpu.roll(own, SUBLANES - 1, 0), pltpu.roll(halo, SUBLANES - 1, 0)
    own_sum = jnp.where(first, halo_less, own_less) + jnp.where(last, halo_more, own_more)
    own_sum = own_sum + (pltpu.roll(own, 1, 1) + pltpu.roll(own, span - 1, 1))
    halo_sum = jnp.where(first, own_less, halo_less) + jnp.where(last, own_more, halo_more)
    halo_sum = halo_sum + (pltpu.roll(halo, 1, 1) + pltpu.roll(halo, span - 1, 1))
    return own_sum, halo_sum


def top_level(theta_ref, before_ref, after_ref, inflow_ref, wet_ref, out_ref):
    count = STEPS + 1

    def joined(k):
        return jnp.concatenate([after_ref[k], before_ref[k]], axis=0)

    wet = (wet_ref[...].astype(f32), joined(1))
    source = tuple(flux_gain * w * s for w, s in zip(wet, (inflow_ref[...], joined(0))))
    keep = tuple(1.0 - (4 * horizontal_rate + 2 * vertical_rate) * w for w in wet)
    side = tuple(horizontal_rate * w for w in wet)
    rise = tuple(vertical_rate * w for w in wet)
    levels = [(theta_ref[k], joined(k + 2)) for k in range(count)]
    for step in range(1, STEPS + 1):
        fresh = []
        for k in range(count - step):
            sums = across(*levels[k])
            value = []
            for part in range(2):
                vertical = levels[k + 1][part]
                if k > 0:
                    vertical = vertical + levels[k - 1][part]
                new = keep[part] * levels[k][part] + side[part] * sums[part] + rise[part] * vertical
                if k == 0:
                    new = new + source[part]
                value.append(new)
            fresh.append(tuple(value))
        levels = fresh
    out_ref[...] = levels[0][0]


def ocean(
    theta_ref,
    before_ref,
    after_ref,
    level_ref,
    before_corner_ref,
    after_corner_ref,
    inflow_ref,
    wet_ref,
    out_ref,
    even,
    odd,
    keep,
    side,
    rise,
    source,
):
    tiers = theta_ref.shape[0]
    places = tiers + STEPS
    lev = lax.axis_index("lev")
    lower = lev.astype(f32)
    upper = 1.0 - lower

    wet_own = wet_ref[...].astype(f32)
    wet_halo = jnp.concatenate([after_ref[1], before_ref[1]], axis=0)
    flow_halo = jnp.concatenate([after_ref[0], before_ref[0]], axis=0)
    for at, wet, flow in ((0, wet_own, inflow_ref[...]), (8, wet_halo, flow_halo)):
        rows = slice(at, at + 8)
        keep[rows, :] = 1.0 - (4 * horizontal_rate + 2 * vertical_rate) * wet
        side[rows, :] = horizontal_rate * wet
        rise[rows, :] = vertical_rate * wet
        source[rows, :] = (flux_gain * upper) * (wet * flow)

    def gather_level(tier, carry):
        even[tier, 0:8, :] = theta_ref[tier]
        even[tier, 8:12, :] = after_ref[tier + 2]
        even[tier, 12:16, :] = before_ref[tier + 2]
        return carry

    lax.fori_loop(0, tiers, gather_level, 0, unroll=2)
    for j in range(STEPS):
        even[tiers + j, 0:8, :] = level_ref[j]
        even[tiers + j, 8:12, :] = after_corner_ref[j]
        even[tiers + j, 12:16, :] = before_corner_ref[j]

    for step in range(1, STEPS + 1):
        held, fresh = (even, odd) if step % 2 else (odd, even)
        final = step == STEPS

        def advance(at, less, more, less_scale=None, more_scale=None, add_source=False):
            own, halo = held[at, 0:8, :], held[at, 8:16, :]
            sums = across(own, halo)
            for part, start in ((0, 0), (1, 8)):
                if final and part == 1:
                    continue
                rows = slice(start, start + 8)
                a, b = held[less, rows, :], held[more, rows, :]
                if less_scale is not None:
                    a = a * less_scale
                if more_scale is not None:
                    b = b * more_scale
                new = (
                    keep[rows, :] * (own, halo)[part]
                    + side[rows, :] * sums[part]
                    + rise[rows, :] * (a + b)
                )
                if add_source:
                    new = new + source[rows, :]
                if final:
                    out_ref[at] = new
                else:
                    fresh[at, rows, :] = new

        advance(0, places - 1, 1, less_scale=lower, add_source=True)

        def inner(at, carry):
            advance(at, at - 1, at + 1)
            return carry

        lax.fori_loop(1, tiers - 1, inner, 0, unroll=2)
        advance(tiers - 1, tiers - 2, tiers, more_scale=upper)
        for j in range(STEPS - step):
            at = tiers + j + lev * step
            more = jnp.where(at == places - 1, 0, at + 1)
            advance(at, at - 1, more)


def columns(
    state_ref,
    classes_ref,
    place_ref,
    drive_ref,
    far_ref,
    link_ref,
    warmth_ref,
    sender_ref,
    share_ref,
    tile_ref,
    top_ref,
    top_far_ref,
    out_ref,
    payload_ref,
):
    rows, count = state_ref.shape
    half = drive_ref.shape[1]
    levels = rows // 2
    width = 256

    own_drive = jnp.concatenate(split(drive_ref[...]), axis=0)
    far_drive = jnp.concatenate(split(far_ref[0:rows, :]), axis=0)
    own_place = place_ref[:, 0:half]
    far_place = far_ref[rows : rows + 1, :].astype(i32)
    link_high, link_low = split(link_ref[...])
    link_both = jnp.concatenate([link_high, link_low], axis=0)

    flux = []
    for start in range(0, count, width):
        cols = slice(start, start + width)
        target = start + lax.broadcasted_iota(i32, (width, half), 0)
        own_pick = jnp.where(target == own_place, 1.0, 0.0).astype(bf16)
        far_pick = jnp.where(target == far_place, 1.0, 0.0).astype(bf16)
        both = dot_nt(own_drive, own_pick) + dot_nt(far_drive, far_pick)
        forcing = both[0:rows] + both[rows : 2 * rows]
        x = state_ref[:, cols]
        kinds = classes_ref[:, cols]
        for k in range(CLASSES):
            high, low = split(x)
            product = dot_nn(link_both, high)
            drive = product[0:rows] + (product[rows : 2 * rows] + dot_nn(link_high, low)) + forcing
            x = x + jnp.where(kinds > k, tendency_scale * jnp.tanh(drive), 0.0)
        out_ref[:, cols] = x
        flux.append(
            surface_exchange_factor * (x[levels - 1 : levels, :] - warmth_ref[:, cols])
            + humidity_exchange_factor * x[rows - 1 : rows, :]
        )
    flux = jnp.concatenate(flux, axis=1)

    entry_rows, slots = sender_ref.shape
    blocks = [
        (slice(r, r + SUBLANES), slice(c, c + LANES))
        for r in range(0, entry_rows, SUBLANES)
        for c in range(0, slots, LANES)
    ]
    block_shape = (SUBLANES, LANES)

    def picked(table, lane):
        spread = jnp.broadcast_to(table, block_shape)
        return jnp.take_along_axis(spread, lane, axis=1, mode="promise_in_bounds")

    lanes = [sender_ref[b] & (LANES - 1) for b in blocks]
    keys = [sender_ref[b] >> 7 for b in blocks]
    found = [jnp.zeros(block_shape, f32) for _ in blocks]
    for r in range(count // LANES):
        table = flux[:, r * LANES : (r + 1) * LANES]
        found = [jnp.where(k == r, picked(table, l), v) for k, l, v in zip(keys, lanes, found)]
    for b, v in zip(blocks, found):
        payload_ref[b] = share_ref[b] * v

    lines, span = top_ref.shape
    surface = jnp.where(lax.axis_index("lev") == 0, top_ref[...], top_far_ref[...])
    chunks = span // LANES
    lanes = [tile_ref[b] & (LANES - 1) for b in blocks]
    keys = [tile_ref[b] >> 7 for b in blocks]
    found = [jnp.zeros(block_shape, f32) for _ in blocks]
    for r in range(lines):
        for c in range(chunks):
            table = surface[r : r + 1, c * LANES : (c + 1) * LANES]
            found = [
                jnp.where(k == r * chunks + c, picked(table, l), v)
                for k, l, v in zip(keys, lanes, found)
            ]
    for (r, c), v in zip(blocks, found):
        payload_ref[r, slots + c.start : slots + c.stop] = v


def entry_sum(index_row, value_row, groups, order):
    entries = index_row.shape[1]
    group = order(index_row)
    hit = lax.broadcasted_iota(i32, (groups, entries), 0) == group
    high = value_row.astype(bf16).astype(f32)
    low = value_row - high
    weighted = jnp.concatenate(
        [jnp.where(hit, high, 0.0).astype(bf16), jnp.where(hit, low, 0.0).astype(bf16)], axis=0
    )
    lane = index_row & (LANES - 1)
    lane_hit = lax.broadcasted_iota(i32, (LANES, entries), 0) == lane
    return dot_nt(weighted, jnp.where(lane_hit, 1.0, 0.0).astype(bf16))


def add_flux(received_ref, tile_ref, out_ref):
    entry_rows, slots = tile_ref.shape
    lines, span = out_ref.shape
    chunks = span // LANES
    groups = lines * chunks
    total = jnp.zeros((2 * groups, LANES), f32)
    for d in range(entry_rows):
        total = total + entry_sum(
            tile_ref[d : d + 1, :],
            received_ref[d : d + 1, 0:slots],
            groups,
            lambda t: ((t >> 7) & (chunks - 1)) * lines + (t >> 10),
        )
    total = total[0:groups] + total[groups:]
    for c in range(chunks):
        out_ref[:, c * LANES : (c + 1) * LANES] = total[c * lines : (c + 1) * lines]


def add_warmth(received_ref, sender_ref, share_ref, out_ref):
    entry_rows, slots = sender_ref.shape
    groups = out_ref.shape[0]
    total = jnp.zeros((2 * groups, LANES), f32)
    for d in range(entry_rows):
        total = total + entry_sum(
            sender_ref[d : d + 1, :],
            received_ref[d : d + 1, slots : 2 * slots] * share_ref[d : d + 1, :],
            groups,
            lambda t: t >> 7,
        )
    out_ref[...] = total[0:groups] + total[groups:]


def on_device(
    air_profile_vector,
    profile_pass_kind,
    position_profile_map,
    sunlight_aerosol_drive,
    profile_link_operator,
    bottom_warmth_seen,
    intersect_sender_index,
    intersect_share,
    intersect_receiver_tile,
    marine_warmth_departure,
    earlier_bottom_inflow,
    marine_tile_indicator,
):
    rows, count = air_profile_vector.shape
    half = count // 2
    tiers, lines, span = marine_warmth_departure.shape
    entry_rows, slots = intersect_sender_index.shape
    n_dom, n_lev = lax.axis_size("dom"), lax.axis_size("lev")
    n_block = lax.axis_size("comp") * n_dom
    place = position_profile_map.reshape(1, count)

    def shape(*dims):
        return jax.ShapeDtypeStruct(dims, f32)

    packed = call(
        pack_forcing,
        shape(rows + SUBLANES, half),
        [pl.BlockSpec((rows, half), lambda i: (0, 1)), whole()],
        (sunlight_aerosol_drive, place),
        "pack_forcing",
        1.5,
        grid=(1,),
    )
    far = lax.ppermute(packed, "dom", [(i, (i + n_dom // 2) % n_dom) for i in range(n_dom)])

    up, down, level, up_corner, down_corner = call(
        pack_ocean,
        [
            shape(tiers + 2, 4, span),
            shape(tiers + 2, 4, span),
            shape(STEPS, lines, span),
            shape(STEPS, 4, span),
            shape(STEPS, 4, span),
        ],
        [whole()] * 3,
        (marine_warmth_departure, earlier_bottom_inflow, marine_tile_indicator),
        "pack_ocean",
        2.0,
    )
    block_axes = ("comp", "dom")
    all_axes = ("comp", "dom", "lev")
    rising = [(i, i + 1) for i in range(n_block - 1)]
    falling = [(j, i) for i, j in rising]
    other = [(0, 1), (1, 0)]

    def corners(pairs):
        return [(a * n_lev + l, b * n_lev + m) for a, b in pairs for l, m in other]

    before = lax.ppermute(up, block_axes, rising)
    after = lax.ppermute(down, block_axes, falling)
    level = lax.ppermute(level, "lev", other)
    before_corner = lax.ppermute(up_corner, all_axes, corners(rising))
    after_corner = lax.ppermute(down_corner, all_axes, corners(falling))

    part = pl.BlockSpec((STEPS + 3, 4, span), lambda i: (0, 0, 0))
    top = call(
        top_level,
        shape(lines, span),
        [pl.BlockSpec((STEPS + 1, lines, span), lambda i: (0, 0, 0)), part, part, whole(), whole()],
        (marine_warmth_departure, before, after, earlier_bottom_inflow, marine_tile_indicator),
        "top_level",
        2.0,
        grid=(1,),
    )
    top_far = lax.ppermute(top, "lev", [(0, 1)])

    air_profile_updated, payload = call(
        columns,
        [shape(rows, count), shape(entry_rows, 2 * slots)],
        [whole()] * 3 + [pl.BlockSpec((rows, half), lambda i: (0, 0))] + [whole()] * 8,
        (
            air_profile_vector,
            profile_pass_kind.reshape(1, count),
            place,
            sunlight_aerosol_drive,
            far,
            profile_link_operator,
            bottom_warmth_seen.reshape(1, count),
            intersect_sender_index,
            intersect_share,
            intersect_receiver_tile,
            top,
            top_far,
        ),
        "columns",
        6.0,
        grid=(1,),
    )
    received = lax.all_to_all(payload, "dom", split_axis=0, concat_axis=0, tiled=True)

    theta = call(
        ocean,
        shape(tiers, lines, span),
        [whole()] * 8,
        (
            marine_warmth_departure,
            before,
            after,
            level,
            before_corner,
            after_corner,
            earlier_bottom_inflow,
            marine_tile_indicator,
        ),
        "ocean",
        6.0,
        scratch=[pltpu.VMEM((tiers + STEPS, 16, span), f32)] * 2 + [pltpu.VMEM((16, span), f32)] * 4,
    )

    partial_flux = call(
        add_flux,
        shape(lines, span),
        [whole()] * 2,
        (received, intersect_receiver_tile),
        "add_flux",
        2.0,
    )
    marine_warming_rate = partial_flux + lax.ppermute(partial_flux, "lev", other)
    air_bottom_warmth = call(
        add_warmth,
        shape(count // LANES, LANES),
        [whole()] * 3,
        (received, intersect_sender_index, intersect_share),
        "add_warmth",
        2.0,
    ).reshape(count)
    return (air_profile_updated, theta, marine_warming_rate, air_bottom_warmth)


def solution(mesh):
    placed = (
        P(None, ("comp", "dom", "lev")),
        P(("comp", "dom", "lev")),
        P(("comp", "dom", "lev")),
        P(None, ("comp", "dom", "lev")),
        P(),
        P(("comp", "dom", "lev")),
        P(("comp", "dom", "lev"), None),
        P(("comp", "dom", "lev"), None),
        P(("comp", "dom", "lev"), None),
        P("lev", ("comp", "dom"), None),
        P(("comp", "dom"), None),
        P(("comp", "dom"), None),
    )
    return jax.shard_map(
        on_device,
        mesh=mesh,
        in_specs=placed,
        out_specs=(
            P(None, ("comp", "dom", "lev")),
            P("lev", ("comp", "dom"), None),
            P(("comp", "dom"), None),
            P(("comp", "dom", "lev")),
        ),
        check_vma=False,
    )
```

time: 303 us -> 83.2 us (0.27)
  the two profiles are of different devices: /device:TPU:64 before, /device:TPU:95 now
where the time goes in v1:
time: 83.2 us; the launch traced here: 82.7 us
  waiting for transfers between devices  32.9 us (40%)
  starting transfers between devices  25.1 us (30%)
  Pallas kernels  18.5 us (22%)
  local copies, waits for them, and re-layouts  4.65 us (6%)
  between operations  0.89 us (1%)
    pallas_call x7, Pallas kernels, call(): pl.pallas_call(body, out_shape=shapes, grid=grid, in_specs=specs, out_spe...  18.5 us
    ppermute x1, waiting for transfers between devices, on_device(): before = lax.ppermute(up, block_axes, rising)  12.9 us
    ppermute x1, waiting for transfers between devices, on_device(): after_corner = lax.ppermute(down_corner, all_axes, corners(falling))  9.98 us
    ppermute x1, waiting for transfers between devices, on_device(): after = lax.ppermute(down, block_axes, falling)  9.02 us
    all_to_all x1, starting transfers between devices, on_device(): lax.all_to_all(payload, 'dom', split_axis=0, concat_axis=0, tiled=True)  6.62 us
    ppermute x1, starting transfers between devices, on_device(): before = lax.ppermute(up, block_axes, rising)  6.38 us
    ppermute x1, starting transfers between devices, on_device(): before_corner = lax.ppermute(up_corner, all_axes, corners(rising))  5.99 us
    unnamed x31, local copies, waits for them, and re-layouts  3.95 us
  transfers between devices with their start and end apart: 9, of which 4 were waited for; matrix products, arithmetic and copies ran while one was open for 1% of the time, Pallas kernels for 22%

profile of v1, /device:TPU:95, one launch (start us, length us, event | category | flops | bytes accessed | tf_op | source)
XLA Modules:
  0.0 82.7 jit_solution(9668694611212236898)
XLA Ops:
  0.6 0.0 copy-start
  0.6 1.3 %copy-done = f32[40,8,1024]{2,1,0:T(8,128)S(1)} copy-done((f32[40,8,1024]{2,1,0:T(8,128)S(1)}, f32[40,8,1024]{2,1,0:T(8,128)}, u32[]{:S(2)}) %copy-start) | copy-done | bytes 1310744
  2.0 0.8 copy-done.4
  2.7 0.8 copy-done.6
  3.5 0.2 pack_ocean.1
  3.7 6.4 %collective-permute-start.1 = (f32[42,4,1024]{2,1,0:T(4,128)S(1)}, f32[42,4,1024]{2,1,0:T(4,128)S(1)}, u32[]{:S(2)}, u32[]{:S(2)}) collective-permute-start(f32[42,4,1024]{2,1,0:T(4,128)S(1)} %get-tuple-element.11), channel_id=1, source_target_pairs={{0,2},{2,4},{4,6},{6,8},{8,10},{10,12},{12,14},{14,16},{16,18},{18... | collective-permute-start | bytes 2064392 | tf_op jit(solution)/shard_map/ppermute | solution.py:412
  10.0 1.9 %collective-permute-start.2 = (f32[42,4,1024]{2,1,0:T(4,128)S(1)}, f32[42,4,1024]{2,1,0:T(4,128)S(1)}, u32[]{:S(2)}, u32[]{:S(2)}) collective-permute-start(f32[42,4,1024]{2,1,0:T(4,128)S(1)} %get-tuple-element.12), channel_id=1, source_target_pairs={{2,0},{4,2},{6,4},{8,6},{10,8},{12,10},{14,12},{16,14},{18,16},{20... | collective-permute-start | bytes 2064392 | tf_op jit(solution)/shard_map/ppermute | solution.py:413
  12.0 0.0 copy-done.12
  12.0 0.0 copy-start.2
  12.0 1.1 %copy-done.2 = f32[144,1024]{1,0:T(8,128)S(1)} copy-done((f32[144,1024]{1,0:T(8,128)S(1)}, f32[144,1024]{1,0:T(8,128)}, u32[]{:S(2)}) %copy-start.2) | copy-done | bytes 589848
  13.1 0.1 collective-permute-start
  13.2 0.0 copy-start.3
  13.2 0.0 copy-start.8
  13.2 0.0 copy-start.9
  13.2 0.0 copy-start.10
  13.2 0.0 copy-start.11
  13.2 0.0 copy-start.13
  13.2 0.0 copy-start.14
  13.3 0.8 collective-permute-start.4
  14.1 12.9 %collective-permute-done.1.before_ref = f32[42,4,1024]{2,1,0:T(4,128)S(1)} collective-permute-done((f32[42,4,1024]{2,1,0:T(4,128)S(1)}, f32[42,4,1024]{2,1,0:T(4,128)S(1)}, u32[]{:S(2)}, u32[]{:S(2)}) %collective-permute-start.1) | collective-permute-done | bytes 688160 | tf_op jit(solution)/shard_map/ppermute | solution.py:412
  27.0 9.0 %collective-permute-done.2.after_ref = f32[42,4,1024]{2,1,0:T(4,128)S(1)} collective-permute-done((f32[42,4,1024]{2,1,0:T(4,128)S(1)}, f32[42,4,1024]{2,1,0:T(4,128)S(1)}, u32[]{:S(2)}, u32[]{:S(2)}) %collective-permute-start.2) | collective-permute-done | bytes 688160 | tf_op jit(solution)/shard_map/ppermute | solution.py:413
  36.0 0.0 copy-done.1
  36.0 0.4 top_level.1.top_ref
  36.4 0.0 copy-start.5
  36.5 0.0 copy-start.7
  36.5 1.3 %collective-permute-start.3 = (f32[8,1024]{1,0:T(8,128)S(1)}, f32[8,1024]{1,0:T(8,128)S(1)}, u32[]{:S(2)}, u32[]{:S(2)}) collective-permute-start(f32[8,1024]{1,0:T(8,128)S(1)} %top_level.1.top_ref), channel_id=1, source_target_pairs={{0,1},{2,3},{4,5},{6,7},{8,9},{10,11},{12,13},{14,15},{16,17},{18,... | collective-permute-start | bytes 98312 | tf_op jit(solution)/shard_map/ppermute | solution.py:428
  37.8 0.0 collective-permute-done.far_ref
  37.8 1.0 %collective-permute-done.3.top_far_ref = f32[8,1024]{1,0:T(8,128)S(1)} collective-permute-done((f32[8,1024]{1,0:T(8,128)S(1)}, f32[8,1024]{1,0:T(8,128)S(1)}, u32[]{:S(2)}, u32[]{:S(2)}) %collective-permute-start.3) | collective-permute-done | bytes 32800 | tf_op jit(solution)/shard_map/ppermute | solution.py:428
  38.8 0.0 copy-done.3
  38.8 0.0 copy-done.8
  38.8 0.0 copy-done.9
  38.8 0.0 copy-done.10
  38.8 3.6 %columns.1 = (f32[144,1024]{1,0:T(8,128)}, f32[32,512]{1,0:T(8,128)S(1)}) custom-call(f32[144,1024]{1,0:T(8,128)S(1)} %copy-done.3, s32[1,1024]{1,0:T(1,128)S(1)} %bitcast.13, s32[1,1024]{1,0:T(1,128)S(1)} %bitcast.12, f32[144,1024]{1,0:T(8,128)S(1)} %copy-done.2, f32[152,512]{1,0:T(8,128)S(1)} %collective-permute-done.far_ref, f32[144,144]{1,0:T(8,128)S(1)} %copy-done.8, ...), custom_call_target="tpu_custom_call" | custom-call | bytes 18000000 | tf_op jit(solution)/shard_map/columns/pallas_call | solution.py:32
  42.4 0.7 copy.16
  43.1 6.6 %all-to-all-start = ((f32[32,1,512]{2,1,0:T(1,128)}), f32[32,1,512]{2,1,0:T(1,128)S(1)}, u32[]{:S(2)}, u32[]{:S(2)}) async-start(f32[32,1,512]{2,1,0:T(1,128)} %copy.16), calls=%async_computation | async-start | bytes 131072 | tf_op jit(solution)/shard_map/all_to_all | solution.py:452
  49.7 6.0 %collective-permute-start.5 = (f32[4,4,1024]{2,1,0:T(4,128)S(1)}, f32[4,4,1024]{2,1,0:T(4,128)S(1)}, u32[]{:S(2)}, u32[]{:S(2)}) collective-permute-start(f32[4,4,1024]{2,1,0:T(4,128)S(1)} %get-tuple-element.15), channel_id=1, source_target_pairs={{0,3},{1,2},{2,5},{3,4},{4,7},{5,6},{6,9},{7,8},{8,11},{9,10},{10,... | collective-permute-start | bytes 196616 | tf_op jit(solution)/shard_map/ppermute | solution.py:415
  55.7 1.9 %collective-permute-start.6 = (f32[4,4,1024]{2,1,0:T(4,128)S(1)}, f32[4,4,1024]{2,1,0:T(4,128)S(1)}, u32[]{:S(2)}, u32[]{:S(2)}) collective-permute-start(f32[4,4,1024]{2,1,0:T(4,128)S(1)} %get-tuple-element.16), channel_id=1, source_target_pairs={{2,1},{3,0},{4,3},{5,2},{6,5},{7,4},{8,7},{9,6},{10,9},{11,8},{12,... | collective-permute-start | bytes 196616 | tf_op jit(solution)/shard_map/ppermute | solution.py:416
  57.7 0.0 all-to-all-done
  57.7 0.8 add_flux.1
  58.5 0.1 collective-permute-start.7
  58.6 0.0 collective-permute-done.5.before_corner_ref
  58.6 10.0 %collective-permute-done.6.after_corner_ref = f32[4,4,1024]{2,1,0:T(4,128)S(1)} collective-permute-done((f32[4,4,1024]{2,1,0:T(4,128)S(1)}, f32[4,4,1024]{2,1,0:T(4,128)S(1)}, u32[]{:S(2)}, u32[]{:S(2)}) %collective-permute-start.6) | collective-permute-done | bytes 65568 | tf_op jit(solution)/shard_map/ppermute | solution.py:416
  68.5 0.0 collective-permute-done.4.level_ref
  68.5 0.0 copy-done.5
  68.6 12.2 %ocean.1 = f32[40,8,1024]{2,1,0:T(8,128)} custom-call(f32[40,8,1024]{2,1,0:T(8,128)S(1)} %copy-done.1, f32[42,4,1024]{2,1,0:T(4,128)S(1)} %collective-permute-done.1.before_ref, f32[42,4,1024]{2,1,0:T(4,128)S(1)} %collective-permute-done.2.after_ref, f32[4,8,1024]{2,1,0:T(8,128)S(1)} %collective-permute-done.4.level_ref, ...), custom_call_target="tpu_custom_call" | custom-call | bytes 18000000 | tf_op jit(solution)/shard_map/ocean/pallas_call | solution.py:32
  80.8 1.3 %add_warmth.1 = f32[8,128]{1,0:T(8,128)} custom-call(f32[32,512]{1,0:T(8,128)S(1)} %bitcast.9, s32[32,256]{1,0:T(8,128)S(1)} %copy-done.10, f32[32,256]{1,0:T(8,128)S(1)} %copy-done.11), custom_call_target="tpu_custom_call" | custom-call | bytes 6000000 | tf_op jit(solution)/shard_map/add_warmth/pallas_call | solution.py:32
  82.1 0.0 collective-permute-done.7
  82.1 0.6 add.3
  (10 shorter events, 0.0 us)
Async XLA Ops:
  0.6 1.3 %copy-start = (f32[40,8,1024]{2,1,0:T(8,128)S(1)}, f32[40,8,1024]{2,1,0:T(8,128)}, u32[]{:S(2)}) copy-start(f32[40,8,1024]{2,1,0:T(8,128)} %theta_ref.5) | copy-start | bytes 3932164
  1.9 0.8 copy-start.4
  2.7 0.8 copy-start.6
  3.5 8.5 %copy-start.12 = (s32[1024]{0:T(1024)S(1)}, s32[1024]{0:T(1024)}, u32[]{:S(2)}) copy-start(s32[1024]{0:T(1024)} %param.14) | copy-start | bytes 12292
  3.5 32.5 %copy-start.1 = (f32[40,8,1024]{2,1,0:T(8,128)S(1)}, f32[40,8,1024]{2,1,0:T(8,128)}, u32[]{:S(2)}) copy-start(f32[40,8,1024]{2,1,0:T(8,128)} %theta_ref.5) | copy-start | bytes 3932164
  3.7 23.3 %collective-permute-start.1 = (f32[42,4,1024]{2,1,0:T(4,128)S(1)}, f32[42,4,1024]{2,1,0:T(4,128)S(1)}, u32[]{:S(2)}, u32[]{:S(2)}) collective-permute-start(f32[42,4,1024]{2,1,0:T(4,128)S(1)} %get-tuple-element.11), channel_id=1, source_target_pairs={{0,2},{2,4},{4,6},{6,8},{8,10},{10,12},{12,14},{14,16},{16,18},{18... | collective-permute-start | bytes 2064392 | tf_op jit(solution)/shard_map/ppermute | solution.py:412
  10.0 26.0 %collective-permute-start.2 = (f32[42,4,1024]{2,1,0:T(4,128)S(1)}, f32[42,4,1024]{2,1,0:T(4,128)S(1)}, u32[]{:S(2)}, u32[]{:S(2)}) collective-permute-start(f32[42,4,1024]{2,1,0:T(4,128)S(1)} %get-tuple-element.12), channel_id=1, source_target_pairs={{2,0},{4,2},{6,4},{8,6},{10,8},{12,10},{14,12},{16,14},{18,16},{20... | collective-permute-start | bytes 2064392 | tf_op jit(solution)/shard_map/ppermute | solution.py:413
  12.0 1.1 %copy-start.2 = (f32[144,1024]{1,0:T(8,128)S(1)}, f32[144,1024]{1,0:T(8,128)}, u32[]{:S(2)}) copy-start(f32[144,1024]{1,0:T(8,128)} %drive_ref.3) | copy-start | bytes 1769476
  13.1 24.7 %collective-permute-start = (f32[152,512]{1,0:T(8,128)S(1)}, f32[152,512]{1,0:T(8,128)S(1)}, u32[]{:S(2)}, u32[]{:S(2)}) collective-permute-start(f32[152,512]{1,0:T(8,128)S(1)} %pack_forcing.1), channel_id=1, source_target_pairs={{0,32},{2,34},{4,36},{6,38},{8,40},{10,42},{12,44},{14,46},{16,48}... | collective-permute-start | bytes 933896 | tf_op jit(solution)/shard_map/ppermute | solution.py:387
  13.2 25.6 %copy-start.3 = (f32[144,1024]{1,0:T(8,128)S(1)}, f32[144,1024]{1,0:T(8,128)}, u32[]{:S(2)}) copy-start(f32[144,1024]{1,0:T(8,128)} %state_ref.1) | copy-start | bytes 1769476
  13.2 25.6 %copy-start.8 = (f32[144,144]{1,0:T(8,128)S(1)}, f32[144,144]{1,0:T(8,128)}, u32[]{:S(2)}) copy-start(f32[144,144]{1,0:T(8,128)} %link_ref.1) | copy-start | bytes 248836
  13.2 25.6 %copy-start.9 = (s32[32,256]{1,0:T(8,128)S(1)}, s32[32,256]{1,0:T(8,128)}, u32[]{:S(2)}) copy-start(s32[32,256]{1,0:T(8,128)} %tile_ref.3) | copy-start | bytes 98308
  13.2 25.6 %copy-start.10 = (s32[32,256]{1,0:T(8,128)S(1)}, s32[32,256]{1,0:T(8,128)}, u32[]{:S(2)}) copy-start(s32[32,256]{1,0:T(8,128)} %sender_ref.3) | copy-start | bytes 98308
  13.2 25.6 %copy-start.11 = (f32[32,256]{1,0:T(8,128)S(1)}, f32[32,256]{1,0:T(8,128)}, u32[]{:S(2)}) copy-start(f32[32,256]{1,0:T(8,128)} %share_ref.3) | copy-start | bytes 98308
  13.2 25.6 %copy-start.13 = (s32[1024]{0:T(1024)S(1)}, s32[1024]{0:T(1024)}, u32[]{:S(2)}) copy-start(s32[1024]{0:T(1024)} %param.13) | copy-start | bytes 12292
  13.2 25.6 %copy-start.14 = (f32[1024]{0:T(1024)S(1)}, f32[1024]{0:T(1024)}, u32[]{:S(2)}) copy-start(f32[1024]{0:T(1024)} %param.17) | copy-start | bytes 12292
  13.3 55.3 %collective-permute-start.4 = (f32[4,8,1024]{2,1,0:T(8,128)S(1)}, f32[4,8,1024]{2,1,0:T(8,128)S(1)}, u32[]{:S(2)}, u32[]{:S(2)}) collective-permute-start(f32[4,8,1024]{2,1,0:T(8,128)S(1)} %get-tuple-element.14), channel_id=1, source_target_pairs={{0,1},{1,0},{2,3},{3,2},{4,5},{5,4},{6,7},{7,6},{8,9},{9,8},{10,11... | collective-permute-start | bytes 393224 | tf_op jit(solution)/shard_map/ppermute | solution.py:414
  36.4 32.1 %copy-start.5 = (f32[8,1024]{1,0:T(8,128)S(1)}, f32[8,1024]{1,0:T(8,128)}, u32[]{:S(2)}) copy-start(f32[8,1024]{1,0:T(8,128)} %inflow_ref.5) | copy-start | bytes 98308
  36.5 32.1 %copy-start.7 = (s32[8,1024]{1,0:T(8,128)S(1)}, s32[8,1024]{1,0:T(8,128)}, u32[]{:S(2)}) copy-start(s32[8,1024]{1,0:T(8,128)} %wet_ref.5) | copy-start | bytes 98308
  36.5 2.3 %collective-permute-start.3 = (f32[8,1024]{1,0:T(8,128)S(1)}, f32[8,1024]{1,0:T(8,128)S(1)}, u32[]{:S(2)}, u32[]{:S(2)}) collective-permute-start(f32[8,1024]{1,0:T(8,128)S(1)} %top_level.1.top_ref), channel_id=1, source_target_pairs={{0,1},{2,3},{4,5},{6,7},{8,9},{10,11},{12,13},{14,15},{16,17},{18,... | collective-permute-start | bytes 98312 | tf_op jit(solution)/shard_map/ppermute | solution.py:428
  43.1 14.6 %all-to-all-start = ((f32[32,1,512]{2,1,0:T(1,128)}), f32[32,1,512]{2,1,0:T(1,128)S(1)}, u32[]{:S(2)}, u32[]{:S(2)}) async-start(f32[32,1,512]{2,1,0:T(1,128)} %copy.16), calls=%async_computation | async-start | bytes 131072 | tf_op jit(solution)/shard_map/all_to_all | solution.py:452
  49.7 8.8 %collective-permute-start.5 = (f32[4,4,1024]{2,1,0:T(4,128)S(1)}, f32[4,4,1024]{2,1,0:T(4,128)S(1)}, u32[]{:S(2)}, u32[]{:S(2)}) collective-permute-start(f32[4,4,1024]{2,1,0:T(4,128)S(1)} %get-tuple-element.15), channel_id=1, source_target_pairs={{0,3},{1,2},{2,5},{3,4},{4,7},{5,6},{6,9},{7,8},{8,11},{9,10},{10,... | collective-permute-start | bytes 196616 | tf_op jit(solution)/shard_map/ppermute | solution.py:415
  55.7 12.8 %collective-permute-start.6 = (f32[4,4,1024]{2,1,0:T(4,128)S(1)}, f32[4,4,1024]{2,1,0:T(4,128)S(1)}, u32[]{:S(2)}, u32[]{:S(2)}) collective-permute-start(f32[4,4,1024]{2,1,0:T(4,128)S(1)} %get-tuple-element.16), channel_id=1, source_target_pairs={{2,1},{3,0},{4,3},{5,2},{6,5},{7,4},{8,7},{9,6},{10,9},{11,8},{12,... | collective-permute-start | bytes 196616 | tf_op jit(solution)/shard_map/ppermute | solution.py:416
  58.5 23.6 %collective-permute-start.7 = (f32[8,1024]{1,0:T(8,128)S(1)}, f32[8,1024]{1,0:T(8,128)S(1)}, u32[]{:S(2)}, u32[]{:S(2)}) collective-permute-start(f32[8,1024]{1,0:T(8,128)S(1)} %add_flux.1), channel_id=1, source_target_pairs={{0,1},{1,0},{2,3},{3,2},{4,5},{5,4},{6,7},{7,6},{8,9},{9,8},{10,11... | collective-permute-start | bytes 98312 | tf_op jit(solution)/shard_map/ppermute | solution.py:481

commit v2 on v1

--- a/solution.py
+++ b/solution.py
@@ -59,31 +59,61 @@
     return lax.dot_general(a, b, (((1,), (0,)), ((), ())), preferred_element_type=f32)
 
 
-def pack_forcing(drive_ref, place_ref, out_ref):
-    rows, half = drive_ref.shape
-    out_ref[0:rows, :] = drive_ref[...]
-    far = place_ref[:, half : 2 * half].astype(f32)
-    out_ref[rows : rows + SUBLANES, :] = jnp.broadcast_to(far, (SUBLANES, half))
-
-
-def pack_ocean(theta_ref, inflow_ref, wet_ref, up_ref, down_ref, level_ref, up_corner_ref, down_corner_ref):
+def pack_first(
+    drive_ref,
+    place_ref,
+    theta_ref,
+    inflow_ref,
+    wet_ref,
+    far_ref,
+    up_ref,
+    down_ref,
+    level_ref,
+    place,
+    surface,
+    inflow,
+    wet,
+    sems,
+):
+    rows = drive_ref.shape[0]
+    half = far_ref.shape[1]
     tiers = theta_ref.shape[0]
-    up_ref[0] = inflow_ref[4:8, :]
-    down_ref[0] = inflow_ref[0:4, :]
-    up_ref[1] = wet_ref[4:8, :].astype(f32)
-    down_ref[1] = wet_ref[0:4, :].astype(f32)
-
-    def copy_level(tier, carry):
-        up_ref[tier + 2] = theta_ref[tier, 4:8, :]
-        down_ref[tier + 2] = theta_ref[tier, 0:4, :]
-        return carry
-
-    lax.fori_loop(0, tiers, copy_level, 0, unroll=4)
     base = jnp.where(lax.axis_index("lev") == 0, tiers - STEPS, 0)
+    pairs = (
+        (drive_ref.at[:, half : 2 * half], far_ref.at[0:rows, :]),
+        (place_ref, place),
+        (theta_ref.at[0 : STEPS + 1], surface),
+        (inflow_ref, inflow),
+        (wet_ref, wet),
+        (theta_ref.at[pl.ds(base, STEPS)], level_ref),
+    )
+    copies = [pltpu.make_async_copy(a, b, sems.at[k]) for k, (a, b) in enumerate(pairs)]
+    for copy in copies:
+        copy.start()
+    for copy in copies[1:5]:
+        copy.wait()
+    far = place[:, half : 2 * half].astype(f32)
+    far_ref[rows : rows + SUBLANES, :] = jnp.broadcast_to(far, (SUBLANES, half))
+    up_ref[0] = inflow[4:8, :]
+    down_ref[0] = inflow[0:4, :]
+    up_ref[1] = wet[4:8, :].astype(f32)
+    down_ref[1] = wet[0:4, :].astype(f32)
+    for k in range(STEPS + 1):
+        up_ref[k + 2] = surface[k, 4:8, :]
+        down_ref[k + 2] = surface[k, 0:4, :]
+    copies[0].wait()
+    copies[5].wait()
+
+
+def pack_bulk(theta_ref, level_ref, up_ref, down_ref):
+    skip = STEPS + 1
+    deep = theta_ref.shape[0] - skip
+    for k in range(deep):
+        up_ref[k] = theta_ref[k + skip, 4:8, :]
+        down_ref[k] = theta_ref[k + skip, 0:4, :]
     for j in range(STEPS):
-        level_ref[j] = theta_ref[base + j]
-        up_corner_ref[j] = theta_ref[base + j, 4:8, :]
-        down_corner_ref[j] = theta_ref[base + j, 0:4, :]
+        up_ref[deep + j] = level_ref[j, 4:8, :]
+        down_ref[deep + j] = level_ref[j, 0:4, :]
 
 
 def across(own, halo):
@@ -133,9 +163,9 @@
     theta_ref,
     before_ref,
     after_ref,
+    before_bulk_ref,
+    after_bulk_ref,
     level_ref,
-    before_corner_ref,
-    after_corner_ref,
     inflow_ref,
     wet_ref,
     out_ref,
@@ -146,8 +176,10 @@
     rise,
     source,
 ):
-    tiers = theta_ref.shape[0]
+    tiers, lines, span = theta_ref.shape
+    chunks = span // LANES
     places = tiers + STEPS
+    skip = STEPS + 1
     lev = lax.axis_index("lev")
     lower = lev.astype(f32)
     upper = 1.0 - lower
@@ -162,58 +194,87 @@
         rise[rows, :] = vertical_rate * wet
         source[rows, :] = (flux_gain * upper) * (wet * flow)
 
-    def gather_level(tier, carry):
-        even[tier, 0:8, :] = theta_ref[tier]
-        even[tier, 8:12, :] = after_ref[tier + 2]
-        even[tier, 12:16, :] = before_ref[tier + 2]
-        return carry
-
-    lax.fori_loop(0, tiers, gather_level, 0, unroll=2)
-    for j in range(STEPS):
-        even[tiers + j, 0:8, :] = level_ref[j]
-        even[tiers + j, 8:12, :] = after_corner_ref[j]
-        even[tiers + j, 12:16, :] = before_corner_ref[j]
+    for at in range(places):
+        even[at, 0:8, :] = theta_ref[at] if at < tiers else level_ref[at - tiers]
+        even[at, 8:12, :] = after_ref[at + 2] if at < skip else after_bulk_ref[at - skip]
+        even[at, 12:16, :] = before_ref[at + 2] if at < skip else before_bulk_ref[at - skip]
+
+    row = lax.broadcasted_iota(i32, (SUBLANES, LANES), 0)
+    lane = lax.broadcasted_iota(i32, (SUBLANES, LANES), 1)
+    first, last = row == 0, row == SUBLANES - 1
+    lane_first, lane_last = lane == 0, lane == LANES - 1
 
     for step in range(1, STEPS + 1):
         held, fresh = (even, odd) if step % 2 else (odd, even)
         final = step == STEPS
+        parts = (0,) if final else (0, 8)
 
         def advance(at, less, more, less_scale=None, more_scale=None, add_source=False):
-            own, halo = held[at, 0:8, :], held[at, 8:16, :]
-            sums = across(own, halo)
-            for part, start in ((0, 0), (1, 8)):
-                if final and part == 1:
-                    continue
-                rows = slice(start, start + 8)
-                a, b = held[less, rows, :], held[more, rows, :]
-                if less_scale is not None:
-                    a = a * less_scale
-                if more_scale is not None:
-                    b = b * more_scale
-                new = (
-                    keep[rows, :] * (own, halo)[part]
-                    + side[rows, :] * sums[part]
-                    + rise[rows, :] * (a + b)
-                )
-                if add_source:
-                    new = new + source[rows, :]
-                if final:
-                    out_ref[at] = new
-                else:
-                    fresh[at, rows, :] = new
+            value = {
+                (p, c): held[at, p : p + 8, c * LANES : (c + 1) * LANES]
+                for p in (0, 8)
+                for c in range(chunks)
+            }
+            right = {(p, c): pltpu.roll(value[p, c], 1, 1) for p in parts for c in range(chunks)}
+            left = {(p, c): pltpu.roll(value[p, c], LANES - 1, 1) for p in parts for c in range(chunks)}
+            for c in range(chunks):
+                cols = slice(c * LANES, (c + 1) * LANES)
+                own, halo = value[0, c], value[8, c]
+                less_rows = {0: pltpu.roll(own, 1, 0), 8: pltpu.roll(halo, 1, 0)}
+                more_rows = {0: pltpu.roll(own, 7, 0), 8: pltpu.roll(halo, 7, 0)}
+                for p in parts:
+                    around = jnp.where(first, less_rows[8 - p], less_rows[p])
+                    around = around + jnp.where(last, more_rows[8 - p], more_rows[p])
+                    along = jnp.where(lane_first, right[p, (c - 1) % chunks], right[p, c])
+                    along = along + jnp.where(lane_last, left[p, (c + 1) % chunks], left[p, c])
+                    rows = slice(p, p + 8)
+                    a, b = held[less, rows, cols], held[more, rows, cols]
+                    if less_scale is not None:
+                        a = a * less_scale
+                    if more_scale is not None:
+                        b = b * more_scale
+                    new = (
+                        keep[rows, cols] * value[p, c]
+                        + side[rows, cols] * (around + along)
+                        + rise[rows, cols] * (a + b)
+                    )
+                    if add_source:
+                        new = new + source[rows, cols]
+                    if final:
+                        out_ref[at, :, cols] = new
+                    else:
+                        fresh[at, rows, cols] = new
 
         advance(0, places - 1, 1, less_scale=lower, add_source=True)
-
-        def inner(at, carry):
+        for at in range(1, tiers - 1):
             advance(at, at - 1, at + 1)
-            return carry
-
-        lax.fori_loop(1, tiers - 1, inner, 0, unroll=2)
         advance(tiers - 1, tiers - 2, tiers, more_scale=upper)
         for j in range(STEPS - step):
             at = tiers + j + lev * step
             more = jnp.where(at == places - 1, 0, at + 1)
             advance(at, at - 1, more)
+
+
+def entry_blocks(ref):
+    rows, slots = ref.shape
+    return [
+        (slice(r, r + SUBLANES), slice(c, c + LANES))
+        for r in range(0, rows, SUBLANES)
+        for c in range(0, slots, LANES)
+    ]
+
+
+def picked(tables, keys, lanes):
+    found = [jnp.zeros((SUBLANES, LANES), f32) for _ in keys]
+    for r, table in enumerate(tables):
+        spread = jnp.broadcast_to(table, (SUBLANES, LANES))
+        found = [
+            jnp.where(
+                k == r, jnp.take_along_axis(spread, l, axis=1, mode="promise_in_bounds"), v
+            )
+            for k, l, v in zip(keys, lanes, found)
+        ]
+    return found
 
 
 def columns(
@@ -226,11 +287,8 @@
     warmth_ref,
     sender_ref,
     share_ref,
-    tile_ref,
-    top_ref,
-    top_far_ref,
     out_ref,
-    payload_ref,
+    pieces_ref,
 ):
     rows, count = state_ref.shape
     half = drive_ref.shape[1]
@@ -266,42 +324,27 @@
         )
     flux = jnp.concatenate(flux, axis=1)
 
-    entry_rows, slots = sender_ref.shape
-    blocks = [
-        (slice(r, r + SUBLANES), slice(c, c + LANES))
-        for r in range(0, entry_rows, SUBLANES)
-        for c in range(0, slots, LANES)
-    ]
-    block_shape = (SUBLANES, LANES)
-
-    def picked(table, lane):
-        spread = jnp.broadcast_to(table, block_shape)
-        return jnp.take_along_axis(spread, lane, axis=1, mode="promise_in_bounds")
-
+    blocks = entry_blocks(sender_ref)
     lanes = [sender_ref[b] & (LANES - 1) for b in blocks]
     keys = [sender_ref[b] >> 7 for b in blocks]
-    found = [jnp.zeros(block_shape, f32) for _ in blocks]
-    for r in range(count // LANES):
-        table = flux[:, r * LANES : (r + 1) * LANES]
-        found = [jnp.where(k == r, picked(table, l), v) for k, l, v in zip(keys, lanes, found)]
-    for b, v in zip(blocks, found):
-        payload_ref[b] = share_ref[b] * v
-
+    tables = [flux[:, r * LANES : (r + 1) * LANES] for r in range(count // LANES)]
+    for b, v in zip(blocks, picked(tables, keys, lanes)):
+        pieces_ref[b] = share_ref[b] * v
+
+
+def targets(tile_ref, top_ref, top_far_ref, pieces_ref, payload_ref):
     lines, span = top_ref.shape
     surface = jnp.where(lax.axis_index("lev") == 0, top_ref[...], top_far_ref[...])
-    chunks = span // LANES
+    blocks = entry_blocks(tile_ref)
     lanes = [tile_ref[b] & (LANES - 1) for b in blocks]
     keys = [tile_ref[b] >> 7 for b in blocks]
-    found = [jnp.zeros(block_shape, f32) for _ in blocks]
-    for r in range(lines):
-        for c in range(chunks):
-            table = surface[r : r + 1, c * LANES : (c + 1) * LANES]
-            found = [
-                jnp.where(k == r * chunks + c, picked(table, l), v)
-                for k, l, v in zip(keys, lanes, found)
-            ]
-    for (r, c), v in zip(blocks, found):
-        payload_ref[r, slots + c.start : slots + c.stop] = v
+    tables = [
+        surface[r : r + 1, c : c + LANES] for r in range(lines) for c in range(0, span, LANES)
+    ]
+    for (r, c), v in zip(blocks, picked(tables, keys, lanes)):
+        part = c.start // LANES
+        payload_ref[pl.ds(4 * r.start + part, SUBLANES, stride=4), :] = pieces_ref[r, c]
+        payload_ref[pl.ds(4 * r.start + 2 + part, SUBLANES, stride=4), :] = v
 
 
 def entry_sum(index_row, value_row, groups, order):
@@ -316,6 +359,10 @@
     lane = index_row & (LANES - 1)
     lane_hit = lax.broadcasted_iota(i32, (LANES, entries), 0) == lane
     return dot_nt(weighted, jnp.where(lane_hit, 1.0, 0.0).astype(bf16))
+
+
+def joined_rows(ref, at):
+    return jnp.concatenate([ref[at : at + 1, :], ref[at + 1 : at + 2, :]], axis=1)
 
 
 def add_flux(received_ref, tile_ref, out_ref):
@@ -327,7 +374,7 @@
     for d in range(entry_rows):
         total = total + entry_sum(
             tile_ref[d : d + 1, :],
-            received_ref[d : d + 1, 0:slots],
+            joined_rows(received_ref, 4 * d),
             groups,
             lambda t: ((t >> 7) & (chunks - 1)) * lines + (t >> 10),
         )
@@ -343,7 +390,7 @@
     for d in range(entry_rows):
         total = total + entry_sum(
             sender_ref[d : d + 1, :],
-            received_ref[d : d + 1, slots : 2 * slots] * share_ref[d : d + 1, :],
+            joined_rows(received_ref, 4 * d + 2) * share_ref[d : d + 1, :],
             groups,
             lambda t: t >> 7,
         )
@@ -368,52 +415,61 @@
     half = count // 2
     tiers, lines, span = marine_warmth_departure.shape
     entry_rows, slots = intersect_sender_index.shape
-    n_dom, n_lev = lax.axis_size("dom"), lax.axis_size("lev")
+    n_dom = lax.axis_size("dom")
     n_block = lax.axis_size("comp") * n_dom
     place = position_profile_map.reshape(1, count)
 
     def shape(*dims):
         return jax.ShapeDtypeStruct(dims, f32)
 
-    packed = call(
-        pack_forcing,
-        shape(rows + SUBLANES, half),
-        [pl.BlockSpec((rows, half), lambda i: (0, 1)), whole()],
-        (sunlight_aerosol_drive, place),
-        "pack_forcing",
+    packed, up, down, level = call(
+        pack_first,
+        [
+            shape(rows + SUBLANES, half),
+            shape(STEPS + 3, 4, span),
+            shape(STEPS + 3, 4, span),
+            shape(STEPS, lines, span),
+        ],
+        [pl.BlockSpec(memory_space=pl.ANY)] * 5,
+        (
+            sunlight_aerosol_drive,
+            place,
+            marine_warmth_departure,
+            earlier_bottom_inflow,
+            marine_tile_indicator,
+        ),
+        "pack_first",
         1.5,
-        grid=(1,),
-    )
-    far = lax.ppermute(packed, "dom", [(i, (i + n_dom // 2) % n_dom) for i in range(n_dom)])
-
-    up, down, level, up_corner, down_corner = call(
-        pack_ocean,
-        [
-            shape(tiers + 2, 4, span),
-            shape(tiers + 2, 4, span),
-            shape(STEPS, lines, span),
-            shape(STEPS, 4, span),
-            shape(STEPS, 4, span),
+        scratch=[
+            pltpu.VMEM((1, count), i32),
+            pltpu.VMEM((STEPS + 1, lines, span), f32),
+            pltpu.VMEM((lines, span), f32),
+            pltpu.VMEM((lines, span), i32),
+            pltpu.SemaphoreType.DMA((6,)),
         ],
-        [whole()] * 3,
-        (marine_warmth_departure, earlier_bottom_inflow, marine_tile_indicator),
-        "pack_ocean",
-        2.0,
+        mib=56,
     )
     block_axes = ("comp", "dom")
-    all_axes = ("comp", "dom", "lev")
     rising = [(i, i + 1) for i in range(n_block - 1)]
     falling = [(j, i) for i, j in rising]
     other = [(0, 1), (1, 0)]
 
-    def corners(pairs):
-        return [(a * n_lev + l, b * n_lev + m) for a, b in pairs for l, m in other]
-
+    far = lax.ppermute(packed, "dom", [(i, (i + n_dom // 2) % n_dom) for i in range(n_dom)])
+    level = lax.ppermute(level, "lev", other)
     before = lax.ppermute(up, block_axes, rising)
     after = lax.ppermute(down, block_axes, falling)
-    level = lax.ppermute(level, "lev", other)
-    before_corner = lax.ppermute(up_corner, all_axes, corners(rising))
-    after_corner = lax.ppermute(down_corner, all_axes, corners(falling))
+    later_level, before, after, far = lax.optimization_barrier((level, before, after, far))
+    bulk = tiers - 1
+    up_bulk, down_bulk = call(
+        pack_bulk,
+        [shape(bulk, 4, span), shape(bulk, 4, span)],
+        [whole()] * 2,
+        (marine_warmth_departure, later_level),
+        "pack_bulk",
+        1.0,
+    )
+    before_bulk = lax.ppermute(up_bulk, block_axes, rising)
+    after_bulk = lax.ppermute(down_bulk, block_axes, falling)
 
     part = pl.BlockSpec((STEPS + 3, 4, span), lambda i: (0, 0, 0))
     top = call(
@@ -422,15 +478,15 @@
         [pl.BlockSpec((STEPS + 1, lines, span), lambda i: (0, 0, 0)), part, part, whole(), whole()],
         (marine_warmth_departure, before, after, earlier_bottom_inflow, marine_tile_indicator),
         "top_level",
-        2.0,
+        1.0,
         grid=(1,),
     )
     top_far = lax.ppermute(top, "lev", [(0, 1)])
 
-    air_profile_updated, payload = call(
+    air_profile_updated, pieces = call(
         columns,
-        [shape(rows, count), shape(entry_rows, 2 * slots)],
-        [whole()] * 3 + [pl.BlockSpec((rows, half), lambda i: (0, 0))] + [whole()] * 8,
+        [shape(rows, count), shape(entry_rows, slots)],
+        [whole()] * 3 + [pl.BlockSpec((rows, half), lambda i: (0, 0))] + [whole()] * 5,
         (
             air_profile_vector,
             profile_pass_kind.reshape(1, count),
@@ -441,15 +497,22 @@
             bottom_warmth_seen.reshape(1, count),
             intersect_sender_index,
             intersect_share,
-            intersect_receiver_tile,
-            top,
-            top_far,
         ),
         "columns",
-        6.0,
+        4.0,
         grid=(1,),
     )
-    received = lax.all_to_all(payload, "dom", split_axis=0, concat_axis=0, tiled=True)
+    payload = call(
+        targets,
+        shape(4 * entry_rows, LANES),
+        [whole()] * 4,
+        (intersect_receiver_tile, top, top_far, pieces),
+        "targets",
+        1.0,
+    )
+    received = lax.all_to_all(
+        payload.reshape(entry_rows, 4, LANES), "dom", split_axis=0, concat_axis=0, tiled=True
+    ).reshape(4 * entry_rows, LANES)
 
     theta = call(
         ocean,
@@ -459,9 +522,9 @@
             marine_warmth_departure,
             before,
             after,
+            before_bulk,
+            after_bulk,
             level,
-            before_corner,
-            after_corner,
             earlier_bottom_inflow,
             marine_tile_indicator,
         ),

time: 83.2 us -> 70.9 us (0.85)
  the two profiles are of different devices: /device:TPU:95 before, /device:TPU:64 now
where the time goes in v2:
time: 70.9 us; the launch traced here: 70.5 us
  starting transfers between devices  30.5 us (43%)
  blocking collectives  17.2 us (24%)
  Pallas kernels  17.1 us (24%)
  waiting for transfers between devices  4.03 us (6%)
  between operations  0.89 us (1%)
    all_to_all x1, blocking collectives, on_device(): lax.all_to_all(payload.reshape(entry_rows, 4, LANES), 'dom', split_axis=0...  17.2 us
    pallas_call x8, Pallas kernels, call(): pl.pallas_call(body, out_shape=shapes, grid=grid, in_specs=specs, out_spe...  17.1 us
    ppermute x1, starting transfers between devices, on_device(): after = lax.ppermute(down, block_axes, falling)  8.89 us
    ppermute x1, starting transfers between devices, on_device(): after_bulk = lax.ppermute(down_bulk, block_axes, falling)  8.83 us
    ppermute x1, starting transfers between devices, on_device(): lax.ppermute(packed, 'dom', [(i, (i + n_dom // 2) % n_dom) for i in range...  3.28 us
    ppermute x1, waiting for transfers between devices, on_device(): after = lax.ppermute(down, block_axes, falling)  2.86 us
    ppermute x1, starting transfers between devices, on_device(): lax.ppermute(partial_flux, 'lev', other)  2.45 us
    ppermute x1, starting transfers between devices, on_device(): before_bulk = lax.ppermute(up_bulk, block_axes, rising)  1.92 us
  transfers between devices with their start and end apart: 8, of which 3 were waited for; matrix products, arithmetic and copies ran while one was open for 1% of the time, Pallas kernels for 11%

profile of v2, /device:TPU:64, one launch (start us, length us, event | category | flops | bytes accessed | tf_op | source)
XLA Modules:
  0.0 70.5 jit_solution(11777000159190624764)
XLA Ops:
  0.6 0.0 copy-start
  0.6 0.0 copy-start.3
  0.7 0.0 copy-start.4
  0.7 2.1 %pack_first.1 = (f32[152,512]{1,0:T(8,128)}, f32[7,4,1024]{2,1,0:T(4,128)}, f32[7,4,1024]{2,1,0:T(4,128)}, f32[4,8,1024]{2,1,0:T(8,128)}) custom-call(f32[144,1024]{1,0:T(8,128)} %drive_ref.3, s32[1,1024]{1,0:T(1,128)} %bitcast.9, f32[40,8,1024]{2,1,0:T(8,128)} %theta_ref.7, f32[8,1024]{1,0:T(8,128)} %inflow_ref.5, s32[8,1024]{1,0:T(8,128)} %wet_ref.5), custom_call_target="tpu_custom_call" | custom-call | bytes 4500000 | tf_op jit(solution)/shard_map/pack_first/pallas_call | solution.py:32
  2.8 3.3 %collective-permute-start.3 = (f32[152,512]{1,0:T(8,128)}, f32[152,512]{1,0:T(8,128)S(1)}, u32[]{:S(2)}, u32[]{:S(2)}) collective-permute-start(f32[152,512]{1,0:T(8,128)} %get-tuple-element.19), channel_id=1, source_target_pairs={{0,32},{2,34},{4,36},{6,38},{8,40},{10,42},{12,44},{14,46},{16,48}... | collective-permute-start | bytes 933896 | tf_op jit(solution)/shard_map/ppermute | solution.py:457
  6.1 1.9 %collective-permute-start = (f32[4,8,1024]{2,1,0:T(8,128)}, f32[4,8,1024]{2,1,0:T(8,128)S(1)}, u32[]{:S(2)}, u32[]{:S(2)}) collective-permute-start(f32[4,8,1024]{2,1,0:T(8,128)} %get-tuple-element.16), channel_id=1, source_target_pairs={{0,1},{1,0},{2,3},{3,2},{4,5},{5,4},{6,7},{7,6},{8,9},{9,8},{10,11... | collective-permute-start | bytes 393224 | tf_op jit(solution)/shard_map/ppermute | solution.py:458
  8.0 1.9 %collective-permute-start.1 = (f32[7,4,1024]{2,1,0:T(4,128)}, f32[7,4,1024]{2,1,0:T(4,128)S(1)}, u32[]{:S(2)}, u32[]{:S(2)}) collective-permute-start(f32[7,4,1024]{2,1,0:T(4,128)} %get-tuple-element.17), channel_id=1, source_target_pairs={{0,2},{2,4},{4,6},{6,8},{8,10},{10,12},{12,14},{14,16},{16,18},{18... | collective-permute-start | bytes 344072 | tf_op jit(solution)/shard_map/ppermute | solution.py:459
  9.9 0.0 copy-start.1
  9.9 0.0 copy-start.2
  9.9 0.0 copy-start.5
  9.9 0.0 copy-start.7
  9.9 0.0 copy-start.8
  10.0 0.0 copy-start.9
  10.0 0.0 copy-start.10
  10.0 0.0 copy-start.11
  10.0 8.9 %collective-permute-start.2 = (f32[7,4,1024]{2,1,0:T(4,128)}, f32[7,4,1024]{2,1,0:T(4,128)S(1)}, u32[]{:S(2)}, u32[]{:S(2)}) collective-permute-start(f32[7,4,1024]{2,1,0:T(4,128)} %get-tuple-element.18), channel_id=1, source_target_pairs={{2,0},{4,2},{6,4},{8,6},{10,8},{12,10},{14,12},{16,14},{18,16},{20... | collective-permute-start | bytes 344072 | tf_op jit(solution)/shard_map/ppermute | solution.py:460
  18.9 0.5 collective-permute-done.1.before_ref
  19.4 2.9 %collective-permute-done.2.after_ref = f32[7,4,1024]{2,1,0:T(4,128)S(1)} collective-permute-done((f32[7,4,1024]{2,1,0:T(4,128)}, f32[7,4,1024]{2,1,0:T(4,128)S(1)}, u32[]{:S(2)}, u32[]{:S(2)}) %collective-permute-start.2) | collective-permute-done | bytes 114720 | tf_op jit(solution)/shard_map/ppermute | solution.py:460
  22.3 0.0 collective-permute-done.level_ref
  22.3 0.0 collective-permute-done.3.far_ref
  22.3 0.0 copy-done
  22.3 0.1 pack_bulk.1
  22.4 1.9 %collective-permute-start.4 = (f32[39,4,1024]{2,1,0:T(4,128)S(1)}, f32[39,4,1024]{2,1,0:T(4,128)S(1)}, u32[]{:S(2)}, u32[]{:S(2)}) collective-permute-start(f32[39,4,1024]{2,1,0:T(4,128)S(1)} %get-tuple-element.25), channel_id=1, source_target_pairs={{0,2},{2,4},{4,6},{6,8},{8,10},{10,12},{12,14},{14,16},{16,18},{18... | collective-permute-start | bytes 1916936 | tf_op jit(solution)/shard_map/ppermute | solution.py:471
  24.3 0.0 copy-start.6
  24.3 8.8 %collective-permute-start.5 = (f32[39,4,1024]{2,1,0:T(4,128)S(1)}, f32[39,4,1024]{2,1,0:T(4,128)S(1)}, u32[]{:S(2)}, u32[]{:S(2)}) collective-permute-start(f32[39,4,1024]{2,1,0:T(4,128)S(1)} %get-tuple-element.26), channel_id=1, source_target_pairs={{2,0},{4,2},{6,4},{8,6},{10,8},{12,10},{14,12},{16,14},{18,16},{20... | collective-permute-start | bytes 1916936 | tf_op jit(solution)/shard_map/ppermute | solution.py:472
  33.1 0.0 copy-done.3
  33.2 0.0 copy-done.4
  33.2 0.4 top_level.1.top_ref
  33.6 1.3 %collective-permute-start.6 = (f32[8,1024]{1,0:T(8,128)S(1)}, f32[8,1024]{1,0:T(8,128)S(1)}, u32[]{:S(2)}, u32[]{:S(2)}) collective-permute-start(f32[8,1024]{1,0:T(8,128)S(1)} %top_level.1.top_ref), channel_id=1, source_target_pairs={{0,1},{2,3},{4,5},{6,7},{8,9},{10,11},{12,13},{14,15},{16,17},{18,... | collective-permute-start | bytes 98312 | tf_op jit(solution)/shard_map/ppermute | solution.py:484
  34.9 0.0 copy-done.1
  35.0 0.0 copy-done.2
  35.0 0.0 copy-done.5
  35.0 0.0 copy-done.7
  35.0 0.0 copy-done.8
  35.0 0.0 copy-done.9
  35.0 3.6 %columns.1 = (f32[144,1024]{1,0:T(8,128)}, f32[32,256]{1,0:T(8,128)S(1)}) custom-call(f32[144,1024]{1,0:T(8,128)S(1)} %copy-done.2, s32[1,1024]{1,0:T(1,128)S(1)} %bitcast.11, s32[1,1024]{1,0:T(1,128)S(1)} %bitcast.10, f32[144,1024]{1,0:T(8,128)S(1)} %copy-done.1, f32[152,512]{1,0:T(8,128)S(1)} %collective-permute-done.3.far_ref, f32[144,144]{1,0:T(8,128)S(1)} %copy-done.5, ...), custom_call_target="tpu_custom_call" | custom-call | bytes 12000000 | tf_op jit(solution)/shard_map/columns/pallas_call | solution.py:32
  38.6 0.0 collective-permute-done.6.top_far_ref
  38.6 0.0 copy-done.6
  38.6 1.5 %targets.1 = f32[128,128]{1,0:T(8,128)S(1)} custom-call(s32[32,256]{1,0:T(8,128)S(1)} %copy-done.6, f32[8,1024]{1,0:T(8,128)S(1)} %top_level.1.top_ref, f32[8,1024]{1,0:T(8,128)S(1)} %collective-permute-done.6.top_far_ref, f32[32,256]{1,0:T(8,128)S(1)} %get-tuple-element.27.pieces_ref), custom_call_target="tpu_custom_call" | custom-call | bytes 3000000 | tf_op jit(solution)/shard_map/targets/pallas_call | solution.py:32
  40.1 17.2 %all_to_all.5 = f32[32,4,128]{2,1,0:T(4,128)S(1)} all-to-all(f32[32,4,128]{2,1,0:T(4,128)S(1)} %bitcast.8), channel_id=1, replica_groups=mesh['comp'=4,'dom'=32,'lev'=2] {'dom'}, dimensions={0} | all-to-all | bytes 131072 | tf_op jit(solution)/shard_map/all_to_all | solution.py:513
  57.3 0.8 %add_flux.1 = f32[8,1024]{1,0:T(8,128)S(1)} custom-call(f32[128,128]{1,0:T(8,128)S(1)} %bitcast.6, s32[32,256]{1,0:T(8,128)S(1)} %copy-done.6), custom_call_target="tpu_custom_call" | custom-call | bytes 6000000 | tf_op jit(solution)/shard_map/add_flux/pallas_call | solution.py:32
  58.1 2.5 %collective-permute-start.7 = (f32[8,1024]{1,0:T(8,128)S(1)}, f32[8,1024]{1,0:T(8,128)S(1)}, u32[]{:S(2)}, u32[]{:S(2)}) collective-permute-start(f32[8,1024]{1,0:T(8,128)S(1)} %add_flux.1), channel_id=1, source_target_pairs={{0,1},{1,0},{2,3},{3,2},{4,5},{5,4},{6,7},{7,6},{8,9},{9,8},{10,11... | collective-permute-start | bytes 98312 | tf_op jit(solution)/shard_map/ppermute | solution.py:544
  60.6 1.3 %add_warmth.1 = f32[8,128]{1,0:T(8,128)} custom-call(f32[128,128]{1,0:T(8,128)S(1)} %bitcast.7, s32[32,256]{1,0:T(8,128)S(1)} %copy-done.7, f32[32,256]{1,0:T(8,128)S(1)} %copy-done.8), custom_call_target="tpu_custom_call" | custom-call | bytes 6000000 | tf_op jit(solution)/shard_map/add_warmth/pallas_call | solution.py:32
  61.8 0.6 collective-permute-done.7
  62.5 0.6 add.3
  63.1 0.0 collective-permute-done.4.before_bulk_ref
  63.1 0.0 collective-permute-done.5.after_bulk_ref
  63.1 7.4 %ocean.1 = f32[40,8,1024]{2,1,0:T(8,128)} custom-call(f32[40,8,1024]{2,1,0:T(8,128)S(1)} %copy-done, f32[7,4,1024]{2,1,0:T(4,128)S(1)} %collective-permute-done.1.before_ref, f32[7,4,1024]{2,1,0:T(4,128)S(1)} %collective-permute-done.2.after_ref, f32[39,4,1024]{2,1,0:T(4,128)S(1)} %collective-permute-done.4.before_bulk_ref, ...), custom_call_target="tpu_custom_call" | custom-call | bytes 18000000 | tf_op jit(solution)/shard_map/ocean/pallas_call | solution.py:32
  (2 shorter events, 0.0 us)
Async XLA Ops:
  0.6 21.6 %copy-start = (f32[40,8,1024]{2,1,0:T(8,128)S(1)}, f32[40,8,1024]{2,1,0:T(8,128)}, u32[]{:S(2)}) copy-start(f32[40,8,1024]{2,1,0:T(8,128)} %theta_ref.7) | copy-start | bytes 3932164
  0.6 32.5 %copy-start.3 = (f32[8,1024]{1,0:T(8,128)S(1)}, f32[8,1024]{1,0:T(8,128)}, u32[]{:S(2)}) copy-start(f32[8,1024]{1,0:T(8,128)} %inflow_ref.5) | copy-start | bytes 98308
  0.7 32.5 %copy-start.4 = (s32[8,1024]{1,0:T(8,128)S(1)}, s32[8,1024]{1,0:T(8,128)}, u32[]{:S(2)}) copy-start(s32[8,1024]{1,0:T(8,128)} %wet_ref.5) | copy-start | bytes 98308
  2.8 19.5 %collective-permute-start.3 = (f32[152,512]{1,0:T(8,128)}, f32[152,512]{1,0:T(8,128)S(1)}, u32[]{:S(2)}, u32[]{:S(2)}) collective-permute-start(f32[152,512]{1,0:T(8,128)} %get-tuple-element.19), channel_id=1, source_target_pairs={{0,32},{2,34},{4,36},{6,38},{8,40},{10,42},{12,44},{14,46},{16,48}... | collective-permute-start | bytes 933896 | tf_op jit(solution)/shard_map/ppermute | solution.py:457
  6.1 16.2 %collective-permute-start = (f32[4,8,1024]{2,1,0:T(8,128)}, f32[4,8,1024]{2,1,0:T(8,128)S(1)}, u32[]{:S(2)}, u32[]{:S(2)}) collective-permute-start(f32[4,8,1024]{2,1,0:T(8,128)} %get-tuple-element.16), channel_id=1, source_target_pairs={{0,1},{1,0},{2,3},{3,2},{4,5},{5,4},{6,7},{7,6},{8,9},{9,8},{10,11... | collective-permute-start | bytes 393224 | tf_op jit(solution)/shard_map/ppermute | solution.py:458
  8.0 11.4 %collective-permute-start.1 = (f32[7,4,1024]{2,1,0:T(4,128)}, f32[7,4,1024]{2,1,0:T(4,128)S(1)}, u32[]{:S(2)}, u32[]{:S(2)}) collective-permute-start(f32[7,4,1024]{2,1,0:T(4,128)} %get-tuple-element.17), channel_id=1, source_target_pairs={{0,2},{2,4},{4,6},{6,8},{8,10},{10,12},{12,14},{14,16},{16,18},{18... | collective-permute-start | bytes 344072 | tf_op jit(solution)/shard_map/ppermute | solution.py:459
  9.9 25.1 %copy-start.1 = (f32[144,1024]{1,0:T(8,128)S(1)}, f32[144,1024]{1,0:T(8,128)}, u32[]{:S(2)}) copy-start(f32[144,1024]{1,0:T(8,128)} %drive_ref.3) | copy-start | bytes 1769476
  9.9 25.1 %copy-start.2 = (f32[144,1024]{1,0:T(8,128)S(1)}, f32[144,1024]{1,0:T(8,128)}, u32[]{:S(2)}) copy-start(f32[144,1024]{1,0:T(8,128)} %state_ref.1) | copy-start | bytes 1769476
  9.9 25.1 %copy-start.5 = (f32[144,144]{1,0:T(8,128)S(1)}, f32[144,144]{1,0:T(8,128)}, u32[]{:S(2)}) copy-start(f32[144,144]{1,0:T(8,128)} %link_ref.1) | copy-start | bytes 248836
  9.9 25.1 %copy-start.7 = (s32[32,256]{1,0:T(8,128)S(1)}, s32[32,256]{1,0:T(8,128)}, u32[]{:S(2)}) copy-start(s32[32,256]{1,0:T(8,128)} %sender_ref.3) | copy-start | bytes 98308
  9.9 25.1 %copy-start.8 = (f32[32,256]{1,0:T(8,128)S(1)}, f32[32,256]{1,0:T(8,128)}, u32[]{:S(2)}) copy-start(f32[32,256]{1,0:T(8,128)} %share_ref.3) | copy-start | bytes 98308
  10.0 25.0 %copy-start.9 = (s32[1024]{0:T(1024)S(1)}, s32[1024]{0:T(1024)}, u32[]{:S(2)}) copy-start(s32[1024]{0:T(1024)} %param.14) | copy-start | bytes 12292
  10.0 25.0 %copy-start.10 = (s32[1024]{0:T(1024)S(1)}, s32[1024]{0:T(1024)}, u32[]{:S(2)}) copy-start(s32[1024]{0:T(1024)} %param.13) | copy-start | bytes 12292
  10.0 25.0 %copy-start.11 = (f32[1024]{0:T(1024)S(1)}, f32[1024]{0:T(1024)}, u32[]{:S(2)}) copy-start(f32[1024]{0:T(1024)} %param.17) | copy-start | bytes 12292
  10.0 12.3 %collective-permute-start.2 = (f32[7,4,1024]{2,1,0:T(4,128)}, f32[7,4,1024]{2,1,0:T(4,128)S(1)}, u32[]{:S(2)}, u32[]{:S(2)}) collective-permute-start(f32[7,4,1024]{2,1,0:T(4,128)} %get-tuple-element.18), channel_id=1, source_target_pairs={{2,0},{4,2},{6,4},{8,6},{10,8},{12,10},{14,12},{16,14},{18,16},{20... | collective-permute-start | bytes 344072 | tf_op jit(solution)/shard_map/ppermute | solution.py:460
  22.4 40.7 %collective-permute-start.4 = (f32[39,4,1024]{2,1,0:T(4,128)S(1)}, f32[39,4,1024]{2,1,0:T(4,128)S(1)}, u32[]{:S(2)}, u32[]{:S(2)}) collective-permute-start(f32[39,4,1024]{2,1,0:T(4,128)S(1)} %get-tuple-element.25), channel_id=1, source_target_pairs={{0,2},{2,4},{4,6},{6,8},{8,10},{10,12},{12,14},{14,16},{16,18},{18... | collective-permute-start | bytes 1916936 | tf_op jit(solution)/shard_map/ppermute | solution.py:471
  24.3 14.3 %copy-start.6 = (s32[32,256]{1,0:T(8,128)S(1)}, s32[32,256]{1,0:T(8,128)}, u32[]{:S(2)}) copy-start(s32[32,256]{1,0:T(8,128)} %tile_ref.3) | copy-start | bytes 98308
  24.3 38.8 %collective-permute-start.5 = (f32[39,4,1024]{2,1,0:T(4,128)S(1)}, f32[39,4,1024]{2,1,0:T(4,128)S(1)}, u32[]{:S(2)}, u32[]{:S(2)}) collective-permute-start(f32[39,4,1024]{2,1,0:T(4,128)S(1)} %get-tuple-element.26), channel_id=1, source_target_pairs={{2,0},{4,2},{6,4},{8,6},{10,8},{12,10},{14,12},{16,14},{18,16},{20... | collective-permute-start | bytes 1916936 | tf_op jit(solution)/shard_map/ppermute | solution.py:472
  33.6 5.0 %collective-permute-start.6 = (f32[8,1024]{1,0:T(8,128)S(1)}, f32[8,1024]{1,0:T(8,128)S(1)}, u32[]{:S(2)}, u32[]{:S(2)}) collective-permute-start(f32[8,1024]{1,0:T(8,128)S(1)} %top_level.1.top_ref), channel_id=1, source_target_pairs={{0,1},{2,3},{4,5},{6,7},{8,9},{10,11},{12,13},{14,15},{16,17},{18,... | collective-permute-start | bytes 98312 | tf_op jit(solution)/shard_map/ppermute | solution.py:484
  58.1 4.3 %collective-permute-start.7 = (f32[8,1024]{1,0:T(8,128)S(1)}, f32[8,1024]{1,0:T(8,128)S(1)}, u32[]{:S(2)}, u32[]{:S(2)}) collective-permute-start(f32[8,1024]{1,0:T(8,128)S(1)} %add_flux.1), channel_id=1, source_target_pairs={{0,1},{1,0},{2,3},{3,2},{4,5},{5,4},{6,7},{7,6},{8,9},{9,8},{10,11... | collective-permute-start | bytes 98312 | tf_op jit(solution)/shard_map/ppermute | solution.py:544

commit v3 on v2

--- a/solution.py
+++ b/solution.py
@@ -38,7 +38,7 @@
         scratch_shapes=list(scratch),
         compiler_params=pltpu.CompilerParams(vmem_limit_bytes=mib * 1024 * 1024),
         cost_estimate=pl.CostEstimate(
-            flops=0, bytes_accessed=int(microseconds * 3.0e6), transcendentals=0
+            flops=int(microseconds * 1.0e9), bytes_accessed=int(microseconds * 3.0e6), transcendentals=0
         ),
         name=name,
     )(*args)
@@ -57,6 +57,19 @@
 
 def dot_nn(a, b):
     return lax.dot_general(a, b, (((1,), (0,)), ((), ())), preferred_element_type=f32)
+
+
+def is_even():
+    return lax.rem(lax.axis_index("dom"), 2) == 0
+
+
+def edges(even, plane):
+    low, high = plane[0:4, :], plane[4:8, :]
+    return jnp.where(even, high, low), jnp.where(even, low, high)
+
+
+def halo_rows(even, mate, other):
+    return jnp.concatenate([jnp.where(even, mate, other), jnp.where(even, other, mate)], axis=0)
 
 
 def pack_first(
@@ -66,8 +79,8 @@
     inflow_ref,
     wet_ref,
     far_ref,
-    up_ref,
-    down_ref,
+    mate_ref,
+    next_ref,
     level_ref,
     place,
     surface,
@@ -94,26 +107,23 @@
         copy.wait()
     far = place[:, half : 2 * half].astype(f32)
     far_ref[rows : rows + SUBLANES, :] = jnp.broadcast_to(far, (SUBLANES, half))
-    up_ref[0] = inflow[4:8, :]
-    down_ref[0] = inflow[0:4, :]
-    up_ref[1] = wet[4:8, :].astype(f32)
-    down_ref[1] = wet[0:4, :].astype(f32)
+    even = is_even()
+    mate_ref[0], next_ref[0] = edges(even, inflow[...])
+    mate_ref[1], next_ref[1] = edges(even, wet[...].astype(f32))
     for k in range(STEPS + 1):
-        up_ref[k + 2] = surface[k, 4:8, :]
-        down_ref[k + 2] = surface[k, 0:4, :]
+        mate_ref[k + 2], next_ref[k + 2] = edges(even, surface[k])
     copies[0].wait()
     copies[5].wait()
 
 
-def pack_bulk(theta_ref, level_ref, up_ref, down_ref):
+def pack_bulk(theta_ref, level_ref, mate_ref, next_ref):
+    even = is_even()
     skip = STEPS + 1
     deep = theta_ref.shape[0] - skip
     for k in range(deep):
-        up_ref[k] = theta_ref[k + skip, 4:8, :]
-        down_ref[k] = theta_ref[k + skip, 0:4, :]
+        mate_ref[k], next_ref[k] = edges(even, theta_ref[k + skip])
     for j in range(STEPS):
-        up_ref[deep + j] = level_ref[j, 4:8, :]
-        down_ref[deep + j] = level_ref[j, 0:4, :]
+        mate_ref[deep + j], next_ref[deep + j] = edges(even, level_ref[j])
 
 
 def across(own, halo):
@@ -129,11 +139,12 @@
     return own_sum, halo_sum
 
 
-def top_level(theta_ref, before_ref, after_ref, inflow_ref, wet_ref, out_ref):
+def top_level(theta_ref, mate_ref, next_ref, inflow_ref, wet_ref, out_ref):
     count = STEPS + 1
+    even = is_even()
 
     def joined(k):
-        return jnp.concatenate([after_ref[k], before_ref[k]], axis=0)
+        return halo_rows(even, mate_ref[k], next_ref[k])
 
     wet = (wet_ref[...].astype(f32), joined(1))
     source = tuple(flux_gain * w * s for w, s in zip(wet, (inflow_ref[...], joined(0))))
@@ -161,10 +172,10 @@
 
 def ocean(
     theta_ref,
-    before_ref,
-    after_ref,
-    before_bulk_ref,
-    after_bulk_ref,
+    mate_ref,
+    next_ref,
+    mate_bulk_ref,
+    next_bulk_ref,
     level_ref,
     inflow_ref,
     wet_ref,
@@ -185,8 +196,9 @@
     upper = 1.0 - lower
 
     wet_own = wet_ref[...].astype(f32)
-    wet_halo = jnp.concatenate([after_ref[1], before_ref[1]], axis=0)
-    flow_halo = jnp.concatenate([after_ref[0], before_ref[0]], axis=0)
+    even_block = is_even()
+    wet_halo = halo_rows(even_block, mate_ref[1], next_ref[1])
+    flow_halo = halo_rows(even_block, mate_ref[0], next_ref[0])
     for at, wet, flow in ((0, wet_own, inflow_ref[...]), (8, wet_halo, flow_halo)):
         rows = slice(at, at + 8)
         keep[rows, :] = 1.0 - (4 * horizontal_rate + 2 * vertical_rate) * wet
@@ -196,8 +208,12 @@
 
     for at in range(places):
         even[at, 0:8, :] = theta_ref[at] if at < tiers else level_ref[at - tiers]
-        even[at, 8:12, :] = after_ref[at + 2] if at < skip else after_bulk_ref[at - skip]
-        even[at, 12:16, :] = before_ref[at + 2] if at < skip else before_bulk_ref[at - skip]
+        if at < skip:
+            mate, other = mate_ref[at + 2], next_ref[at + 2]
+        else:
+            mate, other = mate_bulk_ref[at - skip], next_bulk_ref[at - skip]
+        even[at, 8:12, :] = jnp.where(even_block, mate, other)
+        even[at, 12:16, :] = jnp.where(even_block, other, mate)
 
     row = lax.broadcasted_iota(i32, (SUBLANES, LANES), 0)
     lane = lax.broadcasted_iota(i32, (SUBLANES, LANES), 1)
@@ -422,7 +438,7 @@
     def shape(*dims):
         return jax.ShapeDtypeStruct(dims, f32)
 
-    packed, up, down, level = call(
+    packed, mate, follow, level = call(
         pack_first,
         [
             shape(rows + SUBLANES, half),
@@ -450,17 +466,18 @@
         mib=56,
     )
     block_axes = ("comp", "dom")
-    rising = [(i, i + 1) for i in range(n_block - 1)]
-    falling = [(j, i) for i, j in rising]
+    mates = [(i, i ^ 1) for i in range(n_block)]
+    nexts = [(i, i + 1) for i in range(1, n_block - 1, 2)]
+    nexts = nexts + [(j, i) for i, j in nexts]
     other = [(0, 1), (1, 0)]
 
     far = lax.ppermute(packed, "dom", [(i, (i + n_dom // 2) % n_dom) for i in range(n_dom)])
     level = lax.ppermute(level, "lev", other)
-    before = lax.ppermute(up, block_axes, rising)
-    after = lax.ppermute(down, block_axes, falling)
-    later_level, before, after, far = lax.optimization_barrier((level, before, after, far))
+    mate = lax.ppermute(mate, block_axes, mates)
+    follow = lax.ppermute(follow, block_axes, nexts)
+    later_level = level
     bulk = tiers - 1
-    up_bulk, down_bulk = call(
+    mate_bulk, follow_bulk = call(
         pack_bulk,
         [shape(bulk, 4, span), shape(bulk, 4, span)],
         [whole()] * 2,
@@ -468,20 +485,8 @@
         "pack_bulk",
         1.0,
     )
-    before_bulk = lax.ppermute(up_bulk, block_axes, rising)
-    after_bulk = lax.ppermute(down_bulk, block_axes, falling)
-
-    part = pl.BlockSpec((STEPS + 3, 4, span), lambda i: (0, 0, 0))
-    top = call(
-        top_level,
-        shape(lines, span),
-        [pl.BlockSpec((STEPS + 1, lines, span), lambda i: (0, 0, 0)), part, part, whole(), whole()],
-        (marine_warmth_departure, before, after, earlier_bottom_inflow, marine_tile_indicator),
-        "top_level",
-        1.0,
-        grid=(1,),
-    )
-    top_far = lax.ppermute(top, "lev", [(0, 1)])
+    mate_bulk = lax.ppermute(mate_bulk, block_axes, mates)
+    follow_bulk = lax.ppermute(follow_bulk, block_axes, nexts)
 
     air_profile_updated, pieces = call(
         columns,
@@ -502,6 +507,19 @@
         4.0,
         grid=(1,),
     )
+    mate, follow, pieces = lax.optimization_barrier((mate, follow, pieces))
+    part = pl.BlockSpec((STEPS + 3, 4, span), lambda i: (0, 0, 0))
+    top = call(
+        top_level,
+        shape(lines, span),
+        [pl.BlockSpec((STEPS + 1, lines, span), lambda i: (0, 0, 0)), part, part, whole(), whole()],
+        (marine_warmth_departure, mate, follow, earlier_bottom_inflow, marine_tile_indicator),
+        "top_level",
+        1.0,
+        grid=(1,),
+    )
+    top_far = lax.ppermute(top, "lev", [(0, 1)])
+
     payload = call(
         targets,
         shape(4 * entry_rows, LANES),
@@ -514,25 +532,6 @@
         payload.reshape(entry_rows, 4, LANES), "dom", split_axis=0, concat_axis=0, tiled=True
     ).reshape(4 * entry_rows, LANES)
 
-    theta = call(
-        ocean,
-        shape(tiers, lines, span),
-        [whole()] * 8,
-        (
-            marine_warmth_departure,
-            before,
-            after,
-            before_bulk,
-            after_bulk,
-            level,
-            earlier_bottom_inflow,
-            marine_tile_indicator,
-        ),
-        "ocean",
-        6.0,
-        scratch=[pltpu.VMEM((tiers + STEPS, 16, span), f32)] * 2 + [pltpu.VMEM((16, span), f32)] * 4,
-    )
-
     partial_flux = call(
         add_flux,
         shape(lines, span),
@@ -541,7 +540,29 @@
         "add_flux",
         2.0,
     )
-    marine_warming_rate = partial_flux + lax.ppermute(partial_flux, "lev", other)
+    late_level, partial_flux = lax.optimization_barrier((level, partial_flux))
+    theta = call(
+        ocean,
+        shape(tiers, lines, span),
+        [whole()] * 8,
+        (
+            marine_warmth_departure,
+            mate,
+            follow,
+            mate_bulk,
+            follow_bulk,
+            late_level,
+            earlier_bottom_inflow,
+            marine_tile_indicator,
+        ),
+        "ocean",
+        6.0,
+        scratch=[pltpu.VMEM((tiers + STEPS, 16, span), f32)] * 2 + [pltpu.VMEM((16, span), f32)] * 4,
+    )
+
+    other_flux = lax.ppermute(partial_flux, "lev", other)
+    theta, other_flux = lax.optimization_barrier((theta, other_flux))
+    marine_warming_rate = partial_flux + other_flux
     air_bottom_warmth = call(
         add_warmth,
         shape(count // LANES, LANES),

time: 70.9 us -> 60.8 us (0.86)
  starting transfers between devices: 30.5 us -> 20.6 us
  blocking collectives: 17.2 us -> 19.7 us
  waiting for transfers between devices: 4.03 us -> 1.6 us
    ppermute x5, starting transfers between devices: 24 us -> 13.4 us  [the longest x1 6.33 us: on_device(): follow_bulk = lax.ppermute(follow_bulk, block_axes, nexts)]
    ppermute x5, waiting for transfers between devices: 4.02 us -> 0.01 us  [the longest x1 0.01 us: on_device(): mate = lax.ppermute(mate, block_axes, mates)]
    all_to_all x1, blocking collectives: 17.2 us -> 19.7 us  [on_device(): lax.all_to_all(payload.reshape(entry_rows, 4, LANES), 'dom', split_axis=0...]
    ppermute x1, waiting for transfers between devices: 0.01 us -> 1.58 us  [on_device(): top_far = lax.ppermute(top, 'lev', [(0, 1)])]
  transfers between devices with their start and end apart: 8 -> 8, of which waited for: 3 -> 1; matrix products, arithmetic and copies ran while one was open for 1% -> 0% of each run, Pallas kernels for 11% -> 25%
where the time goes in v3:
time: 60.8 us; the launch traced here: 60.6 us
  starting transfers between devices  20.6 us (34%)
  blocking collectives  19.7 us (32%)
  Pallas kernels  17.2 us (28%)
  waiting for transfers between devices  1.6 us (3%)
  between operations  0.88 us (1%)
  other arithmetic  0.62 us (1%)
    all_to_all x1, blocking collectives, on_device(): lax.all_to_all(payload.reshape(entry_rows, 4, LANES), 'dom', split_axis=0...  19.7 us
    pallas_call x8, Pallas kernels, call(): pl.pallas_call(body, out_shape=shapes, grid=grid, in_specs=specs, out_spe...  17.2 us
    ppermute x1, starting transfers between devices, on_device(): follow_bulk = lax.ppermute(follow_bulk, block_axes, nexts)  6.33 us
    ppermute x1, starting transfers between devices, on_device(): follow = lax.ppermute(follow, block_axes, nexts)  4.48 us
    ppermute x1, starting transfers between devices, on_device(): lax.ppermute(packed, 'dom', [(i, (i + n_dom // 2) % n_dom) for i in range...  3.28 us
    ppermute x1, starting transfers between devices, on_device(): other_flux = lax.ppermute(partial_flux, 'lev', other)  2.45 us
    ppermute x1, starting transfers between devices, on_device(): top_far = lax.ppermute(top, 'lev', [(0, 1)])  2.01 us
    ppermute x1, starting transfers between devices, on_device(): level = lax.ppermute(level, 'lev', other)  1.92 us
  transfers between devices with their start and end apart: 8, of which 1 were waited for; matrix products, arithmetic and copies ran while one was open for 0% of the time, Pallas kernels for 25%

profile of v3, /device:TPU:64, one launch (start us, length us, event | category | flops | bytes accessed | tf_op | source)
XLA Modules:
  0.0 60.6 jit_solution(10084174893578322533)
XLA Ops:
  0.6 0.0 copy-start
  0.6 2.1 %pack_first.1 = (f32[152,512]{1,0:T(8,128)}, f32[7,4,1024]{2,1,0:T(4,128)}, f32[7,4,1024]{2,1,0:T(4,128)}, f32[4,8,1024]{2,1,0:T(8,128)}) custom-call(f32[144,1024]{1,0:T(8,128)} %drive_ref.3, s32[1,1024]{1,0:T(1,128)} %bitcast.10, f32[40,8,1024]{2,1,0:T(8,128)} %theta_ref.7, f32[8,1024]{1,0:T(8,128)} %inflow_ref.5, s32[8,1024]{1,0:T(8,128)} %wet_ref.5), custom_call_target="tpu_custom_call" | custom-call | flops 1500000000 | bytes 4500000 | tf_op jit(solution)/shard_map/pack_first/pallas_call | solution.py:32
  2.8 3.3 %collective-permute-start = (f32[152,512]{1,0:T(8,128)}, f32[152,512]{1,0:T(8,128)S(1)}, u32[]{:S(2)}, u32[]{:S(2)}) collective-permute-start(f32[152,512]{1,0:T(8,128)} %get-tuple-element.19), channel_id=1, source_target_pairs={{0,32},{2,34},{4,36},{6,38},{8,40},{10,42},{12,44},{14,46},{16,48}... | collective-permute-start | bytes 933896 | tf_op jit(solution)/shard_map/ppermute | solution.py:474
  6.0 1.9 %collective-permute-start.3 = (f32[4,8,1024]{2,1,0:T(8,128)}, f32[4,8,1024]{2,1,0:T(8,128)S(1)}, u32[]{:S(2)}, u32[]{:S(2)}) collective-permute-start(f32[4,8,1024]{2,1,0:T(8,128)} %get-tuple-element.26), channel_id=1, source_target_pairs={{0,1},{1,0},{2,3},{3,2},{4,5},{5,4},{6,7},{7,6},{8,9},{9,8},{10,11... | collective-permute-start | bytes 393224 | tf_op jit(solution)/shard_map/ppermute | solution.py:475
  8.0 0.0 collective-permute-start.1
  8.0 0.0 copy-start.1
  8.0 0.0 copy-start.5
  8.0 0.0 copy-start.6
  8.0 0.0 copy-start.9
  8.0 0.0 copy-start.10
  8.0 0.0 copy-start.11
  8.0 4.5 %collective-permute-start.2 = (f32[7,4,1024]{2,1,0:T(4,128)}, f32[7,4,1024]{2,1,0:T(4,128)S(1)}, u32[]{:S(2)}, u32[]{:S(2)}) collective-permute-start(f32[7,4,1024]{2,1,0:T(4,128)} %get-tuple-element.22), channel_id=1, source_target_pairs={{2,4},{6,8},{10,12},{14,16},{18,20},{22,24},{26,28},{30,32},{34,36... | collective-permute-start | bytes 344072 | tf_op jit(solution)/shard_map/ppermute | solution.py:477
  12.5 0.0 collective-permute-done.3.level_ref
  12.5 0.0 copy-done
  12.5 0.1 pack_bulk.1
  12.7 0.1 collective-permute-start.4
  12.8 6.3 %collective-permute-start.5 = (f32[39,4,1024]{2,1,0:T(4,128)S(1)}, f32[39,4,1024]{2,1,0:T(4,128)S(1)}, u32[]{:S(2)}, u32[]{:S(2)}) collective-permute-start(f32[39,4,1024]{2,1,0:T(4,128)S(1)} %get-tuple-element.28), channel_id=1, source_target_pairs={{2,4},{6,8},{10,12},{14,16},{18,20},{22,24},{26,28},{30,32},{34,36... | collective-permute-start | bytes 1916936 | tf_op jit(solution)/shard_map/ppermute | solution.py:489
  19.1 0.0 collective-permute-done.far_ref
  19.1 0.0 copy-done.1
  19.2 0.0 copy-done.2
  19.2 0.0 copy-done.3
  19.2 0.0 copy-done.5
  19.2 0.0 copy-done.6
  19.2 0.0 copy-done.9
  19.2 0.0 copy-done.10
  19.2 0.0 copy-done.11
  19.2 0.0 copy-start.7
  19.2 0.0 copy-start.8
  19.2 3.6 %columns.1 = (f32[144,1024]{1,0:T(8,128)}, f32[32,256]{1,0:T(8,128)S(1)}) custom-call(f32[144,1024]{1,0:T(8,128)S(1)} %copy-done.1, s32[1,1024]{1,0:T(1,128)S(1)} %bitcast.9, s32[1,1024]{1,0:T(1,128)S(1)} %bitcast.11, f32[144,1024]{1,0:T(8,128)S(1)} %copy-done.2, f32[152,512]{1,0:T(8,128)S(1)} %collective-permute-done.far_ref, f32[144,144]{1,0:T(8,128)S(1)} %copy-done.3, ...), custom_call_target="tpu_custom_call" | custom-call | flops 4000000000 | bytes 12000000 | tf_op jit(solution)/shard_map/columns/pallas_call | solution.py:32
  22.8 0.0 collective-permute-done.1.mate_ref
  22.8 0.0 collective-permute-done.2.next_ref
  22.8 0.0 copy-done.7
  22.8 0.0 copy-done.8
  22.9 0.0 copy-start.4
  22.9 0.4 top_level.1.top_ref
  23.3 2.0 %collective-permute-start.6 = (f32[8,1024]{1,0:T(8,128)S(1)}, f32[8,1024]{1,0:T(8,128)S(1)}, u32[]{:S(2)}, u32[]{:S(2)}) collective-permute-start(f32[8,1024]{1,0:T(8,128)S(1)} %top_level.1.top_ref), channel_id=1, source_target_pairs={{0,1},{2,3},{4,5},{6,7},{8,9},{10,11},{12,13},{14,15},{16,17},{18,... | collective-permute-start | bytes 98312 | tf_op jit(solution)/shard_map/ppermute | solution.py:521
  25.3 1.6 %collective-permute-done.6.top_far_ref = f32[8,1024]{1,0:T(8,128)S(1)} collective-permute-done((f32[8,1024]{1,0:T(8,128)S(1)}, f32[8,1024]{1,0:T(8,128)S(1)}, u32[]{:S(2)}, u32[]{:S(2)}) %collective-permute-start.6) | collective-permute-done | bytes 32800 | tf_op jit(solution)/shard_map/ppermute | solution.py:521
  26.9 0.0 copy-done.4
  26.9 1.5 %targets.1 = f32[128,128]{1,0:T(8,128)S(1)} custom-call(s32[32,256]{1,0:T(8,128)S(1)} %copy-done.4, f32[8,1024]{1,0:T(8,128)S(1)} %top_level.1.top_ref, f32[8,1024]{1,0:T(8,128)S(1)} %collective-permute-done.6.top_far_ref, f32[32,256]{1,0:T(8,128)S(1)} %get-tuple-element.29.pieces_ref), custom_call_target="tpu_custom_call" | custom-call | flops 1000000000 | bytes 3000000 | tf_op jit(solution)/shard_map/targets/pallas_call | solution.py:32
  28.4 19.7 %all_to_all.5 = f32[32,4,128]{2,1,0:T(4,128)S(1)} all-to-all(f32[32,4,128]{2,1,0:T(4,128)S(1)} %bitcast.8), channel_id=1, replica_groups=mesh['comp'=4,'dom'=32,'lev'=2] {'dom'}, dimensions={0} | all-to-all | bytes 131072 | tf_op jit(solution)/shard_map/all_to_all | solution.py:531
  48.1 0.8 %add_flux.1 = f32[8,1024]{1,0:T(8,128)S(1)} custom-call(f32[128,128]{1,0:T(8,128)S(1)} %bitcast.6, s32[32,256]{1,0:T(8,128)S(1)} %copy-done.4), custom_call_target="tpu_custom_call" | custom-call | flops 2000000000 | bytes 6000000 | tf_op jit(solution)/shard_map/add_flux/pallas_call | solution.py:32
  48.9 2.5 %collective-permute-start.7 = (f32[8,1024]{1,0:T(8,128)S(1)}, f32[8,1024]{1,0:T(8,128)S(1)}, u32[]{:S(2)}, u32[]{:S(2)}) collective-permute-start(f32[8,1024]{1,0:T(8,128)S(1)} %add_flux.1), channel_id=1, source_target_pairs={{0,1},{1,0},{2,3},{3,2},{4,5},{5,4},{6,7},{7,6},{8,9},{9,8},{10,11... | collective-permute-start | bytes 98312 | tf_op jit(solution)/shard_map/ppermute | solution.py:563
  51.3 1.3 %add_warmth.1 = f32[8,128]{1,0:T(8,128)} custom-call(f32[128,128]{1,0:T(8,128)S(1)} %bitcast.7, s32[32,256]{1,0:T(8,128)S(1)} %copy-done.5, f32[32,256]{1,0:T(8,128)S(1)} %copy-done.6), custom_call_target="tpu_custom_call" | custom-call | flops 2000000000 | bytes 6000000 | tf_op jit(solution)/shard_map/add_warmth/pallas_call | solution.py:32
  52.6 0.0 collective-permute-done.4.mate_bulk_ref
  52.6 0.0 collective-permute-done.5.next_bulk_ref
  52.6 7.4 %ocean.1 = f32[40,8,1024]{2,1,0:T(8,128)} custom-call(f32[40,8,1024]{2,1,0:T(8,128)S(1)} %copy-done, f32[7,4,1024]{2,1,0:T(4,128)S(1)} %collective-permute-done.1.mate_ref, f32[7,4,1024]{2,1,0:T(4,128)S(1)} %collective-permute-done.2.next_ref, f32[39,4,1024]{2,1,0:T(4,128)S(1)} %collective-permute-done.4.mate_bulk_ref, ...), custom_call_target="tpu_custom_call" | custom-call | flops 6000000000 | bytes 18000000 | tf_op jit(solution)/shard_map/ocean/pallas_call | solution.py:32
  60.0 0.0 collective-permute-done.7
  60.0 0.6 %add.3 = f32[8,1024]{1,0:T(8,128)} add(f32[8,1024]{1,0:T(8,128)S(1)} %add_flux.1, f32[8,1024]{1,0:T(8,128)S(1)} %collective-permute-done.7) | non-fusion elementwise | flops 8192 | bytes 98304 | tf_op jit(solution)/shard_map/add | solution.py:565
  (2 shorter events, 0.0 us)
Async XLA Ops:
  0.6 11.9 %copy-start = (f32[40,8,1024]{2,1,0:T(8,128)S(1)}, f32[40,8,1024]{2,1,0:T(8,128)}, u32[]{:S(2)}) copy-start(f32[40,8,1024]{2,1,0:T(8,128)} %theta_ref.7) | copy-start | bytes 3932164
  2.8 16.4 %collective-permute-start = (f32[152,512]{1,0:T(8,128)}, f32[152,512]{1,0:T(8,128)S(1)}, u32[]{:S(2)}, u32[]{:S(2)}) collective-permute-start(f32[152,512]{1,0:T(8,128)} %get-tuple-element.19), channel_id=1, source_target_pairs={{0,32},{2,34},{4,36},{6,38},{8,40},{10,42},{12,44},{14,46},{16,48}... | collective-permute-start | bytes 933896 | tf_op jit(solution)/shard_map/ppermute | solution.py:474
  6.0 6.5 %collective-permute-start.3 = (f32[4,8,1024]{2,1,0:T(8,128)}, f32[4,8,1024]{2,1,0:T(8,128)S(1)}, u32[]{:S(2)}, u32[]{:S(2)}) collective-permute-start(f32[4,8,1024]{2,1,0:T(8,128)} %get-tuple-element.26), channel_id=1, source_target_pairs={{0,1},{1,0},{2,3},{3,2},{4,5},{5,4},{6,7},{7,6},{8,9},{9,8},{10,11... | collective-permute-start | bytes 393224 | tf_op jit(solution)/shard_map/ppermute | solution.py:475
  8.0 14.9 %collective-permute-start.1 = (f32[7,4,1024]{2,1,0:T(4,128)}, f32[7,4,1024]{2,1,0:T(4,128)S(1)}, u32[]{:S(2)}, u32[]{:S(2)}) collective-permute-start(f32[7,4,1024]{2,1,0:T(4,128)} %get-tuple-element.21), channel_id=1, source_target_pairs={{0,2},{2,0},{4,6},{6,4},{8,10},{10,8},{12,14},{14,12},{16,18},{18,... | collective-permute-start | bytes 344072 | tf_op jit(solution)/shard_map/ppermute | solution.py:476
  8.0 11.2 %copy-start.1 = (f32[144,1024]{1,0:T(8,128)S(1)}, f32[144,1024]{1,0:T(8,128)}, u32[]{:S(2)}) copy-start(f32[144,1024]{1,0:T(8,128)} %state_ref.1) | copy-start | bytes 1769476
  8.0 11.2 %copy-start.2 = (f32[144,1024]{1,0:T(8,128)S(1)}, f32[144,1024]{1,0:T(8,128)}, u32[]{:S(2)}) copy-start(f32[144,1024]{1,0:T(8,128)} %drive_ref.3) | copy-start | bytes 1769476
  8.0 11.2 %copy-start.3 = (f32[144,144]{1,0:T(8,128)S(1)}, f32[144,144]{1,0:T(8,128)}, u32[]{:S(2)}) copy-start(f32[144,144]{1,0:T(8,128)} %link_ref.1) | copy-start | bytes 248836
  8.0 11.2 %copy-start.5 = (s32[32,256]{1,0:T(8,128)S(1)}, s32[32,256]{1,0:T(8,128)}, u32[]{:S(2)}) copy-start(s32[32,256]{1,0:T(8,128)} %sender_ref.3) | copy-start | bytes 98308
  8.0 11.2 %copy-start.6 = (f32[32,256]{1,0:T(8,128)S(1)}, f32[32,256]{1,0:T(8,128)}, u32[]{:S(2)}) copy-start(f32[32,256]{1,0:T(8,128)} %share_ref.3) | copy-start | bytes 98308
  8.0 11.2 %copy-start.9 = (s32[1024]{0:T(1024)S(1)}, s32[1024]{0:T(1024)}, u32[]{:S(2)}) copy-start(s32[1024]{0:T(1024)} %param.13) | copy-start | bytes 12292
  8.0 11.2 %copy-start.10 = (s32[1024]{0:T(1024)S(1)}, s32[1024]{0:T(1024)}, u32[]{:S(2)}) copy-start(s32[1024]{0:T(1024)} %param.14) | copy-start | bytes 12292
  8.0 11.2 %copy-start.11 = (f32[1024]{0:T(1024)S(1)}, f32[1024]{0:T(1024)}, u32[]{:S(2)}) copy-start(f32[1024]{0:T(1024)} %param.17) | copy-start | bytes 12292
  8.0 14.8 %collective-permute-start.2 = (f32[7,4,1024]{2,1,0:T(4,128)}, f32[7,4,1024]{2,1,0:T(4,128)S(1)}, u32[]{:S(2)}, u32[]{:S(2)}) collective-permute-start(f32[7,4,1024]{2,1,0:T(4,128)} %get-tuple-element.22), channel_id=1, source_target_pairs={{2,4},{6,8},{10,12},{14,16},{18,20},{22,24},{26,28},{30,32},{34,36... | collective-permute-start | bytes 344072 | tf_op jit(solution)/shard_map/ppermute | solution.py:477
  12.7 39.9 %collective-permute-start.4 = (f32[39,4,1024]{2,1,0:T(4,128)S(1)}, f32[39,4,1024]{2,1,0:T(4,128)S(1)}, u32[]{:S(2)}, u32[]{:S(2)}) collective-permute-start(f32[39,4,1024]{2,1,0:T(4,128)S(1)} %get-tuple-element.27), channel_id=1, source_target_pairs={{0,2},{2,0},{4,6},{6,4},{8,10},{10,8},{12,14},{14,12},{16,18},{18,... | collective-permute-start | bytes 1916936 | tf_op jit(solution)/shard_map/ppermute | solution.py:488
  12.8 39.8 %collective-permute-start.5 = (f32[39,4,1024]{2,1,0:T(4,128)S(1)}, f32[39,4,1024]{2,1,0:T(4,128)S(1)}, u32[]{:S(2)}, u32[]{:S(2)}) collective-permute-start(f32[39,4,1024]{2,1,0:T(4,128)S(1)} %get-tuple-element.28), channel_id=1, source_target_pairs={{2,4},{6,8},{10,12},{14,16},{18,20},{22,24},{26,28},{30,32},{34,36... | collective-permute-start | bytes 1916936 | tf_op jit(solution)/shard_map/ppermute | solution.py:489
  19.2 3.6 %copy-start.7 = (f32[8,1024]{1,0:T(8,128)S(1)}, f32[8,1024]{1,0:T(8,128)}, u32[]{:S(2)}) copy-start(f32[8,1024]{1,0:T(8,128)} %inflow_ref.5) | copy-start | bytes 98308
  19.2 3.6 %copy-start.8 = (s32[8,1024]{1,0:T(8,128)S(1)}, s32[8,1024]{1,0:T(8,128)}, u32[]{:S(2)}) copy-start(s32[8,1024]{1,0:T(8,128)} %wet_ref.5) | copy-start | bytes 98308
  22.9 4.1 %copy-start.4 = (s32[32,256]{1,0:T(8,128)S(1)}, s32[32,256]{1,0:T(8,128)}, u32[]{:S(2)}) copy-start(s32[32,256]{1,0:T(8,128)} %tile_ref.3) | copy-start | bytes 98308
  23.3 3.6 %collective-permute-start.6 = (f32[8,1024]{1,0:T(8,128)S(1)}, f32[8,1024]{1,0:T(8,128)S(1)}, u32[]{:S(2)}, u32[]{:S(2)}) collective-permute-start(f32[8,1024]{1,0:T(8,128)S(1)} %top_level.1.top_ref), channel_id=1, source_target_pairs={{0,1},{2,3},{4,5},{6,7},{8,9},{10,11},{12,13},{14,15},{16,17},{18,... | collective-permute-start | bytes 98312 | tf_op jit(solution)/shard_map/ppermute | solution.py:521
  48.9 11.1 %collective-permute-start.7 = (f32[8,1024]{1,0:T(8,128)S(1)}, f32[8,1024]{1,0:T(8,128)S(1)}, u32[]{:S(2)}, u32[]{:S(2)}) collective-permute-start(f32[8,1024]{1,0:T(8,128)S(1)} %add_flux.1), channel_id=1, source_target_pairs={{0,1},{1,0},{2,3},{3,2},{4,5},{5,4},{6,7},{7,6},{8,9},{9,8},{10,11... | collective-permute-start | bytes 98312 | tf_op jit(solution)/shard_map/ppermute | solution.py:563

commit v4 on v3

--- a/solution.py
+++ b/solution.py
@@ -26,7 +26,7 @@
     return pl.BlockSpec(memory_space=pltpu.VMEM)
 
 
-def call(body, out_shapes, specs, args, name, microseconds, scratch=(), mib=32, grid=()):
+def call(body, out_shapes, specs, args, name, microseconds, scratch=(), mib=32, grid=(), out_specs=None):
     one = not isinstance(out_shapes, (list, tuple))
     shapes = [out_shapes] if one else list(out_shapes)
     out = pl.pallas_call(
@@ -34,7 +34,7 @@
         out_shape=shapes,
         grid=grid,
         in_specs=specs,
-        out_specs=[whole() for _ in shapes],
+        out_specs=out_specs or [whole() for _ in shapes],
         scratch_shapes=list(scratch),
         compiler_params=pltpu.CompilerParams(vmem_limit_bytes=mib * 1024 * 1024),
         cost_estimate=pl.CostEstimate(
@@ -86,6 +86,7 @@
     surface,
     inflow,
     wet,
+    far_rows,
     sems,
 ):
     rows = drive_ref.shape[0]
@@ -106,7 +107,9 @@
     for copy in copies[1:5]:
         copy.wait()
     far = place[:, half : 2 * half].astype(f32)
-    far_ref[rows : rows + SUBLANES, :] = jnp.broadcast_to(far, (SUBLANES, half))
+    far_rows[...] = jnp.broadcast_to(far, (SUBLANES, half))
+    last = pltpu.make_async_copy(far_rows, far_ref.at[rows : rows + SUBLANES, :], sems.at[len(pairs)])
+    last.start()
     even = is_even()
     mate_ref[0], next_ref[0] = edges(even, inflow[...])
     mate_ref[1], next_ref[1] = edges(even, wet[...].astype(f32))
@@ -114,6 +117,7 @@
         mate_ref[k + 2], next_ref[k + 2] = edges(even, surface[k])
     copies[0].wait()
     copies[5].wait()
+    last.wait()
 
 
 def pack_bulk(theta_ref, level_ref, mate_ref, next_ref):
@@ -399,7 +403,8 @@
         out_ref[:, c * LANES : (c + 1) * LANES] = total[c * lines : (c + 1) * lines]
 
 
-def add_warmth(received_ref, sender_ref, share_ref, out_ref):
+def add_warmth(received_ref, sender_ref, share_ref, flux_ref, other_flux_ref, out_ref, rate_ref):
+    rate_ref[...] = flux_ref[...] + other_flux_ref[...]
     entry_rows, slots = sender_ref.shape
     groups = out_ref.shape[0]
     total = jnp.zeros((2 * groups, LANES), f32)
@@ -461,9 +466,16 @@
             pltpu.VMEM((STEPS + 1, lines, span), f32),
             pltpu.VMEM((lines, span), f32),
             pltpu.VMEM((lines, span), i32),
-            pltpu.SemaphoreType.DMA((6,)),
+            pltpu.VMEM((SUBLANES, half), f32),
+            pltpu.SemaphoreType.DMA((7,)),
         ],
         mib=56,
+        out_specs=[
+            pl.BlockSpec(memory_space=pl.ANY),
+            whole(),
+            whole(),
+            pl.BlockSpec(memory_space=pl.ANY),
+        ],
     )
     block_axes = ("comp", "dom")
     mates = [(i, i ^ 1) for i in range(n_block)]
@@ -475,19 +487,6 @@
     level = lax.ppermute(level, "lev", other)
     mate = lax.ppermute(mate, block_axes, mates)
     follow = lax.ppermute(follow, block_axes, nexts)
-    later_level = level
-    bulk = tiers - 1
-    mate_bulk, follow_bulk = call(
-        pack_bulk,
-        [shape(bulk, 4, span), shape(bulk, 4, span)],
-        [whole()] * 2,
-        (marine_warmth_departure, later_level),
-        "pack_bulk",
-        1.0,
-    )
-    mate_bulk = lax.ppermute(mate_bulk, block_axes, mates)
-    follow_bulk = lax.ppermute(follow_bulk, block_axes, nexts)
-
     air_profile_updated, pieces = call(
         columns,
         [shape(rows, count), shape(entry_rows, slots)],
@@ -520,6 +519,19 @@
     )
     top_far = lax.ppermute(top, "lev", [(0, 1)])
 
+    later_level, top = lax.optimization_barrier((level, top))
+    bulk = tiers - 1
+    mate_bulk, follow_bulk = call(
+        pack_bulk,
+        [shape(bulk, 4, span), shape(bulk, 4, span)],
+        [whole()] * 2,
+        (marine_warmth_departure, later_level),
+        "pack_bulk",
+        1.0,
+    )
+    mate_bulk = lax.ppermute(mate_bulk, block_axes, mates)
+    follow_bulk = lax.ppermute(follow_bulk, block_axes, nexts)
+
     payload = call(
         targets,
         shape(4 * entry_rows, LANES),
@@ -538,7 +550,7 @@
         [whole()] * 2,
         (received, intersect_receiver_tile),
         "add_flux",
-        2.0,
+        20.0,
     )
     late_level, partial_flux = lax.optimization_barrier((level, partial_flux))
     theta = call(
@@ -562,15 +574,15 @@
 
     other_flux = lax.ppermute(partial_flux, "lev", other)
     theta, other_flux = lax.optimization_barrier((theta, other_flux))
-    marine_warming_rate = partial_flux + other_flux
-    air_bottom_warmth = call(
+    air_bottom_warmth, marine_warming_rate = call(
         add_warmth,
-        shape(count // LANES, LANES),
-        [whole()] * 3,
-        (received, intersect_sender_index, intersect_share),
+        [shape(count // LANES, LANES), shape(lines, span)],
+        [whole()] * 5,
+        (received, intersect_sender_index, intersect_share, partial_flux, other_flux),
         "add_warmth",
         2.0,
-    ).reshape(count)
+    )
+    air_bottom_warmth = air_bottom_warmth.reshape(count)
     return (air_profile_updated, theta, marine_warming_rate, air_bottom_warmth)
 
 

time: 60.8 us -> 82 us (1.35)
  the two profiles are of different devices: /device:TPU:64 before, /device:TPU:127 now
where the time goes in v4:
time: 82 us; the launch traced here: 81.7 us
  Pallas kernels  31.3 us (38%)
  starting transfers between devices  25.2 us (31%)
  waiting for transfers between devices  23.3 us (28%)
  local copies, waits for them, and re-layouts  1.01 us (1%)
  between operations  0.91 us (1%)
    pallas_call x8, Pallas kernels, call(): pl.pallas_call(body, out_shape=shapes, grid=grid, in_specs=specs, out_spe...  31.3 us
    ppermute x1, waiting for transfers between devices, on_device(): follow_bulk = lax.ppermute(follow_bulk, block_axes, nexts)  18.5 us
    all_to_all x1, starting transfers between devices, on_device(): lax.all_to_all(payload.reshape(entry_rows, 4, LANES), 'dom', split_axis=0...  8.9 us
    ppermute x1, starting transfers between devices, on_device(): follow = lax.ppermute(follow, block_axes, nexts)  6.62 us
    ppermute x1, starting transfers between devices, on_device(): follow_bulk = lax.ppermute(follow_bulk, block_axes, nexts)  4.95 us
    ppermute x1, waiting for transfers between devices, on_device(): top_far = lax.ppermute(top, 'lev', [(0, 1)])  3.35 us
  transfers between devices with their start and end apart: 9, of which 4 were waited for; matrix products, arithmetic and copies ran while one was open for 0% of the time, Pallas kernels for 16%

profile of v4, /device:TPU:127, one launch (start us, length us, event | category | flops | bytes accessed | tf_op | source)
XLA Modules:
  0.0 81.7 jit_solution(17071189745503153611)
XLA Ops:
  0.6 0.0 copy-start.1
  0.6 0.0 copy-start.2
  0.7 0.0 copy-start.3
  0.7 0.0 copy-start.12
  0.7 0.0 copy-start.14
  0.7 0.0 copy-start.16
  0.7 0.0 copy-start.17
  0.7 0.0 copy-start.18
  0.7 14.8 %pack_first.1 = (f32[152,512]{1,0:T(8,128)}, f32[7,4,1024]{2,1,0:T(4,128)}, f32[7,4,1024]{2,1,0:T(4,128)}, f32[4,8,1024]{2,1,0:T(8,128)}) custom-call(f32[144,1024]{1,0:T(8,128)} %drive_ref.3, s32[1,1024]{1,0:T(1,128)} %bitcast.9, f32[40,8,1024]{2,1,0:T(8,128)} %theta_ref.7, f32[8,1024]{1,0:T(8,128)} %inflow_ref.5, s32[8,1024]{1,0:T(8,128)} %wet_ref.5), custom_call_target="tpu_custom_call" | custom-call | flops 1500000000 | bytes 4500000 | tf_op jit(solution)/shard_map/pack_first/pallas_call | solution.py:32
  15.5 1.0 %collective-permute-start = (f32[152,512]{1,0:T(8,128)}, f32[152,512]{1,0:T(8,128)S(1)}, u32[]{:S(2)}, u32[]{:S(2)}) collective-permute-start(f32[152,512]{1,0:T(8,128)} %get-tuple-element.23), channel_id=1, source_target_pairs={{0,32},{2,34},{4,36},{6,38},{8,40},{10,42},{12,44},{14,46},{16,48}... | collective-permute-start | bytes 933896 | tf_op jit(solution)/shard_map/ppermute | solution.py:486
  16.5 1.0 %collective-permute-start.1 = (f32[7,4,1024]{2,1,0:T(4,128)}, f32[7,4,1024]{2,1,0:T(4,128)S(1)}, u32[]{:S(2)}, u32[]{:S(2)}) collective-permute-start(f32[7,4,1024]{2,1,0:T(4,128)} %get-tuple-element.25), channel_id=1, source_target_pairs={{0,2},{2,0},{4,6},{6,4},{8,10},{10,8},{12,14},{14,12},{16,18},{18,... | collective-permute-start | bytes 344072 | tf_op jit(solution)/shard_map/ppermute | solution.py:488
  17.5 6.6 %collective-permute-start.2 = (f32[7,4,1024]{2,1,0:T(4,128)}, f32[7,4,1024]{2,1,0:T(4,128)S(1)}, u32[]{:S(2)}, u32[]{:S(2)}) collective-permute-start(f32[7,4,1024]{2,1,0:T(4,128)} %get-tuple-element.26), channel_id=1, source_target_pairs={{2,4},{6,8},{10,12},{14,16},{18,20},{22,24},{26,28},{30,32},{34,36... | collective-permute-start | bytes 344072 | tf_op jit(solution)/shard_map/ppermute | solution.py:489
  24.1 0.8 collective-permute-start.3
  24.9 0.6 collective-permute-done.far_ref
  25.5 0.0 copy-done.1
  25.5 0.0 copy-done.2
  25.5 0.0 copy-done.3
  25.6 0.0 copy-start
  25.6 0.0 copy-start.8
  25.6 0.0 copy-start.10
  25.6 3.6 %columns.1 = (f32[144,1024]{1,0:T(8,128)}, f32[32,256]{1,0:T(8,128)S(1)}) custom-call(f32[144,1024]{1,0:T(8,128)S(1)} %copy-done.1, s32[1,1024]{1,0:T(1,128)S(1)} %bitcast.8, s32[1,1024]{1,0:T(1,128)S(1)} %bitcast.10, f32[144,1024]{1,0:T(8,128)S(1)} %copy-done.2, f32[152,512]{1,0:T(8,128)S(1)} %collective-permute-done.far_ref, f32[144,144]{1,0:T(8,128)S(1)} %copy-done.3, ...), custom_call_target="tpu_custom_call" | custom-call | flops 4000000000 | bytes 12000000 | tf_op jit(solution)/shard_map/columns/pallas_call | solution.py:32
  29.2 0.0 collective-permute-done.1.mate_ref
  29.2 0.9 %collective-permute-done.2.next_ref = f32[7,4,1024]{2,1,0:T(4,128)S(1)} collective-permute-done((f32[7,4,1024]{2,1,0:T(4,128)}, f32[7,4,1024]{2,1,0:T(4,128)S(1)}, u32[]{:S(2)}, u32[]{:S(2)}) %collective-permute-start.2) | collective-permute-done | bytes 114720 | tf_op jit(solution)/shard_map/ppermute | solution.py:489
  30.1 0.0 copy-done.8
  30.1 0.0 copy-start.6
  30.1 0.4 top_level.1.top_ref
  30.6 0.2 copy-done.4
  30.8 1.3 %collective-permute-start.6 = (f32[8,1024]{1,0:T(8,128)S(1)}, f32[8,1024]{1,0:T(8,128)S(1)}, u32[]{:S(2)}, u32[]{:S(2)}) collective-permute-start(f32[8,1024]{1,0:T(8,128)S(1)} %top_level.1.top_ref), channel_id=1, source_target_pairs={{0,1},{2,3},{4,5},{6,7},{8,9},{10,11},{12,13},{14,15},{16,17},{18,... | collective-permute-start | bytes 98312 | tf_op jit(solution)/shard_map/ppermute | solution.py:520
  32.1 0.0 collective-permute-done.3.level_ref
  32.1 3.3 %collective-permute-done.6.top_far_ref = f32[8,1024]{1,0:T(8,128)S(1)} collective-permute-done((f32[8,1024]{1,0:T(8,128)S(1)}, f32[8,1024]{1,0:T(8,128)S(1)}, u32[]{:S(2)}, u32[]{:S(2)}) %collective-permute-start.6) | collective-permute-done | bytes 32800 | tf_op jit(solution)/shard_map/ppermute | solution.py:520
  35.4 2.1 %targets.1 = f32[128,128]{1,0:T(8,128)} custom-call(s32[32,256]{1,0:T(8,128)S(1)} %copy-done.6, f32[8,1024]{1,0:T(8,128)S(1)} %top_level.1.top_ref, f32[8,1024]{1,0:T(8,128)S(1)} %collective-permute-done.6.top_far_ref, f32[32,256]{1,0:T(8,128)S(1)} %get-tuple-element.35.pieces_ref), custom_call_target="tpu_custom_call" | custom-call | flops 1000000000 | bytes 3000000 | tf_op jit(solution)/shard_map/targets/pallas_call | solution.py:32
  37.5 8.9 %all-to-all-start = ((f32[32,4,128]{2,1,0:T(4,128)}), f32[32,4,128]{2,1,0:T(4,128)S(1)}, u32[]{:S(2)}, u32[]{:S(2)}) async-start(f32[32,4,128]{2,1,0:T(4,128)} %bitcast.3), calls=%async_computation | async-start | bytes 131072 | tf_op jit(solution)/shard_map/all_to_all | solution.py:543
  46.5 1.0 %pack_bulk.1 = (f32[39,4,1024]{2,1,0:T(4,128)}, f32[39,4,1024]{2,1,0:T(4,128)S(1)}) custom-call(f32[40,8,1024]{2,1,0:T(8,128)S(1)} %copy-done, f32[4,8,1024]{2,1,0:T(8,128)S(1)} %collective-permute-done.3.level_ref), custom_call_target="tpu_custom_call" | custom-call | flops 1000000000 | bytes 3000000 | tf_op jit(solution)/shard_map/pack_bulk/pallas_call | solution.py:32
  47.4 0.4 collective-permute-start.4
  47.8 4.9 %collective-permute-start.5 = (f32[39,4,1024]{2,1,0:T(4,128)S(1)}, f32[39,4,1024]{2,1,0:T(4,128)S(1)}, u32[]{:S(2)}, u32[]{:S(2)}) collective-permute-start(f32[39,4,1024]{2,1,0:T(4,128)S(1)} %get-tuple-element.33), channel_id=1, source_target_pairs={{2,4},{6,8},{10,12},{14,16},{18,20},{22,24},{26,28},{30,32},{34,36... | collective-permute-start | bytes 1916936 | tf_op jit(solution)/shard_map/ppermute | solution.py:533
  52.7 0.0 all-to-all-done
  52.8 0.0 copy-start.7
  52.8 0.7 copy-done.7
  53.5 0.8 add_flux.1.flux_ref
  54.3 0.0 copy-start.13
  54.3 0.0 copy-start.15
  54.3 0.3 collective-permute-start.7
  54.6 0.0 collective-permute-done.4.mate_bulk_ref
  54.6 18.5 %collective-permute-done.5.next_bulk_ref = f32[39,4,1024]{2,1,0:T(4,128)S(1)} collective-permute-done((f32[39,4,1024]{2,1,0:T(4,128)S(1)}, f32[39,4,1024]{2,1,0:T(4,128)S(1)}, u32[]{:S(2)}, u32[]{:S(2)}) %collective-permute-start.5) | collective-permute-done | bytes 639008 | tf_op jit(solution)/shard_map/ppermute | solution.py:533
  73.1 0.0 copy-done.11
  73.1 7.4 %ocean.1 = f32[40,8,1024]{2,1,0:T(8,128)} custom-call(f32[40,8,1024]{2,1,0:T(8,128)S(1)} %copy-done, f32[7,4,1024]{2,1,0:T(4,128)S(1)} %collective-permute-done.1.mate_ref, f32[7,4,1024]{2,1,0:T(4,128)S(1)} %copy-done.5, f32[39,4,1024]{2,1,0:T(4,128)S(1)} %collective-permute-done.4.mate_bulk_ref, f32[39,4,1024]{2,1,0:T(4,128)S(1)} %collective-permute-done.5.next_bulk_ref, ...), custom_call_target="tpu_custom_call" | custom-call | flops 6000000000 | bytes 18000000 | tf_op jit(solution)/shard_map/ocean/pallas_call | solution.py:32
  80.5 0.0 collective-permute-done.7.other_flux_ref
  80.5 1.3 %add_warmth.1 = (f32[8,128]{1,0:T(8,128)}, f32[8,1024]{1,0:T(8,128)}) custom-call(f32[128,128]{1,0:T(8,128)S(1)} %bitcast.7, s32[32,256]{1,0:T(8,128)S(1)} %copy-done.13, f32[32,256]{1,0:T(8,128)S(1)} %copy-done.15, f32[8,1024]{1,0:T(8,128)S(1)} %add_flux.1.flux_ref, f32[8,1024]{1,0:T(8,128)S(1)} %collective-permute-done.7.other_flux_ref), custom_call_target="tpu_custom_call" | custom-call | flops 2000000000 | bytes 6000000 | tf_op jit(solution)/shard_map/add_warmth/pallas_call | solution.py:32
  (16 shorter events, 0.0 us)
Async XLA Ops:
  0.6 24.9 %copy-start.1 = (f32[144,1024]{1,0:T(8,128)S(1)}, f32[144,1024]{1,0:T(8,128)}, u32[]{:S(2)}) copy-start(f32[144,1024]{1,0:T(8,128)} %state_ref.1) | copy-start | bytes 1769476
  0.6 24.9 %copy-start.2 = (f32[144,1024]{1,0:T(8,128)S(1)}, f32[144,1024]{1,0:T(8,128)}, u32[]{:S(2)}) copy-start(f32[144,1024]{1,0:T(8,128)} %drive_ref.3) | copy-start | bytes 1769476
  0.7 24.9 %copy-start.3 = (f32[144,144]{1,0:T(8,128)S(1)}, f32[144,144]{1,0:T(8,128)}, u32[]{:S(2)}) copy-start(f32[144,144]{1,0:T(8,128)} %link_ref.1) | copy-start | bytes 248836
  0.7 24.9 %copy-start.12 = (s32[32,256]{1,0:T(8,128)S(1)}, s32[32,256]{1,0:T(8,128)}, u32[]{:S(2)}) copy-start(s32[32,256]{1,0:T(8,128)} %sender_ref.3) | copy-start | bytes 98308
  0.7 24.9 %copy-start.14 = (f32[32,256]{1,0:T(8,128)S(1)}, f32[32,256]{1,0:T(8,128)}, u32[]{:S(2)}) copy-start(f32[32,256]{1,0:T(8,128)} %share_ref.3) | copy-start | bytes 98308
  0.7 24.9 %copy-start.16 = (s32[1024]{0:T(1024)S(1)}, s32[1024]{0:T(1024)}, u32[]{:S(2)}) copy-start(s32[1024]{0:T(1024)} %param.13) | copy-start | bytes 12292
  0.7 24.9 %copy-start.17 = (s32[1024]{0:T(1024)S(1)}, s32[1024]{0:T(1024)}, u32[]{:S(2)}) copy-start(s32[1024]{0:T(1024)} %param.14) | copy-start | bytes 12292
  0.7 24.9 %copy-start.18 = (f32[1024]{0:T(1024)S(1)}, f32[1024]{0:T(1024)}, u32[]{:S(2)}) copy-start(f32[1024]{0:T(1024)} %param.17) | copy-start | bytes 12292
  15.5 10.0 %collective-permute-start = (f32[152,512]{1,0:T(8,128)}, f32[152,512]{1,0:T(8,128)S(1)}, u32[]{:S(2)}, u32[]{:S(2)}) collective-permute-start(f32[152,512]{1,0:T(8,128)} %get-tuple-element.23), channel_id=1, source_target_pairs={{0,32},{2,34},{4,36},{6,38},{8,40},{10,42},{12,44},{14,46},{16,48}... | collective-permute-start | bytes 933896 | tf_op jit(solution)/shard_map/ppermute | solution.py:486
  16.5 12.7 %collective-permute-start.1 = (f32[7,4,1024]{2,1,0:T(4,128)}, f32[7,4,1024]{2,1,0:T(4,128)S(1)}, u32[]{:S(2)}, u32[]{:S(2)}) collective-permute-start(f32[7,4,1024]{2,1,0:T(4,128)} %get-tuple-element.25), channel_id=1, source_target_pairs={{0,2},{2,0},{4,6},{6,4},{8,10},{10,8},{12,14},{14,12},{16,18},{18,... | collective-permute-start | bytes 344072 | tf_op jit(solution)/shard_map/ppermute | solution.py:488
  17.5 12.6 %collective-permute-start.2 = (f32[7,4,1024]{2,1,0:T(4,128)}, f32[7,4,1024]{2,1,0:T(4,128)S(1)}, u32[]{:S(2)}, u32[]{:S(2)}) collective-permute-start(f32[7,4,1024]{2,1,0:T(4,128)} %get-tuple-element.26), channel_id=1, source_target_pairs={{2,4},{6,8},{10,12},{14,16},{18,20},{22,24},{26,28},{30,32},{34,36... | collective-permute-start | bytes 344072 | tf_op jit(solution)/shard_map/ppermute | solution.py:489
  24.1 7.9 %collective-permute-start.3 = (f32[4,8,1024]{2,1,0:T(8,128)}, f32[4,8,1024]{2,1,0:T(8,128)S(1)}, u32[]{:S(2)}, u32[]{:S(2)}) collective-permute-start(f32[4,8,1024]{2,1,0:T(8,128)} %get-tuple-element.30), channel_id=1, source_target_pairs={{0,1},{1,0},{2,3},{3,2},{4,5},{5,4},{6,7},{7,6},{8,9},{9,8},{10,11... | collective-permute-start | bytes 393224 | tf_op jit(solution)/shard_map/ppermute | solution.py:487
  25.6 4.5 %copy-start = (f32[40,8,1024]{2,1,0:T(8,128)S(1)}, f32[40,8,1024]{2,1,0:T(8,128)}, u32[]{:S(2)}) copy-start(f32[40,8,1024]{2,1,0:T(8,128)} %theta_ref.7) | copy-start | bytes 3932164
  25.6 4.5 %copy-start.8 = (f32[8,1024]{1,0:T(8,128)S(1)}, f32[8,1024]{1,0:T(8,128)}, u32[]{:S(2)}) copy-start(f32[8,1024]{1,0:T(8,128)} %inflow_ref.5) | copy-start | bytes 98308
  25.6 4.5 %copy-start.10 = (s32[8,1024]{1,0:T(8,128)S(1)}, s32[8,1024]{1,0:T(8,128)}, u32[]{:S(2)}) copy-start(s32[8,1024]{1,0:T(8,128)} %wet_ref.5) | copy-start | bytes 98308
  30.1 0.6 copy-start.4
  30.1 5.3 %copy-start.6 = (s32[32,256]{1,0:T(8,128)S(1)}, s32[32,256]{1,0:T(8,128)}, u32[]{:S(2)}) copy-start(s32[32,256]{1,0:T(8,128)} %tile_ref.3) | copy-start | bytes 98308
  30.8 4.6 %collective-permute-start.6 = (f32[8,1024]{1,0:T(8,128)S(1)}, f32[8,1024]{1,0:T(8,128)S(1)}, u32[]{:S(2)}, u32[]{:S(2)}) collective-permute-start(f32[8,1024]{1,0:T(8,128)S(1)} %top_level.1.top_ref), channel_id=1, source_target_pairs={{0,1},{2,3},{4,5},{6,7},{8,9},{10,11},{12,13},{14,15},{16,17},{18,... | collective-permute-start | bytes 98312 | tf_op jit(solution)/shard_map/ppermute | solution.py:520
  37.5 15.2 %all-to-all-start = ((f32[32,4,128]{2,1,0:T(4,128)}), f32[32,4,128]{2,1,0:T(4,128)S(1)}, u32[]{:S(2)}, u32[]{:S(2)}) async-start(f32[32,4,128]{2,1,0:T(4,128)} %bitcast.3), calls=%async_computation | async-start | bytes 131072 | tf_op jit(solution)/shard_map/all_to_all | solution.py:543
  47.4 7.2 %collective-permute-start.4 = (f32[39,4,1024]{2,1,0:T(4,128)}, f32[39,4,1024]{2,1,0:T(4,128)S(1)}, u32[]{:S(2)}, u32[]{:S(2)}) collective-permute-start(f32[39,4,1024]{2,1,0:T(4,128)} %get-tuple-element.32), channel_id=1, source_target_pairs={{0,2},{2,0},{4,6},{6,4},{8,10},{10,8},{12,14},{14,12},{16,18},{18,... | collective-permute-start | bytes 1916936 | tf_op jit(solution)/shard_map/ppermute | solution.py:532
  47.8 25.3 %collective-permute-start.5 = (f32[39,4,1024]{2,1,0:T(4,128)S(1)}, f32[39,4,1024]{2,1,0:T(4,128)S(1)}, u32[]{:S(2)}, u32[]{:S(2)}) collective-permute-start(f32[39,4,1024]{2,1,0:T(4,128)S(1)} %get-tuple-element.33), channel_id=1, source_target_pairs={{2,4},{6,8},{10,12},{14,16},{18,20},{22,24},{26,28},{30,32},{34,36... | collective-permute-start | bytes 1916936 | tf_op jit(solution)/shard_map/ppermute | solution.py:533
  52.8 0.8 copy-start.7
  53.5 19.6 %copy-start.5 = (f32[7,4,1024]{2,1,0:T(4,128)S(1)}, f32[7,4,1024]{2,1,0:T(4,128)}, u32[]{:S(2)}) copy-start(f32[7,4,1024]{2,1,0:T(4,128)} %copy-done.4) | copy-start | bytes 344068
  53.5 19.6 %copy-start.9 = (f32[8,1024]{1,0:T(8,128)S(1)}, f32[8,1024]{1,0:T(8,128)}, u32[]{:S(2)}) copy-start(f32[8,1024]{1,0:T(8,128)} %inflow_ref.5) | copy-start | bytes 98308
  53.5 19.6 %copy-start.11 = (s32[8,1024]{1,0:T(8,128)S(1)}, s32[8,1024]{1,0:T(8,128)}, u32[]{:S(2)}) copy-start(s32[8,1024]{1,0:T(8,128)} %wet_ref.5) | copy-start | bytes 98308
  54.3 26.2 %copy-start.13 = (s32[32,256]{1,0:T(8,128)S(1)}, s32[32,256]{1,0:T(8,128)}, u32[]{:S(2)}) copy-start(s32[32,256]{1,0:T(8,128)} %sender_ref.3) | copy-start | bytes 98308
  54.3 26.1 %copy-start.15 = (f32[32,256]{1,0:T(8,128)S(1)}, f32[32,256]{1,0:T(8,128)}, u32[]{:S(2)}) copy-start(f32[32,256]{1,0:T(8,128)} %share_ref.3) | copy-start | bytes 98308
  54.3 26.1 %collective-permute-start.7 = (f32[8,1024]{1,0:T(8,128)S(1)}, f32[8,1024]{1,0:T(8,128)S(1)}, u32[]{:S(2)}, u32[]{:S(2)}) collective-permute-start(f32[8,1024]{1,0:T(8,128)S(1)} %add_flux.1.flux_ref), channel_id=1, source_target_pairs={{0,1},{1,0},{2,3},{3,2},{4,5},{5,4},{6,7},{7,6},{8,9},{9,8},{10,11... | collective-permute-start | bytes 98312 | tf_op jit(solution)/shard_map/ppermute | solution.py:575

commit v5 on v4

--- a/solution.py
+++ b/solution.py
@@ -8,6 +8,7 @@
 STEPS = 4
 CLASSES = 3
 LANES = 128
+STREAM = 8
 SUBLANES = 8
 
 surface_exchange_factor = 0.8
@@ -86,7 +87,6 @@
     surface,
     inflow,
     wet,
-    far_rows,
     sems,
 ):
     rows = drive_ref.shape[0]
@@ -107,9 +107,7 @@
     for copy in copies[1:5]:
         copy.wait()
     far = place[:, half : 2 * half].astype(f32)
-    far_rows[...] = jnp.broadcast_to(far, (SUBLANES, half))
-    last = pltpu.make_async_copy(far_rows, far_ref.at[rows : rows + SUBLANES, :], sems.at[len(pairs)])
-    last.start()
+    far_ref[rows : rows + SUBLANES, :] = jnp.broadcast_to(far, (SUBLANES, half))
     even = is_even()
     mate_ref[0], next_ref[0] = edges(even, inflow[...])
     mate_ref[1], next_ref[1] = edges(even, wet[...].astype(f32))
@@ -117,7 +115,6 @@
         mate_ref[k + 2], next_ref[k + 2] = edges(even, surface[k])
     copies[0].wait()
     copies[5].wait()
-    last.wait()
 
 
 def pack_bulk(theta_ref, level_ref, mate_ref, next_ref):
@@ -190,6 +187,7 @@
     side,
     rise,
     source,
+    sems,
 ):
     tiers, lines, span = theta_ref.shape
     chunks = span // LANES
@@ -224,6 +222,7 @@
     first, last = row == 0, row == SUBLANES - 1
     lane_first, lane_last = lane == 0, lane == LANES - 1
 
+    copies = []
     for step in range(1, STEPS + 1):
         held, fresh = (even, odd) if step % 2 else (odd, even)
         final = step == STEPS
@@ -260,19 +259,24 @@
                     )
                     if add_source:
                         new = new + source[rows, cols]
-                    if final:
-                        out_ref[at, :, cols] = new
-                    else:
-                        fresh[at, rows, cols] = new
+                    fresh[at, rows, cols] = new
 
         advance(0, places - 1, 1, less_scale=lower, add_source=True)
-        for at in range(1, tiers - 1):
-            advance(at, at - 1, at + 1)
-        advance(tiers - 1, tiers - 2, tiers, more_scale=upper)
+        for at in range(1, tiers):
+            advance(at, at - 1, at + 1, more_scale=upper if at == tiers - 1 else None)
+            if final and (at + 1) % STREAM == 0:
+                k = at // STREAM
+                some = slice(k * STREAM, (k + 1) * STREAM)
+                copies.append(
+                    pltpu.make_async_copy(fresh.at[some, 0:8, :], out_ref.at[some], sems.at[k])
+                )
+                copies[-1].start()
         for j in range(STEPS - step):
             at = tiers + j + lev * step
             more = jnp.where(at == places - 1, 0, at + 1)
             advance(at, at - 1, more)
+    for copy in copies:
+        copy.wait()
 
 
 def entry_blocks(ref):
@@ -466,16 +470,9 @@
             pltpu.VMEM((STEPS + 1, lines, span), f32),
             pltpu.VMEM((lines, span), f32),
             pltpu.VMEM((lines, span), i32),
-            pltpu.VMEM((SUBLANES, half), f32),
-            pltpu.SemaphoreType.DMA((7,)),
+            pltpu.SemaphoreType.DMA((6,)),
         ],
         mib=56,
-        out_specs=[
-            pl.BlockSpec(memory_space=pl.ANY),
-            whole(),
-            whole(),
-            pl.BlockSpec(memory_space=pl.ANY),
-        ],
     )
     block_axes = ("comp", "dom")
     mates = [(i, i ^ 1) for i in range(n_block)]
@@ -538,7 +535,7 @@
         [whole()] * 4,
         (intersect_receiver_tile, top, top_far, pieces),
         "targets",
-        1.0,
+        8.0,
     )
     received = lax.all_to_all(
         payload.reshape(entry_rows, 4, LANES), "dom", split_axis=0, concat_axis=0, tiled=True
@@ -550,7 +547,7 @@
         [whole()] * 2,
         (received, intersect_receiver_tile),
         "add_flux",
-        20.0,
+        2.0,
     )
     late_level, partial_flux = lax.optimization_barrier((level, partial_flux))
     theta = call(
@@ -569,7 +566,9 @@
         ),
         "ocean",
         6.0,
-        scratch=[pltpu.VMEM((tiers + STEPS, 16, span), f32)] * 2 + [pltpu.VMEM((16, span), f32)] * 4,
+        scratch=[pltpu.VMEM((tiers + STEPS, 16, span), f32)] * 2 + [pltpu.VMEM((16, span), f32)] * 4
+        + [pltpu.SemaphoreType.DMA((tiers // STREAM,))],
+        out_specs=[pl.BlockSpec(memory_space=pl.ANY)],
     )
 
     other_flux = lax.ppermute(partial_flux, "lev", other)

time: 82 us -> 56.5 us (0.69)
  the two profiles are of different devices: /device:TPU:127 before, /device:TPU:64 now
where the time goes in v5:
time: 56.5 us; the launch traced here: 56.2 us
  starting transfers between devices  21.3 us (38%)
  Pallas kernels  16.8 us (30%)
  blocking collectives  15.3 us (27%)
  waiting for transfers between devices  1.82 us (3%)
  between operations  0.9 us (2%)
    pallas_call x8, Pallas kernels, call(): pl.pallas_call(body, out_shape=shapes, grid=grid, in_specs=specs, out_spe...  16.8 us
    all_to_all x1, blocking collectives, on_device(): lax.all_to_all(payload.reshape(entry_rows, 4, LANES), 'dom', split_axis=0...  15.3 us
    ppermute x1, starting transfers between devices, on_device(): follow_bulk = lax.ppermute(follow_bulk, block_axes, nexts)  5.22 us
    ppermute x1, starting transfers between devices, on_device(): top_far = lax.ppermute(top, 'lev', [(0, 1)])  4.37 us
    ppermute x1, starting transfers between devices, on_device(): follow = lax.ppermute(follow, block_axes, nexts)  4.35 us
    ppermute x1, starting transfers between devices, on_device(): lax.ppermute(packed, 'dom', [(i, (i + n_dom // 2) % n_dom) for i in range...  3.28 us
    ppermute x1, starting transfers between devices, on_device(): level = lax.ppermute(level, 'lev', other)  2 us
    ppermute x1, starting transfers between devices, on_device(): other_flux = lax.ppermute(partial_flux, 'lev', other)  1.99 us
  transfers between devices with their start and end apart: 8, of which 1 were waited for; matrix products, arithmetic and copies ran while one was open for 0% of the time, Pallas kernels for 24%

profile of v5, /device:TPU:64, one launch (start us, length us, event | category | flops | bytes accessed | tf_op | source)
XLA Modules:
  0.0 56.2 jit_solution(5097524808646295784)
XLA Ops:
  0.6 0.0 copy-start.1
  0.6 0.0 copy-start.2
  0.7 0.0 copy-start.3
  0.7 0.0 copy-start.7
  0.7 0.0 copy-start.8
  0.7 0.0 copy-start.9
  0.7 0.0 copy-start.10
  0.7 0.0 copy-start.11
  0.7 2.1 %pack_first.1 = (f32[152,512]{1,0:T(8,128)}, f32[7,4,1024]{2,1,0:T(4,128)}, f32[7,4,1024]{2,1,0:T(4,128)}, f32[4,8,1024]{2,1,0:T(8,128)}) custom-call(f32[144,1024]{1,0:T(8,128)} %drive_ref.3, s32[1,1024]{1,0:T(1,128)} %bitcast.10, f32[40,8,1024]{2,1,0:T(8,128)} %theta_ref.7, f32[8,1024]{1,0:T(8,128)} %inflow_ref.5, s32[8,1024]{1,0:T(8,128)} %wet_ref.5), custom_call_target="tpu_custom_call" | custom-call | flops 1500000000 | bytes 4500000 | tf_op jit(solution)/shard_map/pack_first/pallas_call | solution.py:33
  2.8 3.3 %collective-permute-start = (f32[152,512]{1,0:T(8,128)}, f32[152,512]{1,0:T(8,128)S(1)}, u32[]{:S(2)}, u32[]{:S(2)}) collective-permute-start(f32[152,512]{1,0:T(8,128)} %get-tuple-element.23), channel_id=1, source_target_pairs={{0,32},{2,34},{4,36},{6,38},{8,40},{10,42},{12,44},{14,46},{16,48}... | collective-permute-start | bytes 933896 | tf_op jit(solution)/shard_map/ppermute | solution.py:483
  6.1 0.0 collective-permute-start.1
  6.1 4.3 %collective-permute-start.2 = (f32[7,4,1024]{2,1,0:T(4,128)}, f32[7,4,1024]{2,1,0:T(4,128)S(1)}, u32[]{:S(2)}, u32[]{:S(2)}) collective-permute-start(f32[7,4,1024]{2,1,0:T(4,128)} %get-tuple-element.26), channel_id=1, source_target_pairs={{2,4},{6,8},{10,12},{14,16},{18,20},{22,24},{26,28},{30,32},{34,36... | collective-permute-start | bytes 344072 | tf_op jit(solution)/shard_map/ppermute | solution.py:486
  10.4 2.0 %collective-permute-start.3 = (f32[4,8,1024]{2,1,0:T(8,128)}, f32[4,8,1024]{2,1,0:T(8,128)S(1)}, u32[]{:S(2)}, u32[]{:S(2)}) collective-permute-start(f32[4,8,1024]{2,1,0:T(8,128)} %get-tuple-element.30), channel_id=1, source_target_pairs={{0,1},{1,0},{2,3},{3,2},{4,5},{5,4},{6,7},{7,6},{8,9},{9,8},{10,11... | collective-permute-start | bytes 393224 | tf_op jit(solution)/shard_map/ppermute | solution.py:484
  12.4 1.8 %collective-permute-done.far_ref = f32[152,512]{1,0:T(8,128)S(1)} collective-permute-done((f32[152,512]{1,0:T(8,128)}, f32[152,512]{1,0:T(8,128)S(1)}, u32[]{:S(2)}, u32[]{:S(2)}) %collective-permute-start) | collective-permute-done | bytes 311328 | tf_op jit(solution)/shard_map/ppermute | solution.py:483
  14.2 0.0 copy-done.1
  14.2 0.0 copy-done.2
  14.3 0.0 copy-done.3
  14.3 0.0 copy-done.7
  14.3 0.0 copy-done.8
  14.3 0.0 copy-done.9
  14.3 0.0 copy-done.10
  14.3 0.0 copy-done.11
  14.3 0.0 copy-start
  14.3 0.0 copy-start.5
  14.3 0.0 copy-start.6
  14.3 3.6 %columns.1 = (f32[144,1024]{1,0:T(8,128)}, f32[32,256]{1,0:T(8,128)S(1)}) custom-call(f32[144,1024]{1,0:T(8,128)S(1)} %copy-done.1, s32[1,1024]{1,0:T(1,128)S(1)} %bitcast.9, s32[1,1024]{1,0:T(1,128)S(1)} %bitcast.11, f32[144,1024]{1,0:T(8,128)S(1)} %copy-done.2, f32[152,512]{1,0:T(8,128)S(1)} %collective-permute-done.far_ref, f32[144,144]{1,0:T(8,128)S(1)} %copy-done.3, ...), custom_call_target="tpu_custom_call" | custom-call | flops 4000000000 | bytes 12000000 | tf_op jit(solution)/shard_map/columns/pallas_call | solution.py:33
  17.9 0.0 collective-permute-done.1.mate_ref
  17.9 0.0 collective-permute-done.2.next_ref
  17.9 0.0 copy-done
  17.9 0.0 copy-done.5
  17.9 0.0 copy-done.6
  17.9 0.4 top_level.1.top_ref
  18.4 0.0 copy-start.4
  18.4 4.4 %collective-permute-start.6 = (f32[8,1024]{1,0:T(8,128)S(1)}, f32[8,1024]{1,0:T(8,128)S(1)}, u32[]{:S(2)}, u32[]{:S(2)}) collective-permute-start(f32[8,1024]{1,0:T(8,128)S(1)} %top_level.1.top_ref), channel_id=1, source_target_pairs={{0,1},{2,3},{4,5},{6,7},{8,9},{10,11},{12,13},{14,15},{16,17},{18,... | collective-permute-start | bytes 98312 | tf_op jit(solution)/shard_map/ppermute | solution.py:517
  22.8 0.0 collective-permute-done.3.level_ref
  22.8 0.1 pack_bulk.1
  22.9 0.1 collective-permute-start.4
  23.0 5.2 %collective-permute-start.5 = (f32[39,4,1024]{2,1,0:T(4,128)S(1)}, f32[39,4,1024]{2,1,0:T(4,128)S(1)}, u32[]{:S(2)}, u32[]{:S(2)}) collective-permute-start(f32[39,4,1024]{2,1,0:T(4,128)S(1)} %get-tuple-element.33), channel_id=1, source_target_pairs={{2,4},{6,8},{10,12},{14,16},{18,20},{22,24},{26,28},{30,32},{34,36... | collective-permute-start | bytes 1916936 | tf_op jit(solution)/shard_map/ppermute | solution.py:530
  28.3 0.0 collective-permute-done.6.top_far_ref
  28.3 1.5 %targets.1 = f32[128,128]{1,0:T(8,128)S(1)} custom-call(s32[32,256]{1,0:T(8,128)S(1)} %copy-done.4, f32[8,1024]{1,0:T(8,128)S(1)} %top_level.1.top_ref, f32[8,1024]{1,0:T(8,128)S(1)} %collective-permute-done.6.top_far_ref, f32[32,256]{1,0:T(8,128)S(1)} %get-tuple-element.35.pieces_ref), custom_call_target="tpu_custom_call" | custom-call | flops 8000000000 | bytes 24000000 | tf_op jit(solution)/shard_map/targets/pallas_call | solution.py:33
  29.8 15.3 %all_to_all.5 = f32[32,4,128]{2,1,0:T(4,128)S(1)} all-to-all(f32[32,4,128]{2,1,0:T(4,128)S(1)} %bitcast.8), channel_id=1, replica_groups=mesh['comp'=4,'dom'=32,'lev'=2] {'dom'}, dimensions={0} | all-to-all | bytes 131072 | tf_op jit(solution)/shard_map/all_to_all | solution.py:540
  45.1 0.8 %add_flux.1.flux_ref = f32[8,1024]{1,0:T(8,128)S(1)} custom-call(f32[128,128]{1,0:T(8,128)S(1)} %bitcast.6, s32[32,256]{1,0:T(8,128)S(1)} %copy-done.4), custom_call_target="tpu_custom_call" | custom-call | flops 2000000000 | bytes 6000000 | tf_op jit(solution)/shard_map/add_flux/pallas_call | solution.py:33
  45.9 2.0 %collective-permute-start.7 = (f32[8,1024]{1,0:T(8,128)S(1)}, f32[8,1024]{1,0:T(8,128)S(1)}, u32[]{:S(2)}, u32[]{:S(2)}) collective-permute-start(f32[8,1024]{1,0:T(8,128)S(1)} %add_flux.1.flux_ref), channel_id=1, source_target_pairs={{0,1},{1,0},{2,3},{3,2},{4,5},{5,4},{6,7},{7,6},{8,9},{9,8},{10,11... | collective-permute-start | bytes 98312 | tf_op jit(solution)/shard_map/ppermute | solution.py:574
  47.9 0.0 collective-permute-done.4.mate_bulk_ref
  47.9 0.0 collective-permute-done.5.next_bulk_ref
  47.9 7.0 %ocean.1 = f32[40,8,1024]{2,1,0:T(8,128)} custom-call(f32[40,8,1024]{2,1,0:T(8,128)S(1)} %copy-done, f32[7,4,1024]{2,1,0:T(4,128)S(1)} %collective-permute-done.1.mate_ref, f32[7,4,1024]{2,1,0:T(4,128)S(1)} %collective-permute-done.2.next_ref, f32[39,4,1024]{2,1,0:T(4,128)S(1)} %collective-permute-done.4.mate_bulk_ref, ...), custom_call_target="tpu_custom_call" | custom-call | flops 6000000000 | bytes 18000000 | tf_op jit(solution)/shard_map/ocean/pallas_call | solution.py:33
  54.9 0.0 collective-permute-done.7.other_flux_ref
  54.9 1.3 %add_warmth.1 = (f32[8,128]{1,0:T(8,128)}, f32[8,1024]{1,0:T(8,128)}) custom-call(f32[128,128]{1,0:T(8,128)S(1)} %bitcast.7, s32[32,256]{1,0:T(8,128)S(1)} %copy-done.7, f32[32,256]{1,0:T(8,128)S(1)} %copy-done.8, f32[8,1024]{1,0:T(8,128)S(1)} %add_flux.1.flux_ref, f32[8,1024]{1,0:T(8,128)S(1)} %collective-permute-done.7.other_flux_ref), custom_call_target="tpu_custom_call" | custom-call | flops 2000000000 | bytes 6000000 | tf_op jit(solution)/shard_map/add_warmth/pallas_call | solution.py:33
  (1 shorter events, 0.0 us)
Async XLA Ops:
  0.6 13.6 %copy-start.1 = (f32[144,1024]{1,0:T(8,128)S(1)}, f32[144,1024]{1,0:T(8,128)}, u32[]{:S(2)}) copy-start(f32[144,1024]{1,0:T(8,128)} %state_ref.1) | copy-start | bytes 1769476
  0.6 13.6 %copy-start.2 = (f32[144,1024]{1,0:T(8,128)S(1)}, f32[144,1024]{1,0:T(8,128)}, u32[]{:S(2)}) copy-start(f32[144,1024]{1,0:T(8,128)} %drive_ref.3) | copy-start | bytes 1769476
  0.7 13.6 %copy-start.3 = (f32[144,144]{1,0:T(8,128)S(1)}, f32[144,144]{1,0:T(8,128)}, u32[]{:S(2)}) copy-start(f32[144,144]{1,0:T(8,128)} %link_ref.1) | copy-start | bytes 248836
  0.7 13.6 %copy-start.7 = (s32[32,256]{1,0:T(8,128)S(1)}, s32[32,256]{1,0:T(8,128)}, u32[]{:S(2)}) copy-start(s32[32,256]{1,0:T(8,128)} %sender_ref.3) | copy-start | bytes 98308
  0.7 13.6 %copy-start.8 = (f32[32,256]{1,0:T(8,128)S(1)}, f32[32,256]{1,0:T(8,128)}, u32[]{:S(2)}) copy-start(f32[32,256]{1,0:T(8,128)} %share_ref.3) | copy-start | bytes 98308
  0.7 13.6 %copy-start.9 = (s32[1024]{0:T(1024)S(1)}, s32[1024]{0:T(1024)}, u32[]{:S(2)}) copy-start(s32[1024]{0:T(1024)} %param.13) | copy-start | bytes 12292
  0.7 13.6 %copy-start.10 = (s32[1024]{0:T(1024)S(1)}, s32[1024]{0:T(1024)}, u32[]{:S(2)}) copy-start(s32[1024]{0:T(1024)} %param.14) | copy-start | bytes 12292
  0.7 13.6 %copy-start.11 = (f32[1024]{0:T(1024)S(1)}, f32[1024]{0:T(1024)}, u32[]{:S(2)}) copy-start(f32[1024]{0:T(1024)} %param.17) | copy-start | bytes 12292
  2.8 11.4 %collective-permute-start = (f32[152,512]{1,0:T(8,128)}, f32[152,512]{1,0:T(8,128)S(1)}, u32[]{:S(2)}, u32[]{:S(2)}) collective-permute-start(f32[152,512]{1,0:T(8,128)} %get-tuple-element.23), channel_id=1, source_target_pairs={{0,32},{2,34},{4,36},{6,38},{8,40},{10,42},{12,44},{14,46},{16,48}... | collective-permute-start | bytes 933896 | tf_op jit(solution)/shard_map/ppermute | solution.py:483
  6.1 11.8 %collective-permute-start.1 = (f32[7,4,1024]{2,1,0:T(4,128)}, f32[7,4,1024]{2,1,0:T(4,128)S(1)}, u32[]{:S(2)}, u32[]{:S(2)}) collective-permute-start(f32[7,4,1024]{2,1,0:T(4,128)} %get-tuple-element.25), channel_id=1, source_target_pairs={{0,2},{2,0},{4,6},{6,4},{8,10},{10,8},{12,14},{14,12},{16,18},{18,... | collective-permute-start | bytes 344072 | tf_op jit(solution)/shard_map/ppermute | solution.py:485
  6.1 11.8 %collective-permute-start.2 = (f32[7,4,1024]{2,1,0:T(4,128)}, f32[7,4,1024]{2,1,0:T(4,128)S(1)}, u32[]{:S(2)}, u32[]{:S(2)}) collective-permute-start(f32[7,4,1024]{2,1,0:T(4,128)} %get-tuple-element.26), channel_id=1, source_target_pairs={{2,4},{6,8},{10,12},{14,16},{18,20},{22,24},{26,28},{30,32},{34,36... | collective-permute-start | bytes 344072 | tf_op jit(solution)/shard_map/ppermute | solution.py:486
  10.4 12.3 %collective-permute-start.3 = (f32[4,8,1024]{2,1,0:T(8,128)}, f32[4,8,1024]{2,1,0:T(8,128)S(1)}, u32[]{:S(2)}, u32[]{:S(2)}) collective-permute-start(f32[4,8,1024]{2,1,0:T(8,128)} %get-tuple-element.30), channel_id=1, source_target_pairs={{0,1},{1,0},{2,3},{3,2},{4,5},{5,4},{6,7},{7,6},{8,9},{9,8},{10,11... | collective-permute-start | bytes 393224 | tf_op jit(solution)/shard_map/ppermute | solution.py:484
  14.3 3.6 %copy-start = (f32[40,8,1024]{2,1,0:T(8,128)S(1)}, f32[40,8,1024]{2,1,0:T(8,128)}, u32[]{:S(2)}) copy-start(f32[40,8,1024]{2,1,0:T(8,128)} %theta_ref.7) | copy-start | bytes 3932164
  14.3 3.6 %copy-start.5 = (f32[8,1024]{1,0:T(8,128)S(1)}, f32[8,1024]{1,0:T(8,128)}, u32[]{:S(2)}) copy-start(f32[8,1024]{1,0:T(8,128)} %inflow_ref.5) | copy-start | bytes 98308
  14.3 3.6 %copy-start.6 = (s32[8,1024]{1,0:T(8,128)S(1)}, s32[8,1024]{1,0:T(8,128)}, u32[]{:S(2)}) copy-start(s32[8,1024]{1,0:T(8,128)} %wet_ref.5) | copy-start | bytes 98308
  18.4 9.9 %copy-start.4 = (s32[32,256]{1,0:T(8,128)S(1)}, s32[32,256]{1,0:T(8,128)}, u32[]{:S(2)}) copy-start(s32[32,256]{1,0:T(8,128)} %tile_ref.3) | copy-start | bytes 98308
  18.4 9.9 %collective-permute-start.6 = (f32[8,1024]{1,0:T(8,128)S(1)}, f32[8,1024]{1,0:T(8,128)S(1)}, u32[]{:S(2)}, u32[]{:S(2)}) collective-permute-start(f32[8,1024]{1,0:T(8,128)S(1)} %top_level.1.top_ref), channel_id=1, source_target_pairs={{0,1},{2,3},{4,5},{6,7},{8,9},{10,11},{12,13},{14,15},{16,17},{18,... | collective-permute-start | bytes 98312 | tf_op jit(solution)/shard_map/ppermute | solution.py:517
  22.9 24.9 %collective-permute-start.4 = (f32[39,4,1024]{2,1,0:T(4,128)S(1)}, f32[39,4,1024]{2,1,0:T(4,128)S(1)}, u32[]{:S(2)}, u32[]{:S(2)}) collective-permute-start(f32[39,4,1024]{2,1,0:T(4,128)S(1)} %get-tuple-element.32), channel_id=1, source_target_pairs={{0,2},{2,0},{4,6},{6,4},{8,10},{10,8},{12,14},{14,12},{16,18},{18,... | collective-permute-start | bytes 1916936 | tf_op jit(solution)/shard_map/ppermute | solution.py:529
  23.0 24.8 %collective-permute-start.5 = (f32[39,4,1024]{2,1,0:T(4,128)S(1)}, f32[39,4,1024]{2,1,0:T(4,128)S(1)}, u32[]{:S(2)}, u32[]{:S(2)}) collective-permute-start(f32[39,4,1024]{2,1,0:T(4,128)S(1)} %get-tuple-element.33), channel_id=1, source_target_pairs={{2,4},{6,8},{10,12},{14,16},{18,20},{22,24},{26,28},{30,32},{34,36... | collective-permute-start | bytes 1916936 | tf_op jit(solution)/shard_map/ppermute | solution.py:530
  45.9 9.0 %collective-permute-start.7 = (f32[8,1024]{1,0:T(8,128)S(1)}, f32[8,1024]{1,0:T(8,128)S(1)}, u32[]{:S(2)}, u32[]{:S(2)}) collective-permute-start(f32[8,1024]{1,0:T(8,128)S(1)} %add_flux.1.flux_ref), channel_id=1, source_target_pairs={{0,1},{1,0},{2,3},{3,2},{4,5},{5,4},{6,7},{7,6},{8,9},{9,8},{10,11... | collective-permute-start | bytes 98312 | tf_op jit(solution)/shard_map/ppermute | solution.py:574

commit v6 on v5

--- a/solution.py
+++ b/solution.py
@@ -209,7 +209,10 @@
         source[rows, :] = (flux_gain * upper) * (wet * flow)
 
     for at in range(places):
-        even[at, 0:8, :] = theta_ref[at] if at < tiers else level_ref[at - tiers]
+        if at >= tiers:
+            even[at, 0:8, :] = level_ref[at - tiers]
+        elif at in (0, tiers - 1):
+            even[at, 0:8, :] = theta_ref[at]
         if at < skip:
             mate, other = mate_ref[at + 2], next_ref[at + 2]
         else:
@@ -229,8 +232,13 @@
         parts = (0,) if final else (0, 8)
 
         def advance(at, less, more, less_scale=None, more_scale=None, add_source=False):
+            def plane(index, p, cols):
+                if step == 1 and p == 0 and isinstance(index, int) and index < tiers:
+                    return theta_ref[index, :, cols]
+                return held[index, p : p + 8, cols]
+
             value = {
-                (p, c): held[at, p : p + 8, c * LANES : (c + 1) * LANES]
+                (p, c): plane(at, p, slice(c * LANES, (c + 1) * LANES))
                 for p in (0, 8)
                 for c in range(chunks)
             }
@@ -238,16 +246,14 @@
             left = {(p, c): pltpu.roll(value[p, c], LANES - 1, 1) for p in parts for c in range(chunks)}
             for c in range(chunks):
                 cols = slice(c * LANES, (c + 1) * LANES)
-                own, halo = value[0, c], value[8, c]
-                less_rows = {0: pltpu.roll(own, 1, 0), 8: pltpu.roll(halo, 1, 0)}
-                more_rows = {0: pltpu.roll(own, 7, 0), 8: pltpu.roll(halo, 7, 0)}
                 for p in parts:
-                    around = jnp.where(first, less_rows[8 - p], less_rows[p])
-                    around = around + jnp.where(last, more_rows[8 - p], more_rows[p])
+                    mine, next_to = value[p, c], value[8 - p, c]
+                    around = pltpu.roll(jnp.where(last, next_to, mine), 1, 0)
+                    around = around + pltpu.roll(jnp.where(first, next_to, mine), 7, 0)
                     along = jnp.where(lane_first, right[p, (c - 1) % chunks], right[p, c])
                     along = along + jnp.where(lane_last, left[p, (c + 1) % chunks], left[p, c])
                     rows = slice(p, p + 8)
-                    a, b = held[less, rows, cols], held[more, rows, cols]
+                    a, b = plane(less, p, cols), plane(more, p, cols)
                     if less_scale is not None:
                         a = a * less_scale
                     if more_scale is not None:
@@ -301,11 +307,22 @@
     return found
 
 
+def own_forcing(place_ref, drive_ref, out_ref):
+    rows, half = drive_ref.shape
+    count = out_ref.shape[1]
+    drive = jnp.concatenate(split(drive_ref[...]), axis=0)
+    place = place_ref[:, 0:half]
+    width = 256
+    for start in range(0, count, width):
+        target = start + lax.broadcasted_iota(i32, (width, half), 0)
+        both = dot_nt(drive, jnp.where(target == place, 1.0, 0.0).astype(bf16))
+        out_ref[:, start : start + width] = both[0:rows] + both[rows : 2 * rows]
+
+
 def columns(
     state_ref,
     classes_ref,
-    place_ref,
-    drive_ref,
+    forcing_ref,
     far_ref,
     link_ref,
     warmth_ref,
@@ -313,35 +330,41 @@
     share_ref,
     out_ref,
     pieces_ref,
+    result,
+    sems,
 ):
     rows, count = state_ref.shape
-    half = drive_ref.shape[1]
+    half = far_ref.shape[1]
     levels = rows // 2
     width = 256
 
-    own_drive = jnp.concatenate(split(drive_ref[...]), axis=0)
     far_drive = jnp.concatenate(split(far_ref[0:rows, :]), axis=0)
-    own_place = place_ref[:, 0:half]
     far_place = far_ref[rows : rows + 1, :].astype(i32)
     link_high, link_low = split(link_ref[...])
     link_both = jnp.concatenate([link_high, link_low], axis=0)
 
-    flux = []
-    for start in range(0, count, width):
-        cols = slice(start, start + width)
-        target = start + lax.broadcasted_iota(i32, (width, half), 0)
-        own_pick = jnp.where(target == own_place, 1.0, 0.0).astype(bf16)
+    chunks = [slice(start, start + width) for start in range(0, count, width)]
+    forcing = []
+    for cols in chunks:
+        target = cols.start + lax.broadcasted_iota(i32, (width, half), 0)
         far_pick = jnp.where(target == far_place, 1.0, 0.0).astype(bf16)
-        both = dot_nt(own_drive, own_pick) + dot_nt(far_drive, far_pick)
-        forcing = both[0:rows] + both[rows : 2 * rows]
-        x = state_ref[:, cols]
-        kinds = classes_ref[:, cols]
-        for k in range(CLASSES):
+        both = dot_nt(far_drive, far_pick)
+        forcing.append(forcing_ref[:, cols] + (both[0:rows] + both[rows : 2 * rows]))
+    states = [state_ref[:, cols] for cols in chunks]
+    for k in range(CLASSES):
+        for c, cols in enumerate(chunks):
+            x = states[c]
             high, low = split(x)
             product = dot_nn(link_both, high)
-            drive = product[0:rows] + (product[rows : 2 * rows] + dot_nn(link_high, low)) + forcing
-            x = x + jnp.where(kinds > k, tendency_scale * jnp.tanh(drive), 0.0)
-        out_ref[:, cols] = x
+            drive = product[0:rows] + (product[rows : 2 * rows] + dot_nn(link_high, low)) + forcing[c]
+            states[c] = x + jnp.where(classes_ref[:, cols] > k, tendency_scale * jnp.tanh(drive), 0.0)
+    copies = []
+    flux = []
+    for c, cols in enumerate(chunks):
+        x = states[c]
+        result[:, cols] = x
+        copies.append(pltpu.make_async_copy(result.at[:, cols], out_ref.at[:, cols], sems.at[c]))
+        copies[c].start()
         flux.append(
             surface_exchange_factor * (x[levels - 1 : levels, :] - warmth_ref[:, cols])
             + humidity_exchange_factor * x[rows - 1 : rows, :]
@@ -354,6 +377,8 @@
     tables = [flux[:, r * LANES : (r + 1) * LANES] for r in range(count // LANES)]
     for b, v in zip(blocks, picked(tables, keys, lanes)):
         pieces_ref[b] = share_ref[b] * v
+    for copy in copies:
+        copy.wait()
 
 
 def targets(tile_ref, top_ref, top_far_ref, pieces_ref, payload_ref):
@@ -371,7 +396,7 @@
         payload_ref[pl.ds(4 * r.start + 2 + part, SUBLANES, stride=4), :] = v
 
 
-def entry_sum(index_row, value_row, groups, order):
+def entry_sum(index_row, value_row, groups, order, width=LANES):
     entries = index_row.shape[1]
     group = order(index_row)
     hit = lax.broadcasted_iota(i32, (groups, entries), 0) == group
@@ -380,8 +405,8 @@
     weighted = jnp.concatenate(
         [jnp.where(hit, high, 0.0).astype(bf16), jnp.where(hit, low, 0.0).astype(bf16)], axis=0
     )
-    lane = index_row & (LANES - 1)
-    lane_hit = lax.broadcasted_iota(i32, (LANES, entries), 0) == lane
+    lane = index_row & (width - 1)
+    lane_hit = lax.broadcasted_iota(i32, (width, entries), 0) == lane
     return dot_nt(weighted, jnp.where(lane_hit, 1.0, 0.0).astype(bf16))
 
 
@@ -410,16 +435,22 @@
 def add_warmth(received_ref, sender_ref, share_ref, flux_ref, other_flux_ref, out_ref, rate_ref):
     rate_ref[...] = flux_ref[...] + other_flux_ref[...]
     entry_rows, slots = sender_ref.shape
-    groups = out_ref.shape[0]
-    total = jnp.zeros((2 * groups, LANES), f32)
+    lines = out_ref.shape[0]
+    parts = 4
+    width = LANES // parts
+    groups = lines * parts
+    total = jnp.zeros((2 * groups, width), f32)
     for d in range(entry_rows):
         total = total + entry_sum(
             sender_ref[d : d + 1, :],
             joined_rows(received_ref, 4 * d + 2) * share_ref[d : d + 1, :],
             groups,
-            lambda t: t >> 7,
+            lambda t: ((t >> 5) & (parts - 1)) * lines + (t >> 7),
+            width,
         )
-    out_ref[...] = total[0:groups] + total[groups:]
+    total = total[0:groups] + total[groups:]
+    for k in range(parts):
+        out_ref[:, k * width : (k + 1) * width] = total[k * lines : (k + 1) * lines]
 
 
 def on_device(
@@ -484,15 +515,23 @@
     level = lax.ppermute(level, "lev", other)
     mate = lax.ppermute(mate, block_axes, mates)
     follow = lax.ppermute(follow, block_axes, nexts)
+    forcing = call(
+        own_forcing,
+        shape(rows, count),
+        [whole(), pl.BlockSpec((rows, half), lambda i: (0, 0))],
+        (place, sunlight_aerosol_drive),
+        "own_forcing",
+        1.0,
+        grid=(1,),
+    )
     air_profile_updated, pieces = call(
         columns,
         [shape(rows, count), shape(entry_rows, slots)],
-        [whole()] * 3 + [pl.BlockSpec((rows, half), lambda i: (0, 0))] + [whole()] * 5,
+        [whole()] * 8,
         (
             air_profile_vector,
             profile_pass_kind.reshape(1, count),
-            place,
-            sunlight_aerosol_drive,
+            forcing,
             far,
             profile_link_operator,
             bottom_warmth_seen.reshape(1, count),
@@ -500,8 +539,9 @@
             intersect_share,
         ),
         "columns",
-        4.0,
-        grid=(1,),
+        3.0,
+        scratch=[pltpu.VMEM((rows, count), f32), pltpu.SemaphoreType.DMA((count // 256,))],
+        out_specs=[pl.BlockSpec(memory_space=pl.ANY), whole()],
     )
     mate, follow, pieces = lax.optimization_barrier((mate, follow, pieces))
     part = pl.BlockSpec((STEPS + 3, 4, span), lambda i: (0, 0, 0))

time: 56.5 us -> 55.9 us (0.989)
  Pallas kernels: 16.8 us -> 15.3 us
  blocking collectives: 15.3 us -> 16.7 us
  starting transfers between devices: 21.3 us -> 20 us
  waiting for transfers between devices: 1.82 us -> 2.59 us
    ppermute x1, starting transfers between devices: 5.22 us -> 3.7 us  [on_device(): follow_bulk = lax.ppermute(follow_bulk, block_axes, nexts)]
    pallas_call x8 -> x9, Pallas kernels: 16.8 us -> 15.3 us  [call(): pl.pallas_call(body, out_shape=shapes, grid=grid, in_specs=specs, out_spe...]
    all_to_all x1, blocking collectives: 15.3 us -> 16.7 us  [on_device(): lax.all_to_all(payload.reshape(entry_rows, 4, LANES), 'dom', split_axis=0...]
    ppermute x1, waiting for transfers between devices: 0.01 us -> 1.37 us  [on_device(): follow = lax.ppermute(follow, block_axes, nexts)]
    ppermute x1, waiting for transfers between devices: 1.8 us -> 1.21 us  [on_device(): lax.ppermute(packed, 'dom', [(i, (i + n_dom // 2) % n_dom) for i in range...]
  transfers between devices with their start and end apart: 8 -> 8, of which waited for: 1 -> 2; matrix products, arithmetic and copies ran while one was open for 0% -> 0% of each run, Pallas kernels for 24% -> 22%
where the time goes in v6:
time: 55.9 us; the launch traced here: 55.7 us
  starting transfers between devices  20 us (36%)
  blocking collectives  16.7 us (30%)
  Pallas kernels  15.3 us (27%)
  waiting for transfers between devices  2.59 us (5%)
  between operations  0.89 us (2%)
    all_to_all x1, blocking collectives, on_device(): lax.all_to_all(payload.reshape(entry_rows, 4, LANES), 'dom', split_axis=0...  16.7 us
    pallas_call x9, Pallas kernels, call(): pl.pallas_call(body, out_shape=shapes, grid=grid, in_specs=specs, out_spe...  15.3 us
    ppermute x1, starting transfers between devices, on_device(): top_far = lax.ppermute(top, 'lev', [(0, 1)])  4.55 us
    ppermute x1, starting transfers between devices, on_device(): follow = lax.ppermute(follow, block_axes, nexts)  4.35 us
    ppermute x1, starting transfers between devices, on_device(): follow_bulk = lax.ppermute(follow_bulk, block_axes, nexts)  3.7 us
    ppermute x1, starting transfers between devices, on_device(): lax.ppermute(packed, 'dom', [(i, (i + n_dom // 2) % n_dom) for i in range...  3.28 us
    ppermute x1, starting transfers between devices, on_device(): other_flux = lax.ppermute(partial_flux, 'lev', other)  2.07 us
    ppermute x1, starting transfers between devices, on_device(): level = lax.ppermute(level, 'lev', other)  2 us
  transfers between devices with their start and end apart: 8, of which 2 were waited for; matrix products, arithmetic and copies ran while one was open for 0% of the time, Pallas kernels for 22%

profile of v6, /device:TPU:64, one launch (start us, length us, event | category | flops | bytes accessed | tf_op | source)
XLA Modules:
  0.0 55.7 jit_solution(9692030912583681978)
XLA Ops:
  0.6 0.0 copy-start.1
  0.6 0.0 copy-start.9
  0.7 2.1 %pack_first.1 = (f32[152,512]{1,0:T(8,128)}, f32[7,4,1024]{2,1,0:T(4,128)}, f32[7,4,1024]{2,1,0:T(4,128)}, f32[4,8,1024]{2,1,0:T(8,128)}) custom-call(f32[144,1024]{1,0:T(8,128)} %drive_ref.3, s32[1,1024]{1,0:T(1,128)} %bitcast.9, f32[40,8,1024]{2,1,0:T(8,128)} %theta_ref.7, f32[8,1024]{1,0:T(8,128)} %inflow_ref.5, s32[8,1024]{1,0:T(8,128)} %wet_ref.5), custom_call_target="tpu_custom_call" | custom-call | flops 1500000000 | bytes 4500000 | tf_op jit(solution)/shard_map/pack_first/pallas_call | solution.py:33
  2.7 3.3 %collective-permute-start = (f32[152,512]{1,0:T(8,128)}, f32[152,512]{1,0:T(8,128)S(1)}, u32[]{:S(2)}, u32[]{:S(2)}) collective-permute-start(f32[152,512]{1,0:T(8,128)} %get-tuple-element.23), channel_id=1, source_target_pairs={{0,32},{2,34},{4,36},{6,38},{8,40},{10,42},{12,44},{14,46},{16,48}... | collective-permute-start | bytes 933896 | tf_op jit(solution)/shard_map/ppermute | solution.py:514
  6.0 0.0 collective-permute-start.1
  6.0 4.3 %collective-permute-start.2 = (f32[7,4,1024]{2,1,0:T(4,128)}, f32[7,4,1024]{2,1,0:T(4,128)S(1)}, u32[]{:S(2)}, u32[]{:S(2)}) collective-permute-start(f32[7,4,1024]{2,1,0:T(4,128)} %get-tuple-element.26), channel_id=1, source_target_pairs={{2,4},{6,8},{10,12},{14,16},{18,20},{22,24},{26,28},{30,32},{34,36... | collective-permute-start | bytes 344072 | tf_op jit(solution)/shard_map/ppermute | solution.py:517
  10.4 0.0 copy-start.2
  10.4 0.0 copy-start.3
  10.4 0.0 copy-start.7
  10.4 0.0 copy-start.8
  10.4 0.0 copy-start.10
  10.4 0.0 copy-start.11
  10.4 2.0 %collective-permute-start.3 = (f32[4,8,1024]{2,1,0:T(8,128)}, f32[4,8,1024]{2,1,0:T(8,128)S(1)}, u32[]{:S(2)}, u32[]{:S(2)}) collective-permute-start(f32[4,8,1024]{2,1,0:T(8,128)} %get-tuple-element.30), channel_id=1, source_target_pairs={{0,1},{1,0},{2,3},{3,2},{4,5},{5,4},{6,7},{7,6},{8,9},{9,8},{10,11... | collective-permute-start | bytes 393224 | tf_op jit(solution)/shard_map/ppermute | solution.py:515
  12.4 0.0 copy-done.1
  12.4 0.0 copy-done.9
  12.4 0.5 own_forcing.1.forcing_ref
  13.0 1.2 %collective-permute-done.far_ref = f32[152,512]{1,0:T(8,128)S(1)} collective-permute-done((f32[152,512]{1,0:T(8,128)}, f32[152,512]{1,0:T(8,128)S(1)}, u32[]{:S(2)}, u32[]{:S(2)}) %collective-permute-start) | collective-permute-done | bytes 311328 | tf_op jit(solution)/shard_map/ppermute | solution.py:514
  14.2 0.0 copy-done.2
  14.2 0.0 copy-done.3
  14.2 0.0 copy-done.7
  14.2 0.0 copy-done.8
  14.2 0.0 copy-done.10
  14.2 0.0 copy-done.11
  14.2 0.0 copy-start
  14.2 0.0 copy-start.5
  14.2 0.0 copy-start.6
  14.2 2.1 %columns.1 = (f32[144,1024]{1,0:T(8,128)}, f32[32,256]{1,0:T(8,128)S(1)}) custom-call(f32[144,1024]{1,0:T(8,128)S(1)} %copy-done.2, s32[1,1024]{1,0:T(1,128)S(1)} %bitcast.11, f32[144,1024]{1,0:T(8,128)S(1)} %own_forcing.1.forcing_ref, f32[152,512]{1,0:T(8,128)S(1)} %collective-permute-done.far_ref, f32[144,144]{1,0:T(8,128)S(1)} %copy-done.3, ...), custom_call_target="tpu_custom_call" | custom-call | flops 3000000000 | bytes 9000000 | tf_op jit(solution)/shard_map/columns/pallas_call | solution.py:33
  16.4 0.0 collective-permute-done.1.mate_ref
  16.4 1.4 %collective-permute-done.2.next_ref = f32[7,4,1024]{2,1,0:T(4,128)S(1)} collective-permute-done((f32[7,4,1024]{2,1,0:T(4,128)}, f32[7,4,1024]{2,1,0:T(4,128)S(1)}, u32[]{:S(2)}, u32[]{:S(2)}) %collective-permute-start.2) | collective-permute-done | bytes 114720 | tf_op jit(solution)/shard_map/ppermute | solution.py:517
  17.7 0.0 copy-done
  17.8 0.0 copy-done.5
  17.8 0.4 top_level.1.top_ref
  18.2 0.0 copy-start.4
  18.2 4.6 %collective-permute-start.6 = (f32[8,1024]{1,0:T(8,128)S(1)}, f32[8,1024]{1,0:T(8,128)S(1)}, u32[]{:S(2)}, u32[]{:S(2)}) collective-permute-start(f32[8,1024]{1,0:T(8,128)S(1)} %top_level.1.top_ref), channel_id=1, source_target_pairs={{0,1},{2,3},{4,5},{6,7},{8,9},{10,11},{12,13},{14,15},{16,17},{18,... | collective-permute-start | bytes 98312 | tf_op jit(solution)/shard_map/ppermute | solution.py:557
  22.8 0.0 collective-permute-done.3.level_ref
  22.8 0.1 pack_bulk.1
  22.9 0.1 collective-permute-start.4
  23.1 3.7 %collective-permute-start.5 = (f32[39,4,1024]{2,1,0:T(4,128)S(1)}, f32[39,4,1024]{2,1,0:T(4,128)S(1)}, u32[]{:S(2)}, u32[]{:S(2)}) collective-permute-start(f32[39,4,1024]{2,1,0:T(4,128)S(1)} %get-tuple-element.33), channel_id=1, source_target_pairs={{2,4},{6,8},{10,12},{14,16},{18,20},{22,24},{26,28},{30,32},{34,36... | collective-permute-start | bytes 1916936 | tf_op jit(solution)/shard_map/ppermute | solution.py:570
  26.8 0.0 collective-permute-done.6.top_far_ref
  26.8 1.5 %targets.1 = f32[128,128]{1,0:T(8,128)S(1)} custom-call(s32[32,256]{1,0:T(8,128)S(1)} %copy-done.4, f32[8,1024]{1,0:T(8,128)S(1)} %top_level.1.top_ref, f32[8,1024]{1,0:T(8,128)S(1)} %collective-permute-done.6.top_far_ref, f32[32,256]{1,0:T(8,128)S(1)} %get-tuple-element.35.pieces_ref), custom_call_target="tpu_custom_call" | custom-call | flops 8000000000 | bytes 24000000 | tf_op jit(solution)/shard_map/targets/pallas_call | solution.py:33
  28.3 16.7 %all_to_all.5 = f32[32,4,128]{2,1,0:T(4,128)S(1)} all-to-all(f32[32,4,128]{2,1,0:T(4,128)S(1)} %bitcast.8), channel_id=1, replica_groups=mesh['comp'=4,'dom'=32,'lev'=2] {'dom'}, dimensions={0} | all-to-all | bytes 131072 | tf_op jit(solution)/shard_map/all_to_all | solution.py:580
  45.0 0.8 %add_flux.1.flux_ref = f32[8,1024]{1,0:T(8,128)S(1)} custom-call(f32[128,128]{1,0:T(8,128)S(1)} %bitcast.6, s32[32,256]{1,0:T(8,128)S(1)} %copy-done.4), custom_call_target="tpu_custom_call" | custom-call | flops 2000000000 | bytes 6000000 | tf_op jit(solution)/shard_map/add_flux/pallas_call | solution.py:33
  45.8 2.1 %collective-permute-start.7 = (f32[8,1024]{1,0:T(8,128)S(1)}, f32[8,1024]{1,0:T(8,128)S(1)}, u32[]{:S(2)}, u32[]{:S(2)}) collective-permute-start(f32[8,1024]{1,0:T(8,128)S(1)} %add_flux.1.flux_ref), channel_id=1, source_target_pairs={{0,1},{1,0},{2,3},{3,2},{4,5},{5,4},{6,7},{7,6},{8,9},{9,8},{10,11... | collective-permute-start | bytes 98312 | tf_op jit(solution)/shard_map/ppermute | solution.py:614
  47.9 0.0 collective-permute-done.4.mate_bulk_ref
  47.9 0.0 collective-permute-done.5.next_bulk_ref
  47.9 6.7 %ocean.1 = f32[40,8,1024]{2,1,0:T(8,128)} custom-call(f32[40,8,1024]{2,1,0:T(8,128)S(1)} %copy-done, f32[7,4,1024]{2,1,0:T(4,128)S(1)} %collective-permute-done.1.mate_ref, f32[7,4,1024]{2,1,0:T(4,128)S(1)} %collective-permute-done.2.next_ref, f32[39,4,1024]{2,1,0:T(4,128)S(1)} %collective-permute-done.4.mate_bulk_ref, ...), custom_call_target="tpu_custom_call" | custom-call | flops 6000000000 | bytes 18000000 | tf_op jit(solution)/shard_map/ocean/pallas_call | solution.py:33
  54.6 0.0 collective-permute-done.7.other_flux_ref
  54.6 1.1 %add_warmth.1 = (f32[8,128]{1,0:T(8,128)}, f32[8,1024]{1,0:T(8,128)}) custom-call(f32[128,128]{1,0:T(8,128)S(1)} %bitcast.7, s32[32,256]{1,0:T(8,128)S(1)} %copy-done.7, f32[32,256]{1,0:T(8,128)S(1)} %copy-done.8, f32[8,1024]{1,0:T(8,128)S(1)} %add_flux.1.flux_ref, f32[8,1024]{1,0:T(8,128)S(1)} %collective-permute-done.7.other_flux_ref), custom_call_target="tpu_custom_call" | custom-call | flops 2000000000 | bytes 6000000 | tf_op jit(solution)/shard_map/add_warmth/pallas_call | solution.py:33
  (2 shorter events, 0.0 us)
Async XLA Ops:
  0.6 11.8 %copy-start.1 = (f32[144,1024]{1,0:T(8,128)S(1)}, f32[144,1024]{1,0:T(8,128)}, u32[]{:S(2)}) copy-start(f32[144,1024]{1,0:T(8,128)} %drive_ref.3) | copy-start | bytes 1769476
  0.6 11.8 %copy-start.9 = (s32[1024]{0:T(1024)S(1)}, s32[1024]{0:T(1024)}, u32[]{:S(2)}) copy-start(s32[1024]{0:T(1024)} %param.14) | copy-start | bytes 12292
  2.7 11.4 %collective-permute-start = (f32[152,512]{1,0:T(8,128)}, f32[152,512]{1,0:T(8,128)S(1)}, u32[]{:S(2)}, u32[]{:S(2)}) collective-permute-start(f32[152,512]{1,0:T(8,128)} %get-tuple-element.23), channel_id=1, source_target_pairs={{0,32},{2,34},{4,36},{6,38},{8,40},{10,42},{12,44},{14,46},{16,48}... | collective-permute-start | bytes 933896 | tf_op jit(solution)/shard_map/ppermute | solution.py:514
  6.0 10.4 %collective-permute-start.1 = (f32[7,4,1024]{2,1,0:T(4,128)}, f32[7,4,1024]{2,1,0:T(4,128)S(1)}, u32[]{:S(2)}, u32[]{:S(2)}) collective-permute-start(f32[7,4,1024]{2,1,0:T(4,128)} %get-tuple-element.25), channel_id=1, source_target_pairs={{0,2},{2,0},{4,6},{6,4},{8,10},{10,8},{12,14},{14,12},{16,18},{18,... | collective-permute-start | bytes 344072 | tf_op jit(solution)/shard_map/ppermute | solution.py:516
  6.0 11.7 %collective-permute-start.2 = (f32[7,4,1024]{2,1,0:T(4,128)}, f32[7,4,1024]{2,1,0:T(4,128)S(1)}, u32[]{:S(2)}, u32[]{:S(2)}) collective-permute-start(f32[7,4,1024]{2,1,0:T(4,128)} %get-tuple-element.26), channel_id=1, source_target_pairs={{2,4},{6,8},{10,12},{14,16},{18,20},{22,24},{26,28},{30,32},{34,36... | collective-permute-start | bytes 344072 | tf_op jit(solution)/shard_map/ppermute | solution.py:517
  10.4 3.8 %copy-start.2 = (f32[144,1024]{1,0:T(8,128)S(1)}, f32[144,1024]{1,0:T(8,128)}, u32[]{:S(2)}) copy-start(f32[144,1024]{1,0:T(8,128)} %state_ref.1) | copy-start | bytes 1769476
  10.4 3.8 %copy-start.3 = (f32[144,144]{1,0:T(8,128)S(1)}, f32[144,144]{1,0:T(8,128)}, u32[]{:S(2)}) copy-start(f32[144,144]{1,0:T(8,128)} %link_ref.1) | copy-start | bytes 248836
  10.4 3.8 %copy-start.7 = (s32[32,256]{1,0:T(8,128)S(1)}, s32[32,256]{1,0:T(8,128)}, u32[]{:S(2)}) copy-start(s32[32,256]{1,0:T(8,128)} %sender_ref.3) | copy-start | bytes 98308
  10.4 3.8 %copy-start.8 = (f32[32,256]{1,0:T(8,128)S(1)}, f32[32,256]{1,0:T(8,128)}, u32[]{:S(2)}) copy-start(f32[32,256]{1,0:T(8,128)} %share_ref.3) | copy-start | bytes 98308
  10.4 3.8 %copy-start.10 = (s32[1024]{0:T(1024)S(1)}, s32[1024]{0:T(1024)}, u32[]{:S(2)}) copy-start(s32[1024]{0:T(1024)} %param.13) | copy-start | bytes 12292
  10.4 3.8 %copy-start.11 = (f32[1024]{0:T(1024)S(1)}, f32[1024]{0:T(1024)}, u32[]{:S(2)}) copy-start(f32[1024]{0:T(1024)} %param.17) | copy-start | bytes 12292
  10.4 12.4 %collective-permute-start.3 = (f32[4,8,1024]{2,1,0:T(8,128)}, f32[4,8,1024]{2,1,0:T(8,128)S(1)}, u32[]{:S(2)}, u32[]{:S(2)}) collective-permute-start(f32[4,8,1024]{2,1,0:T(8,128)} %get-tuple-element.30), channel_id=1, source_target_pairs={{0,1},{1,0},{2,3},{3,2},{4,5},{5,4},{6,7},{7,6},{8,9},{9,8},{10,11... | collective-permute-start | bytes 393224 | tf_op jit(solution)/shard_map/ppermute | solution.py:515
  14.2 3.6 %copy-start = (f32[40,8,1024]{2,1,0:T(8,128)S(1)}, f32[40,8,1024]{2,1,0:T(8,128)}, u32[]{:S(2)}) copy-start(f32[40,8,1024]{2,1,0:T(8,128)} %theta_ref.7) | copy-start | bytes 3932164
  14.2 3.5 %copy-start.5 = (f32[8,1024]{1,0:T(8,128)S(1)}, f32[8,1024]{1,0:T(8,128)}, u32[]{:S(2)}) copy-start(f32[8,1024]{1,0:T(8,128)} %inflow_ref.5) | copy-start | bytes 98308
  14.2 3.5 %copy-start.6 = (s32[8,1024]{1,0:T(8,128)S(1)}, s32[8,1024]{1,0:T(8,128)}, u32[]{:S(2)}) copy-start(s32[8,1024]{1,0:T(8,128)} %wet_ref.5) | copy-start | bytes 98308
  18.2 8.6 %copy-start.4 = (s32[32,256]{1,0:T(8,128)S(1)}, s32[32,256]{1,0:T(8,128)}, u32[]{:S(2)}) copy-start(s32[32,256]{1,0:T(8,128)} %tile_ref.3) | copy-start | bytes 98308
  18.2 8.5 %collective-permute-start.6 = (f32[8,1024]{1,0:T(8,128)S(1)}, f32[8,1024]{1,0:T(8,128)S(1)}, u32[]{:S(2)}, u32[]{:S(2)}) collective-permute-start(f32[8,1024]{1,0:T(8,128)S(1)} %top_level.1.top_ref), channel_id=1, source_target_pairs={{0,1},{2,3},{4,5},{6,7},{8,9},{10,11},{12,13},{14,15},{16,17},{18,... | collective-permute-start | bytes 98312 | tf_op jit(solution)/shard_map/ppermute | solution.py:557
  22.9 24.9 %collective-permute-start.4 = (f32[39,4,1024]{2,1,0:T(4,128)S(1)}, f32[39,4,1024]{2,1,0:T(4,128)S(1)}, u32[]{:S(2)}, u32[]{:S(2)}) collective-permute-start(f32[39,4,1024]{2,1,0:T(4,128)S(1)} %get-tuple-element.32), channel_id=1, source_target_pairs={{0,2},{2,0},{4,6},{6,4},{8,10},{10,8},{12,14},{14,12},{16,18},{18,... | collective-permute-start | bytes 1916936 | tf_op jit(solution)/shard_map/ppermute | solution.py:569
  23.1 24.8 %collective-permute-start.5 = (f32[39,4,1024]{2,1,0:T(4,128)S(1)}, f32[39,4,1024]{2,1,0:T(4,128)S(1)}, u32[]{:S(2)}, u32[]{:S(2)}) collective-permute-start(f32[39,4,1024]{2,1,0:T(4,128)S(1)} %get-tuple-element.33), channel_id=1, source_target_pairs={{2,4},{6,8},{10,12},{14,16},{18,20},{22,24},{26,28},{30,32},{34,36... | collective-permute-start | bytes 1916936 | tf_op jit(solution)/shard_map/ppermute | solution.py:570
  45.8 8.7 %collective-permute-start.7 = (f32[8,1024]{1,0:T(8,128)S(1)}, f32[8,1024]{1,0:T(8,128)S(1)}, u32[]{:S(2)}, u32[]{:S(2)}) collective-permute-start(f32[8,1024]{1,0:T(8,128)S(1)} %add_flux.1.flux_ref), channel_id=1, source_target_pairs={{0,1},{1,0},{2,3},{3,2},{4,5},{5,4},{6,7},{7,6},{8,9},{9,8},{10,11... | collective-permute-start | bytes 98312 | tf_op jit(solution)/shard_map/ppermute | solution.py:614

commit v7 on v6

--- a/solution.py
+++ b/solution.py
@@ -1,3 +1,5 @@
+import functools
+
 import jax
 import jax.numpy as jnp
 from jax import lax
@@ -117,14 +119,14 @@
     copies[5].wait()
 
 
-def pack_bulk(theta_ref, level_ref, mate_ref, next_ref):
+def pack_bulk(side, theta_ref, level_ref, out_ref):
     even = is_even()
     skip = STEPS + 1
     deep = theta_ref.shape[0] - skip
     for k in range(deep):
-        mate_ref[k], next_ref[k] = edges(even, theta_ref[k + skip])
+        out_ref[k] = edges(even, theta_ref[k + skip])[side]
     for j in range(STEPS):
-        mate_ref[deep + j], next_ref[deep + j] = edges(even, level_ref[j])
+        out_ref[deep + j] = edges(even, level_ref[j])[side]
 
 
 def across(own, halo):
@@ -556,19 +558,25 @@
     )
     top_far = lax.ppermute(top, "lev", [(0, 1)])
 
+    mate_bulk = call(
+        functools.partial(pack_bulk, 0),
+        shape(tiers - 1, 4, span),
+        [whole()] * 2,
+        (marine_warmth_departure, level),
+        "pack_bulk_0",
+        0.5,
+    )
+    mate_bulk = lax.ppermute(mate_bulk, block_axes, mates)
     later_level, top = lax.optimization_barrier((level, top))
-    bulk = tiers - 1
-    mate_bulk, follow_bulk = call(
-        pack_bulk,
-        [shape(bulk, 4, span), shape(bulk, 4, span)],
+    follow_bulk = call(
+        functools.partial(pack_bulk, 1),
+        shape(tiers - 1, 4, span),
         [whole()] * 2,
         (marine_warmth_departure, later_level),
-        "pack_bulk",
-        1.0,
-    )
-    mate_bulk = lax.ppermute(mate_bulk, block_axes, mates)
+        "pack_bulk_1",
+        0.5,
+    )
     follow_bulk = lax.ppermute(follow_bulk, block_axes, nexts)
-
     payload = call(
         targets,
         shape(4 * entry_rows, LANES),

time: 55.9 us -> 56.3 us (level)
  the two profiles are of different devices: /device:TPU:64 before, /device:TPU:71 now
where the time goes in v7:
time: 56.3 us; the launch traced here: 56 us
  blocking collectives  21.7 us (39%)
  Pallas kernels  15.4 us (27%)
  starting transfers between devices  15.4 us (27%)
  waiting for transfers between devices  2.57 us (5%)
  between operations  0.93 us (2%)
    all_to_all x1, blocking collectives, on_device(): lax.all_to_all(payload.reshape(entry_rows, 4, LANES), 'dom', split_axis=0...  21.7 us
    pallas_call x10, Pallas kernels, call(): pl.pallas_call(body, out_shape=shapes, grid=grid, in_specs=specs, out_spe...  15.4 us
    ppermute x1, starting transfers between devices, on_device(): follow_bulk = lax.ppermute(follow_bulk, block_axes, nexts)  4.44 us
    ppermute x1, starting transfers between devices, on_device(): lax.ppermute(packed, 'dom', [(i, (i + n_dom // 2) % n_dom) for i in range...  3 us
    ppermute x1, starting transfers between devices, on_device(): follow = lax.ppermute(follow, block_axes, nexts)  2.23 us
    ppermute x1, waiting for transfers between devices, on_device(): follow = lax.ppermute(follow, block_axes, nexts)  2.22 us
    ppermute x1, starting transfers between devices, on_device(): top_far = lax.ppermute(top, 'lev', [(0, 1)])  1.73 us
    ppermute x1, starting transfers between devices, on_device(): level = lax.ppermute(level, 'lev', other)  1.64 us
  transfers between devices with their start and end apart: 8, of which 2 were waited for; matrix products, arithmetic and copies ran while one was open for 0% of the time, Pallas kernels for 22%

profile of v7, /device:TPU:71, one launch (start us, length us, event | category | flops | bytes accessed | tf_op | source)
XLA Modules:
  0.0 56.0 jit_solution(3188002050822950733)
XLA Ops:
  0.6 0.0 copy-start.1
  0.6 0.0 copy-start.9
  0.7 2.1 %pack_first.1 = (f32[152,512]{1,0:T(8,128)}, f32[7,4,1024]{2,1,0:T(4,128)}, f32[7,4,1024]{2,1,0:T(4,128)}, f32[4,8,1024]{2,1,0:T(8,128)}) custom-call(f32[144,1024]{1,0:T(8,128)} %drive_ref.3, s32[1,1024]{1,0:T(1,128)} %bitcast.9, f32[40,8,1024]{2,1,0:T(8,128)} %theta_ref.9, f32[8,1024]{1,0:T(8,128)} %inflow_ref.5, s32[8,1024]{1,0:T(8,128)} %wet_ref.5), custom_call_target="tpu_custom_call" | custom-call | flops 1500000000 | bytes 4500000 | tf_op jit(solution)/shard_map/pack_first/pallas_call | solution.py:35
  2.7 3.0 %collective-permute-start = (f32[152,512]{1,0:T(8,128)}, f32[152,512]{1,0:T(8,128)S(1)}, u32[]{:S(2)}, u32[]{:S(2)}) collective-permute-start(f32[152,512]{1,0:T(8,128)} %get-tuple-element.21), channel_id=1, source_target_pairs={{0,32},{2,34},{4,36},{6,38},{8,40},{10,42},{12,44},{14,46},{16,48}... | collective-permute-start | bytes 933896 | tf_op jit(solution)/shard_map/ppermute | solution.py:516
  5.7 1.6 %collective-permute-start.3 = (f32[4,8,1024]{2,1,0:T(8,128)}, f32[4,8,1024]{2,1,0:T(8,128)S(1)}, u32[]{:S(2)}, u32[]{:S(2)}) collective-permute-start(f32[4,8,1024]{2,1,0:T(8,128)} %get-tuple-element.28), channel_id=1, source_target_pairs={{0,1},{1,0},{2,3},{3,2},{4,5},{5,4},{6,7},{7,6},{8,9},{9,8},{10,11... | collective-permute-start | bytes 393224 | tf_op jit(solution)/shard_map/ppermute | solution.py:517
  7.4 1.2 %collective-permute-start.1 = (f32[7,4,1024]{2,1,0:T(4,128)}, f32[7,4,1024]{2,1,0:T(4,128)S(1)}, u32[]{:S(2)}, u32[]{:S(2)}) collective-permute-start(f32[7,4,1024]{2,1,0:T(4,128)} %get-tuple-element.23), channel_id=1, source_target_pairs={{0,2},{2,0},{4,6},{6,4},{8,10},{10,8},{12,14},{14,12},{16,18},{18,... | collective-permute-start | bytes 344072 | tf_op jit(solution)/shard_map/ppermute | solution.py:518
  8.6 2.2 %collective-permute-start.2 = (f32[7,4,1024]{2,1,0:T(4,128)}, f32[7,4,1024]{2,1,0:T(4,128)S(1)}, u32[]{:S(2)}, u32[]{:S(2)}) collective-permute-start(f32[7,4,1024]{2,1,0:T(4,128)} %get-tuple-element.24), channel_id=1, source_target_pairs={{2,4},{6,8},{10,12},{14,16},{18,20},{22,24},{26,28},{30,32},{34,36... | collective-permute-start | bytes 344072 | tf_op jit(solution)/shard_map/ppermute | solution.py:519
  10.8 0.0 copy-done.1
  10.8 0.0 copy-done.9
  10.9 0.5 own_forcing.1.forcing_ref
  11.4 0.0 copy-start.2
  11.4 0.0 copy-start.3
  11.4 0.0 copy-start.7
  11.4 0.0 copy-start.8
  11.4 0.0 copy-start.10
  11.4 0.0 copy-start.11
  11.4 0.0 collective-permute-done.3.level_ref
  11.5 0.0 copy-done
  11.5 0.1 pack_bulk_0.1
  11.6 0.8 %collective-permute-start.4 = (f32[39,4,1024]{2,1,0:T(4,128)S(1)}, f32[39,4,1024]{2,1,0:T(4,128)S(1)}, u32[]{:S(2)}, u32[]{:S(2)}) collective-permute-start(f32[39,4,1024]{2,1,0:T(4,128)S(1)} %pack_bulk_0.1), channel_id=1, source_target_pairs={{0,2},{2,0},{4,6},{6,4},{8,10},{10,8},{12,14},{14,12},{16,18},{18,... | collective-permute-start | bytes 1916936 | tf_op jit(solution)/shard_map/ppermute | solution.py:569
  12.4 0.3 collective-permute-done.far_ref
  12.8 0.0 copy-done.2
  12.8 0.0 copy-done.3
  12.8 0.0 copy-done.7
  12.8 0.0 copy-done.8
  12.8 0.0 copy-done.10
  12.8 0.0 copy-done.11
  12.8 0.0 copy-start.5
  12.8 0.0 copy-start.6
  12.8 2.1 %columns.1 = (f32[144,1024]{1,0:T(8,128)}, f32[32,256]{1,0:T(8,128)S(1)}) custom-call(f32[144,1024]{1,0:T(8,128)S(1)} %copy-done.2, s32[1,1024]{1,0:T(1,128)S(1)} %bitcast.11, f32[144,1024]{1,0:T(8,128)S(1)} %own_forcing.1.forcing_ref, f32[152,512]{1,0:T(8,128)S(1)} %collective-permute-done.far_ref, f32[144,144]{1,0:T(8,128)S(1)} %copy-done.3, ...), custom_call_target="tpu_custom_call" | custom-call | flops 3000000000 | bytes 9000000 | tf_op jit(solution)/shard_map/columns/pallas_call | solution.py:35
  14.9 0.0 collective-permute-done.1.mate_ref
  14.9 2.2 %collective-permute-done.2.next_ref = f32[7,4,1024]{2,1,0:T(4,128)S(1)} collective-permute-done((f32[7,4,1024]{2,1,0:T(4,128)}, f32[7,4,1024]{2,1,0:T(4,128)S(1)}, u32[]{:S(2)}, u32[]{:S(2)}) %collective-permute-start.2) | collective-permute-done | bytes 114720 | tf_op jit(solution)/shard_map/ppermute | solution.py:519
  17.2 0.0 copy-done.5
  17.2 0.4 top_level.1.top_ref
  17.6 0.0 copy-start.4
  17.6 1.7 %collective-permute-start.6 = (f32[8,1024]{1,0:T(8,128)S(1)}, f32[8,1024]{1,0:T(8,128)S(1)}, u32[]{:S(2)}, u32[]{:S(2)}) collective-permute-start(f32[8,1024]{1,0:T(8,128)S(1)} %top_level.1.top_ref), channel_id=1, source_target_pairs={{0,1},{2,3},{4,5},{6,7},{8,9},{10,11},{12,13},{14,15},{16,17},{18,... | collective-permute-start | bytes 98312 | tf_op jit(solution)/shard_map/ppermute | solution.py:559
  19.4 0.1 pack_bulk_1.1
  19.5 4.4 %collective-permute-start.5 = (f32[39,4,1024]{2,1,0:T(4,128)S(1)}, f32[39,4,1024]{2,1,0:T(4,128)S(1)}, u32[]{:S(2)}, u32[]{:S(2)}) collective-permute-start(f32[39,4,1024]{2,1,0:T(4,128)S(1)} %pack_bulk_1.1), channel_id=1, source_target_pairs={{2,4},{6,8},{10,12},{14,16},{18,20},{22,24},{26,28},{30,32},{34,36... | collective-permute-start | bytes 1916936 | tf_op jit(solution)/shard_map/ppermute | solution.py:579
  23.9 0.0 collective-permute-done.6.top_far_ref
  24.0 1.5 %targets.1 = f32[128,128]{1,0:T(8,128)S(1)} custom-call(s32[32,256]{1,0:T(8,128)S(1)} %copy-done.4, f32[8,1024]{1,0:T(8,128)S(1)} %top_level.1.top_ref, f32[8,1024]{1,0:T(8,128)S(1)} %collective-permute-done.6.top_far_ref, f32[32,256]{1,0:T(8,128)S(1)} %get-tuple-element.31.pieces_ref), custom_call_target="tpu_custom_call" | custom-call | flops 8000000000 | bytes 24000000 | tf_op jit(solution)/shard_map/targets/pallas_call | solution.py:35
  25.5 21.7 %all_to_all.5 = f32[32,4,128]{2,1,0:T(4,128)S(1)} all-to-all(f32[32,4,128]{2,1,0:T(4,128)S(1)} %bitcast.8), channel_id=1, replica_groups=mesh['comp'=4,'dom'=32,'lev'=2] {'dom'}, dimensions={0} | all-to-all | bytes 131072 | tf_op jit(solution)/shard_map/all_to_all | solution.py:588
  47.1 0.8 %add_flux.1.flux_ref = f32[8,1024]{1,0:T(8,128)S(1)} custom-call(f32[128,128]{1,0:T(8,128)S(1)} %bitcast.6, s32[32,256]{1,0:T(8,128)S(1)} %copy-done.4), custom_call_target="tpu_custom_call" | custom-call | flops 2000000000 | bytes 6000000 | tf_op jit(solution)/shard_map/add_flux/pallas_call | solution.py:35
  47.9 0.3 collective-permute-start.7
  48.2 0.0 collective-permute-done.4.mate_bulk_ref
  48.2 0.0 collective-permute-done.5.next_bulk_ref
  48.2 6.7 %ocean.1 = f32[40,8,1024]{2,1,0:T(8,128)} custom-call(f32[40,8,1024]{2,1,0:T(8,128)S(1)} %copy-done, f32[7,4,1024]{2,1,0:T(4,128)S(1)} %collective-permute-done.1.mate_ref, f32[7,4,1024]{2,1,0:T(4,128)S(1)} %collective-permute-done.2.next_ref, f32[39,4,1024]{2,1,0:T(4,128)S(1)} %collective-permute-done.4.mate_bulk_ref, ...), custom_call_target="tpu_custom_call" | custom-call | flops 6000000000 | bytes 18000000 | tf_op jit(solution)/shard_map/ocean/pallas_call | solution.py:35
  54.9 0.0 collective-permute-done.7.other_flux_ref
  54.9 1.1 %add_warmth.1 = (f32[8,128]{1,0:T(8,128)}, f32[8,1024]{1,0:T(8,128)}) custom-call(f32[128,128]{1,0:T(8,128)S(1)} %bitcast.7, s32[32,256]{1,0:T(8,128)S(1)} %copy-done.7, f32[32,256]{1,0:T(8,128)S(1)} %copy-done.8, f32[8,1024]{1,0:T(8,128)S(1)} %add_flux.1.flux_ref, f32[8,1024]{1,0:T(8,128)S(1)} %collective-permute-done.7.other_flux_ref), custom_call_target="tpu_custom_call" | custom-call | flops 2000000000 | bytes 6000000 | tf_op jit(solution)/shard_map/add_warmth/pallas_call | solution.py:35
  (3 shorter events, 0.0 us)
Async XLA Ops:
  0.6 10.2 %copy-start.1 = (f32[144,1024]{1,0:T(8,128)S(1)}, f32[144,1024]{1,0:T(8,128)}, u32[]{:S(2)}) copy-start(f32[144,1024]{1,0:T(8,128)} %drive_ref.3) | copy-start | bytes 1769476
  0.6 10.2 %copy-start.9 = (s32[1024]{0:T(1024)S(1)}, s32[1024]{0:T(1024)}, u32[]{:S(2)}) copy-start(s32[1024]{0:T(1024)} %param.14) | copy-start | bytes 12292
  2.7 10.0 %collective-permute-start = (f32[152,512]{1,0:T(8,128)}, f32[152,512]{1,0:T(8,128)S(1)}, u32[]{:S(2)}, u32[]{:S(2)}) collective-permute-start(f32[152,512]{1,0:T(8,128)} %get-tuple-element.21), channel_id=1, source_target_pairs={{0,32},{2,34},{4,36},{6,38},{8,40},{10,42},{12,44},{14,46},{16,48}... | collective-permute-start | bytes 933896 | tf_op jit(solution)/shard_map/ppermute | solution.py:516
  5.7 5.7 %collective-permute-start.3 = (f32[4,8,1024]{2,1,0:T(8,128)}, f32[4,8,1024]{2,1,0:T(8,128)S(1)}, u32[]{:S(2)}, u32[]{:S(2)}) collective-permute-start(f32[4,8,1024]{2,1,0:T(8,128)} %get-tuple-element.28), channel_id=1, source_target_pairs={{0,1},{1,0},{2,3},{3,2},{4,5},{5,4},{6,7},{7,6},{8,9},{9,8},{10,11... | collective-permute-start | bytes 393224 | tf_op jit(solution)/shard_map/ppermute | solution.py:517
  7.4 7.6 %collective-permute-start.1 = (f32[7,4,1024]{2,1,0:T(4,128)}, f32[7,4,1024]{2,1,0:T(4,128)S(1)}, u32[]{:S(2)}, u32[]{:S(2)}) collective-permute-start(f32[7,4,1024]{2,1,0:T(4,128)} %get-tuple-element.23), channel_id=1, source_target_pairs={{0,2},{2,0},{4,6},{6,4},{8,10},{10,8},{12,14},{14,12},{16,18},{18,... | collective-permute-start | bytes 344072 | tf_op jit(solution)/shard_map/ppermute | solution.py:518
  8.6 2.9 %copy-start = (f32[40,8,1024]{2,1,0:T(8,128)S(1)}, f32[40,8,1024]{2,1,0:T(8,128)}, u32[]{:S(2)}) copy-start(f32[40,8,1024]{2,1,0:T(8,128)} %theta_ref.9) | copy-start | bytes 3932164
  8.6 8.6 %collective-permute-start.2 = (f32[7,4,1024]{2,1,0:T(4,128)}, f32[7,4,1024]{2,1,0:T(4,128)S(1)}, u32[]{:S(2)}, u32[]{:S(2)}) collective-permute-start(f32[7,4,1024]{2,1,0:T(4,128)} %get-tuple-element.24), channel_id=1, source_target_pairs={{2,4},{6,8},{10,12},{14,16},{18,20},{22,24},{26,28},{30,32},{34,36... | collective-permute-start | bytes 344072 | tf_op jit(solution)/shard_map/ppermute | solution.py:519
  11.4 1.4 %copy-start.2 = (f32[144,1024]{1,0:T(8,128)S(1)}, f32[144,1024]{1,0:T(8,128)}, u32[]{:S(2)}) copy-start(f32[144,1024]{1,0:T(8,128)} %state_ref.1) | copy-start | bytes 1769476
  11.4 1.4 %copy-start.3 = (f32[144,144]{1,0:T(8,128)S(1)}, f32[144,144]{1,0:T(8,128)}, u32[]{:S(2)}) copy-start(f32[144,144]{1,0:T(8,128)} %link_ref.1) | copy-start | bytes 248836
  11.4 1.4 %copy-start.7 = (s32[32,256]{1,0:T(8,128)S(1)}, s32[32,256]{1,0:T(8,128)}, u32[]{:S(2)}) copy-start(s32[32,256]{1,0:T(8,128)} %sender_ref.3) | copy-start | bytes 98308
  11.4 1.4 %copy-start.8 = (f32[32,256]{1,0:T(8,128)S(1)}, f32[32,256]{1,0:T(8,128)}, u32[]{:S(2)}) copy-start(f32[32,256]{1,0:T(8,128)} %share_ref.3) | copy-start | bytes 98308
  11.4 1.4 %copy-start.10 = (s32[1024]{0:T(1024)S(1)}, s32[1024]{0:T(1024)}, u32[]{:S(2)}) copy-start(s32[1024]{0:T(1024)} %param.13) | copy-start | bytes 12292
  11.4 1.4 %copy-start.11 = (f32[1024]{0:T(1024)S(1)}, f32[1024]{0:T(1024)}, u32[]{:S(2)}) copy-start(f32[1024]{0:T(1024)} %param.17) | copy-start | bytes 12292
  11.6 36.6 %collective-permute-start.4 = (f32[39,4,1024]{2,1,0:T(4,128)S(1)}, f32[39,4,1024]{2,1,0:T(4,128)S(1)}, u32[]{:S(2)}, u32[]{:S(2)}) collective-permute-start(f32[39,4,1024]{2,1,0:T(4,128)S(1)} %pack_bulk_0.1), channel_id=1, source_target_pairs={{0,2},{2,0},{4,6},{6,4},{8,10},{10,8},{12,14},{14,12},{16,18},{18,... | collective-permute-start | bytes 1916936 | tf_op jit(solution)/shard_map/ppermute | solution.py:569
  12.8 4.4 %copy-start.5 = (f32[8,1024]{1,0:T(8,128)S(1)}, f32[8,1024]{1,0:T(8,128)}, u32[]{:S(2)}) copy-start(f32[8,1024]{1,0:T(8,128)} %inflow_ref.5) | copy-start | bytes 98308
  12.8 4.3 %copy-start.6 = (s32[8,1024]{1,0:T(8,128)S(1)}, s32[8,1024]{1,0:T(8,128)}, u32[]{:S(2)}) copy-start(s32[8,1024]{1,0:T(8,128)} %wet_ref.5) | copy-start | bytes 98308
  17.6 6.3 %copy-start.4 = (s32[32,256]{1,0:T(8,128)S(1)}, s32[32,256]{1,0:T(8,128)}, u32[]{:S(2)}) copy-start(s32[32,256]{1,0:T(8,128)} %tile_ref.3) | copy-start | bytes 98308
  17.6 6.3 %collective-permute-start.6 = (f32[8,1024]{1,0:T(8,128)S(1)}, f32[8,1024]{1,0:T(8,128)S(1)}, u32[]{:S(2)}, u32[]{:S(2)}) collective-permute-start(f32[8,1024]{1,0:T(8,128)S(1)} %top_level.1.top_ref), channel_id=1, source_target_pairs={{0,1},{2,3},{4,5},{6,7},{8,9},{10,11},{12,13},{14,15},{16,17},{18,... | collective-permute-start | bytes 98312 | tf_op jit(solution)/shard_map/ppermute | solution.py:559
  19.5 28.7 %collective-permute-start.5 = (f32[39,4,1024]{2,1,0:T(4,128)S(1)}, f32[39,4,1024]{2,1,0:T(4,128)S(1)}, u32[]{:S(2)}, u32[]{:S(2)}) collective-permute-start(f32[39,4,1024]{2,1,0:T(4,128)S(1)} %pack_bulk_1.1), channel_id=1, source_target_pairs={{2,4},{6,8},{10,12},{14,16},{18,20},{22,24},{26,28},{30,32},{34,36... | collective-permute-start | bytes 1916936 | tf_op jit(solution)/shard_map/ppermute | solution.py:579
  47.9 7.0 %collective-permute-start.7 = (f32[8,1024]{1,0:T(8,128)S(1)}, f32[8,1024]{1,0:T(8,128)S(1)}, u32[]{:S(2)}, u32[]{:S(2)}) collective-permute-start(f32[8,1024]{1,0:T(8,128)S(1)} %add_flux.1.flux_ref), channel_id=1, source_target_pairs={{0,1},{1,0},{2,3},{3,2},{4,5},{5,4},{6,7},{7,6},{8,9},{9,8},{10,11... | collective-permute-start | bytes 98312 | tf_op jit(solution)/shard_map/ppermute | solution.py:622
